TPU v7x, 128 devices: a whole 4x4x4 slice. The times are simulated.
128 devices in a mesh: ty: 8 (over y, core), tx: 16 (over z, x).
Axes of the slice: x: 4, y: 4, z: 4, core: 2. Of those that a mesh axis runs over, the one named last changes fastest.
Arguments:
- object_tiles: float32 [2, 2048, 4096], P(None, 'ty', 'tx'), may hold values from -6 to 6
- previous_tiles: float32 [2, 2048, 4096], P(None, 'ty', 'tx'), may hold values from -6 to 6
- probe_modes: float32 [2, 2, 128, 128], replicated, may hold values from -1.5 to 1.5
- amplitude: float32 [128, 32, 128, 128], P(('ty', 'tx')), may hold values from 0.1 to 13.5
- row_tops: int32 [128], replicated, may hold values from 0 to 128
- scan_cols: int32 [128, 32], P(('ty', 'tx')), may hold values from 0 to 3968, as said below
- restart: int32 [2], replicated, may hold values from 1 to 100, as said below
- owner_map: int32 [8, 16], replicated, may hold values from 0 to 15, each once within a row
Outputs:
- object_out: float32 [2, 2048, 4096], P(None, 'ty', 'tx')
- losses: float32 [2], replicated
Inputs may be any that keep to these rules, and one draw needn't show every extreme that they name: `scan_cols`: position j's left column lies in j * 128 to (j + 1) * 128 - 1. `restart`: the counters of the iterations differ from one another. `owner_map`: each row of the map names every tile column once.
All inputs are finite; a program needn't handle non-finite values.
Results may differ from a plain program's by a relative error of at most 0.0003.
Values sent between devices are 32-bit elements; how exact they have to be, the bound alone decides.
No kernel may reach another device: no remote copies, remote signals or barrier semaphores. Data moves between devices by JAX's collectives and lax.ppermute only.
A program may use at most 128 MiB of HBM per device.

v0:
```python
import math

import jax
import jax.numpy as jnp
from jax import lax
from jax.sharding import PartitionSpec as P

ITERS = 2
START = 100


stabilizer = 0.05
step_length = 0.25


def momentum_table():
    values = [1.0]
    for counter in range(START):
        previous_value = values[-1]
        values.append((1.0 + (1.0 + 4.0 * previous_value * previous_value) ** 0.5) / 2.0)
    return jnp.asarray(values, jnp.float32)


def dft_tables(width):
    position_index = jnp.arange(width, dtype=jnp.int32)
    phase_grid = position_index[:, None] * position_index[None, :] % width
    angle_grid = phase_grid.astype(jnp.float32) * (2.0 * math.pi / width)
    unit_scale = 1.0 / math.sqrt(width)
    return (jnp.cos(angle_grid) * unit_scale, -jnp.sin(angle_grid) * unit_scale)


def rows_mix(table, block):
    return jnp.einsum("ab,nmbc->nmac", table, block, precision=lax.Precision.HIGHEST)


def cols_mix(block, table):
    return jnp.einsum("nmab,bc->nmac", block, table, precision=lax.Precision.HIGHEST)


def transform(real_part, imag_part, cos_table, sin_table):
    left_real = rows_mix(cos_table, real_part) - rows_mix(sin_table, imag_part)
    left_imag = rows_mix(cos_table, imag_part) + rows_mix(sin_table, real_part)
    out_real = cols_mix(left_real, cos_table) - cols_mix(left_imag, sin_table)
    out_imag = cols_mix(left_real, sin_table) + cols_mix(left_imag, cos_table)
    return (out_real, out_imag)


def lay_windows(shifted_grads):
    half_count = shifted_grads.shape[0]
    window = shifted_grads.shape[-1]
    moved = jnp.transpose(shifted_grads, (1, 2, 0, 3))
    return moved.reshape(2, shifted_grads.shape[2], half_count * window)


def row_gradient(patch_strip, probe_modes, offsets, measured, cos_table, sin_table):
    width = probe_modes.shape[-1]
    position_count = offsets.shape[0]
    full_width = patch_strip.shape[-1]
    spacing = full_width // position_count
    patches = jax.vmap(
        lambda col_start: lax.dynamic_slice(patch_strip, (0, 0, col_start), (2, width, width))
    )(offsets)
    probe_real = probe_modes[:, 0][None]
    probe_imag = probe_modes[:, 1][None]
    patch_real = patches[:, 0][:, None]
    patch_imag = patches[:, 1][:, None]
    exit_real = probe_real * patch_real - probe_imag * patch_imag
    exit_imag = probe_real * patch_imag + probe_imag * patch_real
    wave_real, wave_imag = transform(exit_real, exit_imag, cos_table, sin_table)
    magnitude = jnp.sqrt(
        jnp.sum(wave_real * wave_real + wave_imag * wave_imag, axis=1) + stabilizer
    )
    local_loss = 0.5 * jnp.sum((magnitude - measured) ** 2)
    weight = (1.0 - measured / magnitude)[:, None]
    back_real, back_imag = transform(weight * wave_real, weight * wave_imag, cos_table, -sin_table)
    grad_real = jnp.sum(probe_real * back_real + probe_imag * back_imag, axis=1)
    grad_imag = jnp.sum(probe_real * back_imag - probe_imag * back_real, axis=1)
    patch_grads = jnp.stack([grad_real, grad_imag], axis=1)
    window = 2 * spacing
    relative = offsets - jnp.arange(position_count, dtype=jnp.int32) * spacing
    padded = jnp.pad(patch_grads, ((0, 0), (0, 0), (0, 0), (0, window - width)))
    doubled = jnp.concatenate([padded, padded], axis=3)
    shifted = jax.vmap(
        lambda block, shift_by: lax.dynamic_slice_in_dim(block, window - shift_by, window, 2)
    )(doubled, relative)
    even_strip = lay_windows(shifted[0::2])
    odd_strip = lay_windows(shifted[1::2])
    odd_placed = jnp.pad(odd_strip, ((0, 0), (0, 0), (spacing, 0)))[:, :, :full_width]
    strip_grad = even_strip + odd_placed
    return (strip_grad, local_loss)


def shards(
    object_tiles, previous_tiles, probe_modes, amplitude, row_tops, scan_cols, restart, owner_map
):
    band_index = lax.axis_index("ty")
    column_index = lax.axis_index("tx")
    tile_count = lax.axis_size("tx")
    scan_row = band_index * tile_count + column_index
    row_top = row_tops[scan_row]
    owner_row = owner_map[band_index]
    inverse = jnp.zeros_like(owner_row).at[owner_row].set(jnp.arange(tile_count, dtype=jnp.int32))
    offsets = scan_cols[0]
    measured = amplitude[0]
    height = object_tiles.shape[1]
    tile_width = object_tiles.shape[2]
    full_width = tile_count * tile_width
    probe_size = probe_modes.shape[-1]
    cos_table, sin_table = dft_tables(probe_size)
    total_rows = lax.axis_size("ty") * tile_count
    loss_scale = 1.0 / (total_rows * offsets.shape[0] * probe_size * probe_size)
    table = momentum_table()
    current = object_tiles
    before = previous_tiles
    loss_list = []
    for iteration in range(ITERS):
        counter = restart[iteration]
        momentum = (table[counter - 1] - 1.0) / table[counter]
        extrapolated = current + momentum * (current - before)
        whole_band = lax.all_gather(extrapolated, "tx", axis=2, tiled=True)
        stored_rows = lax.dynamic_slice_in_dim(whole_band, row_top, probe_size, 1)
        patch_strip = jnp.take(
            stored_rows.reshape(2, probe_size, tile_count, tile_width), owner_row, axis=2
        ).reshape(2, probe_size, full_width)
        strip_grad, local_loss = row_gradient(
            patch_strip, probe_modes, offsets, measured, cos_table, sin_table
        )
        loss_list.append(local_loss)
        stored_grad = jnp.take(
            strip_grad.reshape(2, probe_size, tile_count, tile_width), inverse, axis=2
        ).reshape(2, probe_size, full_width)
        band_grad = lax.dynamic_update_slice_in_dim(
            jnp.zeros((2, height, full_width), jnp.float32), stored_grad, row_top, 1
        )
        tile_grad = lax.psum_scatter(band_grad, "tx", scatter_dimension=2, tiled=True)
        before = current
        current = extrapolated - step_length * tile_grad
    loss_sums = lax.psum(jnp.stack(loss_list), ("ty", "tx"))
    return (current, loss_sums * loss_scale)


def solution(mesh):
    in_specs = (
        P(None, "ty", "tx"),
        P(None, "ty", "tx"),
        P(),
        P(("ty", "tx"), None, None, None),
        P(),
        P(("ty", "tx"), None),
        P(),
        P(),
    )
    out_specs = (P(None, "ty", "tx"), P())
    return jax.shard_map(shards, mesh=mesh, in_specs=in_specs, out_specs=out_specs, check_vma=False)
```

profile of v0, /device:TPU:1, one launch (start us, length us, event | category | flops | bytes accessed | tf_op | source)
XLA Modules:
  0.0 917.0 jit_solution(14760953936843565914)
XLA Ops:
  25.9 69.6 %all-gather.3.cloned.1.call-done = f32[2,256,4096]{1,2,0:T(8,128)} async-done(((f32[2,256,256]{1,2,0:T(8,128)}), f32[2,256,4096]{1,2,0:T(8,128)}) %all-gather.3.cloned.1.call-update) | async-done | bytes 8388624 | tf_op jit(solution)/shard_map/all_gather | solution.py:120
  122.4 8.8 copy.143
  131.1 9.1 gather_fusion
  140.2 9.8 %fusion.360 = (f32[32,1,128,128]{2,1,3,0:T(1,128)}, f32[32,1,128,128]{2,1,3,0:T(1,128)}) fusion(f32[32,2,128,128]{2,1,3,0:T(2,128)} %gather_fusion), kind=kLoop, calls=%fused_computation.396 | loop fusion | bytes 8388608 | tf_op jit(solution)/shard_map/slice | solution.py:65
  155.3 8.9 fusion.39
  192.5 7.6 fusion.122
  229.3 7.6 fusion.85
  265.0 11.3 %add_reduce_fusion.2 = (f32[32,128,128]{2,1,0:T(8,128)}, f32[32,128,128]{2,1,0:T(8,128)}) fusion(f32[32,2,128,128]{3,2,1,0:T(8,128)S(1)} %fusion.64, f32[2,128,128]{2,1,0:T(8,128)S(1)} %get-tuple-element.25, f32[2,128,128]{2,1,0:T(8,128)S(1)} %get-tuple-element.24, f32[32,2,128,128]{3,2,1,0:T(8,128)S(1)} %fusion.18, f32[32,2,128,128]{3,2,1,0:T(8,128)S(1)} %fusion.82), kind=kOutput, calls=%fused_computation.64 | convolution fusion | flops 1619279872 | bytes 17039360 | tf_op jit(solution)/shard_map/nmab,bc->nmac/dot_general | solution.py:37
  288.8 10.8 %pad_maximum_fusion = f32[32,2,128,512]{2,1,0,3:T(2,128)} fusion(f32[32,2,128,256]{2,1,0,3:T(2,128)S(1)} %select_maximum_fusion.1), kind=kLoop, calls=%fused_computation.9 | loop fusion | flops 4194304 | bytes 25165824 | tf_op jit(solution)/shard_map/concatenate | solution.py:82
  299.6 20.7 %gather_fusion.2 = f32[32,2,128,256]{2,1,3,0:T(2,128)} fusion(f32[32,2,128,512]{2,1,0,3:T(2,128)} %pad_maximum_fusion, s32[32]{0:T(128)S(1)} %get-tuple-element.32), kind=kCustom, calls=%fused_computation.6 | custom fusion | bytes 16777728 | tf_op jit(solution)/shard_map/vmap()/gather | solution.py:84
  355.5 24.4 %dynamic_update_slice.6 = f32[2,256,4096]{1,2,0:T(8,128)} dynamic-update-slice(f32[2,256,4096]{1,2,0:T(8,128)} %broadcast.144.clone, f32[2,128,4096]{1,2,0:T(8,128)} %bitcast.232, s32[]{:T(128)} %constant.27.clone.1, s32[]{:T(128)S(6)} %select_n.135, s32[]{:T(128)} %constant.27.clone.1) | dynamic-update-slice | bytes 8388612 | tf_op jit(solution)/shard_map/dynamic_update_slice | solution.py:132
  381.4 82.4 %reduce-scatter.3.cloned.1.call-done = f32[2,256,256]{1,2,0:T(8,128)} async-done(((f32[2,256,4096]{1,2,0:T(8,128)}), f32[2,256,256]{1,2,0:T(8,128)}) %reduce-scatter.3.cloned.1.call-update) | async-done | bytes 524304 | tf_op jit(solution)/shard_map/reduce_scatter | solution.py:135
  465.8 72.1 %all-gather.5.cloned.1.call-done = f32[2,256,4096]{1,2,0:T(8,128)} async-done(((f32[2,256,256]{1,2,0:T(8,128)}), f32[2,256,4096]{1,2,0:T(8,128)}) %all-gather.5.cloned.1.call-update) | async-done | bytes 8388624 | tf_op jit(solution)/shard_map/all_gather | solution.py:120
  564.7 8.8 copy.171
  573.5 9.1 gather_fusion.1
  582.6 9.8 %fusion.359 = (f32[32,1,128,128]{2,1,3,0:T(1,128)}, f32[32,1,128,128]{2,1,3,0:T(1,128)}) fusion(f32[32,2,128,128]{2,1,3,0:T(2,128)} %gather_fusion.1), kind=kLoop, calls=%fused_computation.395 | loop fusion | bytes 8388608 | tf_op jit(solution)/shard_map/slice | solution.py:65
  597.6 8.9 fusion.35
  634.8 7.6 fusion.108
  709.8 10.8 %add_reduce_fusion = (f32[32,128,128]{2,1,0:T(8,128)}, f32[32,128,128]{2,1,0:T(8,128)}) fusion(f32[32,2,128,128]{3,2,1,0:T(8,128)S(1)} %fusion.76, f32[2,128,128]{2,1,0:T(8,128)S(1)} %get-tuple-element.25, f32[2,128,128]{2,1,0:T(8,128)S(1)} %get-tuple-element.24, f32[32,2,128,128]{3,2,1,0:T(8,128)S(1)} %fusion.2, f32[32,2,128,128]{3,2,1,0:T(8,128)S(1)} %fusion.88), kind=kOutput, calls=%fused_computation.55 | convolution fusion | flops 1619279872 | bytes 17039360 | tf_op jit(solution)/shard_map/nmab,bc->nmac/dot_general | solution.py:37
  733.1 10.8 %pad_maximum_fusion.1 = f32[32,2,128,512]{2,1,0,3:T(2,128)} fusion(f32[32,2,128,256]{2,1,0,3:T(2,128)S(1)} %select_maximum_fusion), kind=kLoop, calls=%fused_computation.10 | loop fusion | flops 4194304 | bytes 25165824 | tf_op jit(solution)/shard_map/concatenate | solution.py:82
  743.9 20.7 %gather_fusion.3 = f32[32,2,128,256]{2,1,3,0:T(2,128)} fusion(f32[32,2,128,512]{2,1,0,3:T(2,128)} %pad_maximum_fusion.1, s32[32]{0:T(128)S(1)} %get-tuple-element.32), kind=kCustom, calls=%fused_computation.7 | custom fusion | bytes 16777728 | tf_op jit(solution)/shard_map/vmap()/gather | solution.py:84
  799.9 24.4 %dynamic_update_slice.7 = f32[2,256,4096]{1,2,0:T(8,128)} dynamic-update-slice(f32[2,256,4096]{1,2,0:T(8,128)} %broadcast.144, f32[2,128,4096]{1,2,0:T(8,128)} %bitcast.229, s32[]{:T(128)} %constant.27.clone.1, s32[]{:T(128)S(6)} %select_n.135, s32[]{:T(128)} %constant.27.clone.1) | dynamic-update-slice | bytes 8388612 | tf_op jit(solution)/shard_map/dynamic_update_slice | solution.py:132
  825.6 65.4 %psum.7 = f32[2]{0:T(128)S(1)} all-reduce(f32[2]{0:T(128)S(1)} %pad_maximum_fusion.2), channel_id=1, replica_groups=mesh['ty'=8,'tx'=16] {'ty','tx'}, use_global_device_ids=true, to_apply=%region_11.13 | all-reduce | flops 2 | bytes 16 | tf_op jit(solution)/shard_map/psum | solution.py:138
  891.5 16.6 %reduce-scatter.5.cloned.1.call-done = f32[2,256,256]{1,2,0:T(8,128)} async-done(((f32[2,256,4096]{1,2,0:T(8,128)}), f32[2,256,256]{1,2,0:T(8,128)}) %reduce-scatter.5.cloned.1.call-update) | async-done | bytes 524304 | tf_op jit(solution)/shard_map/reduce_scatter | solution.py:135
  (113 shorter events, 354.5 us)
Async XLA Ops:
  7.2 14.1 %copy-start.9 = (s32[128]{0:T(128)S(1)}, s32[128]{0:T(128)}, u32[]{:S(2)}) copy-start(s32[128]{0:T(128)} %param.15) | copy-start | bytes 1540
  7.2 18.7 %copy-start.10 = (s32[1,32]{1,0:T(1,128)S(1)}, s32[1,32]{1,0:T(1,128)}, u32[]{:S(2)}) copy-start(s32[1,32]{1,0:T(1,128)} %param.16) | copy-start | bytes 388
  7.2 18.7 %copy-start.8 = (f32[2,2,128,128]{3,2,1,0:T(8,128)S(1)}, f32[2,2,128,128]{3,2,1,0:T(8,128)}, u32[]{:S(2)}) copy-start(f32[2,2,128,128]{3,2,1,0:T(8,128)} %param.13) | copy-start | bytes 786436
  7.2 88.3 %all-gather.3.cloned.1.call-start = ((), (), s32[]{:S(2)}) async-start(), calls=%async_computation.2 | async-start | bytes 8912896 | tf_op jit(solution)/shard_map/all_gather | solution.py:120
  21.2 442.5 %reduce-scatter.3.cloned.1.call-start = ((), (), s32[]{:S(2)}) async-start(), calls=%async_computation.3 | async-start | bytes 8912896 | tf_op jit(solution)/shard_map/reduce_scatter | solution.py:135
  155.3 8.9 copy-start
  207.1 7.2 copy-start.4
  214.3 7.9 copy-start.2
  379.9 83.9 %copy-start.7 = (f32[2,256,256]{1,2,0:T(8,128)S(1)}, f32[2,256,256]{1,2,0:T(8,128)}, u32[]{:S(2)}) copy-start(f32[2,256,256]{1,2,0:T(8,128)} %multiply_add_fusion.7) | copy-start | bytes 1572868
  379.9 157.9 %all-gather.5.cloned.1.call-start = ((), (), s32[]{:S(2)}) async-start(), calls=%async_computation.4 | async-start | bytes 8912896 | tf_op jit(solution)/shard_map/all_gather | solution.py:120
  465.7 442.4 %reduce-scatter.5.cloned.1.call-start = ((), (), s32[]{:S(2)}) async-start(), calls=%async_computation.5 | async-start | bytes 8912896 | tf_op jit(solution)/shard_map/reduce_scatter | solution.py:135
  597.6 8.9 copy-start.1
  649.5 7.2 copy-start.3
  649.5 7.2 copy-start.5
  824.3 83.9 %copy-start.6 = (f32[2,256,256]{1,2,0:T(8,128)S(1)}, f32[2,256,256]{1,2,0:T(8,128)}, u32[]{:S(2)}) copy-start(f32[2,256,256]{1,2,0:T(8,128)} %multiply_add_fusion.6) | copy-start | bytes 1572868
Sparse Core Ops, SparseCore 0:
  21.3 74.0 all-gather.2
  380.0 83.6 reduce-scatter.2
  466.5 71.3 all-gather.4
  824.4 83.6 reduce-scatter.4
where the time goes:
time: 930 us; the launch traced here: 917 us
  local copies, waits for them, and re-layouts  275 us (30%)
  waiting for transfers between devices  241 us (26%)
  matrix products  241 us (26%)
  other arithmetic  68.7 us (7%)
  blocking collectives  65.4 us (7%)
  between operations  26.9 us (3%)
    all_gather x2, waiting for transfers between devices, shards(): whole_band = lax.all_gather(extrapolated, 'tx', axis=2, tiled=True)  142 us
    dot_general x16, matrix products, cols_mix(): jnp.einsum('nmab,bc->nmac', block, table, precision=lax.Precision.HIGHEST)  121 us
    dot_general x16, matrix products, rows_mix(): jnp.einsum('ab,nmbc->nmac', table, block, precision=lax.Precision.HIGHEST)  120 us
    reduce_scatter x2, waiting for transfers between devices, shards(): lax.psum_scatter(band_grad, 'tx', scatter_dimension=2, tiled=True)  99 us
    psum x1, blocking collectives, shards(): loss_sums = lax.psum(jnp.stack(loss_list), ('ty', 'tx'))  65.4 us
    dynamic_update_slice x2, local copies, waits for them, and re-layouts, shards(): lax.dynamic_update_slice_in_dim(jnp.zeros((2, height, full_width), jnp.fl...  48.8 us
    gather x2, local copies, waits for them, and re-layouts, row_gradient(): lax.dynamic_slice_in_dim(block, window - shift_by, window, 2)  41.5 us
    concatenate x2, other arithmetic, row_gradient(): doubled = jnp.concatenate([padded, padded], axis=3)  21.6 us
  transfers between devices with their start and end apart: 4, of which 4 were waited for; matrix products, arithmetic and copies ran while one was open for 0% of the time, Pallas kernels for 0%

commit v1 on v0

v1 whole, which is shorter than its diff:
```python
import functools
import math

import jax
import jax.numpy as jnp
import ml_dtypes
import numpy as np
from jax import lax
from jax.experimental import pallas as pl
from jax.experimental.pallas import tpu as pltpu
from jax.sharding import PartitionSpec as P

START = 100
STABILIZER = 0.05
STEP = 0.25
N = 128
GROUP = 4
f32 = jnp.float32
bf16 = jnp.bfloat16
SMEM = pl.BlockSpec(memory_space=pltpu.SMEM)
VMEM = pl.BlockSpec(memory_space=pltpu.VMEM)
ANY = pl.BlockSpec(memory_space=pl.ANY)


def momentum_table():
    values = [1.0]
    for counter in range(START):
        last = values[-1]
        values.append((1.0 + (1.0 + 4.0 * last * last) ** 0.5) / 2.0)
    return jnp.asarray(values, f32)


def dft_tables():
    index = np.arange(N)
    angle = (index[:, None] * index[None, :] % N).astype(np.float64) * (2.0 * math.pi / N)
    cos, sin = np.cos(angle) / math.sqrt(N), np.sin(angle) / math.sqrt(N)

    def stacked(table):
        high = table.astype(ml_dtypes.bfloat16)
        low = (table - high.astype(np.float64)).astype(ml_dtypes.bfloat16)
        return jnp.asarray(np.concatenate([high, high, low], 0))

    return stacked(np.block([[cos, -sin], [sin, cos]])), stacked(np.block([[cos, sin], [-sin, cos]]))


def times_table(block, table):
    high = block.astype(bf16)
    low = (block - high.astype(f32)).astype(bf16)
    return jnp.dot(jnp.concatenate([high, low, high], 1), table, preferred_element_type=f32)


def flip_blocks(block):
    rows = []
    for at in range(0, block.shape[0], N):
        rows.append(jnp.concatenate([block[at : at + N, :N].T, block[at : at + N, N:].T], 1))
    return jnp.concatenate(rows, 0)


def add_positions(rows, offs, z, probe, amp, fwd, bwd, low, high, loss):
    lane = lax.broadcasted_iota(jnp.int32, (N, N), 1)
    first = pl.program_id(0) * GROUP
    waves, places = [], []
    for u in range(GROUP):
        top, off = rows[first + u], offs[first + u]
        inside = lane >= off
        patch = [
            pltpu.roll(jnp.where(inside, z[0, k, pl.ds(top, N), :], z[1, k, pl.ds(top, N), :]), (N - off) & (N - 1), 1)
            for k in range(2)
        ]
        for m in range(2):
            re, im = probe[m, 0], probe[m, 1]
            waves.append(jnp.concatenate([re * patch[0] - im * patch[1], re * patch[1] + im * patch[0]], 1))
        places.append((top, off, inside))
    wave = times_table(flip_blocks(times_table(jnp.concatenate(waves, 0), fwd[...])), fwd[...])
    backs = []
    total = jnp.zeros((8, N), f32)
    for u in range(GROUP):
        w = wave[u * 2 * N : (u + 1) * 2 * N]
        square = w * w
        square = square[:N] + square[N:]
        square = square[:, :N] + square[:, N:] + STABILIZER
        inverse = lax.rsqrt(square)
        measured = amp[u].T
        miss = square * inverse - measured
        total = total + jnp.sum((miss * miss).reshape(N // 8, 8, N), 0)
        weight = 1.0 - measured * inverse
        weight = jnp.concatenate([weight, weight], 1)
        backs += [weight * w[:N], weight * w[N:]]
    loss[...] += total
    back = times_table(flip_blocks(times_table(jnp.concatenate(backs, 0), bwd[...])), bwd[...])
    for u, (top, off, inside) in enumerate(places):
        grad_re, grad_im = 0.0, 0.0
        for m in range(2):
            re, im = probe[m, 0], probe[m, 1]
            b = back[(2 * u + m) * N : (2 * u + m + 1) * N]
            grad_re = grad_re + re * b[:, :N] + im * b[:, N:]
            grad_im = grad_im + re * b[:, N:] - im * b[:, :N]
        for k, grad in ((0, grad_re), (1, grad_im)):
            moved = pltpu.roll(grad, off, 1)
            low[k, pl.ds(top, N), :] += jnp.where(inside, moved, 0.0)
            high[k, pl.ds(top, N), :] += jnp.where(inside, 0.0, moved)


def clear(*refs):
    for ref in refs:
        ref[...] = jnp.zeros_like(ref)


def unit(tile, k, u):
    return tile[k, :, u * N : (u + 1) * N]


def even_first(rows, offs, beta, z0, obj, probe, amp, fwd, bwd, low, high, ahead, loss):
    @pl.when(pl.program_id(0) == 0)
    def _():
        clear(low, high, loss)

    add_positions(rows, offs, z0, probe, amp, fwd, bwd, low, high, loss)

    @pl.when(pl.program_id(0) == pl.num_programs(0) - 1)
    def _():
        b = beta[1]
        for k in range(2):
            ahead[k] = (1.0 + b) * (z0[0, k] - STEP * low[k]) - b * unit(obj, k, 0)


def odd_first(rows, offs, z0, halo, probe, amp, fwd, bwd, low, high, loss, z):
    @pl.when(pl.program_id(0) == 0)
    def _():
        clear(low, high, loss)
        z[0] = z0[1]
        z[1] = halo[...]

    add_positions(rows, offs, z, probe, amp, fwd, bwd, low, high, loss)


def odd_second(rows, offs, beta, z0, obj, even_high, odd_low, odd_high, ahead, probe, amp, fwd, bwd, low, high, loss, z):
    @pl.when(pl.program_id(0) == 0)
    def _():
        clear(low, high, loss)
        b = beta[1]
        for k in range(2):
            now = z0[1, k] - STEP * (even_high[k] + odd_low[k])
            z[0, k] = now + b * (now - unit(obj, k, 1))
            z[1, k] = ahead[k] - ((1.0 + b) * STEP) * odd_high[k]

    add_positions(rows, offs, z, probe, amp, fwd, bwd, low, high, loss)


def even_second(
    rows, offs, beta, z0, obj, even_low, even_high, odd_low, left, odd_low_second, loss_a, loss_b, loss_c,
    probe, amp, fwd, bwd, tile, sums, low, high, loss, z,
):
    @pl.when(pl.program_id(0) == 0)
    def _():
        clear(low, high, loss)
        b = beta[1]
        for k in range(2):
            now = z0[0, k] - STEP * (even_low[k] + left[k])
            z[0, k] = now + b * (now - unit(obj, k, 0))
            now = z0[1, k] - STEP * (even_high[k] + odd_low[k])
            z[1, k] = now + b * (now - unit(obj, k, 1))

    add_positions(rows, offs, z, probe, amp, fwd, bwd, low, high, loss)

    @pl.when(pl.program_id(0) == pl.num_programs(0) - 1)
    def _():
        for k in range(2):
            tile[k, :, :N] = z[0, k] - STEP * low[k]
            tile[k, :, N:] = z[1, k] - STEP * (high[k] + odd_low_second[k])
        before = jnp.sum(loss_a[...] + loss_b[...], axis=0, keepdims=True)
        after = jnp.sum(loss_c[...] + loss[...], axis=0, keepdims=True)
        lane = lax.broadcasted_iota(jnp.int32, (1, N), 1)
        line = jnp.where(lane < N // 2, before + pltpu.roll(before, N // 2, 1), after + pltpu.roll(after, N // 2, 1))
        sums[...] = jnp.broadcast_to(line, sums.shape)


def run(kernel, count, smalls, blocks, probe, amp, tables, outs, scratch):
    shape = lambda s: jax.ShapeDtypeStruct(s, f32)
    whole = lambda a: pl.BlockSpec(a.shape, lambda i, n=len(a.shape): (0,) * n)
    out_shape = [shape(s) for s in outs]
    return pl.pallas_call(
        kernel,
        grid=(count // GROUP,),
        out_shape=out_shape,
        in_specs=[SMEM] * len(smalls)
        + [whole(b) for b in blocks]
        + [whole(probe), pl.BlockSpec((GROUP, N, N), lambda i: (i, 0, 0))]
        + [whole(t) for t in tables],
        out_specs=[whole(o) for o in out_shape],
        scratch_shapes=scratch,
        compiler_params=pltpu.CompilerParams(vmem_limit_bytes=40 * 2**20),
        cost_estimate=pl.CostEstimate(flops=count * 400_000_000, bytes_accessed=2**22, transcendentals=count * N * N),
    )(*smalls, *blocks, probe, amp, *tables)


def prepare(inv, cols, beta, obj, prev, amp, z0, send_even, send_odd, chunk, places, sems):
    copies = []

    def copy(source, target):
        c = pltpu.make_async_copy(source, target, sems.at[len(copies)])
        c.start()
        copies.append(c)

    for d in range(16):
        col = inv[d]
        copy(amp.at[2 * col], send_even.at[d, pl.ds(0, N)])
        copy(amp.at[2 * col + 1], send_odd.at[d])
    b = beta[0]
    for u in range(2):
        for k in range(2):
            now = unit(obj, k, u)
            z0[u, k] = now + b * (now - unit(prev, k, u))
    lane = lax.broadcasted_iota(jnp.int32, (8, N), 1)
    for d in range(16):
        col = inv[d]
        even = cols[2 * col] - 2 * N * col
        odd = cols[2 * col + 1] - 2 * N * col - N
        places[d] = jnp.where(lane < N // 2, even, odd).astype(f32)
        chunk[d] = z0[0, d // 8, pl.ds(32 * (d % 8), 32), :]
    for d in range(16):
        copy(chunk.at[d], send_even.at[d, pl.ds(N, 32)])
        copy(places.at[d], send_even.at[d, pl.ds(N + 32, 8)])
    for c in copies:
        c.wait()


def pick(source, got, sent):
    for d in range(16):
        sent[d] = got[source[d]]


def pick_chunks(got, source, at):
    return pl.pallas_call(
        pick,
        grid=(1,),
        out_shape=jax.ShapeDtypeStruct((16, 32, N), f32),
        in_specs=[SMEM, pl.BlockSpec((16, 32, N), lambda i: (0, at, 0))],
        out_specs=pl.BlockSpec((16, 32, N), lambda i: (0, 0, 0)),
        compiler_params=pltpu.CompilerParams(vmem_limit_bytes=4 * 2**20),
    )(source, got)


def swap(block):
    return lax.all_to_all(block, "tx", 0, 0, tiled=True)


def shards(obj, prev, probe, amplitude, row_tops, scan_cols, restart, owner_map):
    band = lax.axis_index("ty")
    owner = owner_map[band]
    columns = jnp.arange(16, dtype=jnp.int32)
    inv = jnp.sum(jnp.where(owner[None, :] == columns[:, None], columns[None, :], 0), axis=1)
    hot = lambda want: jnp.sum(jnp.where(want[:, None] == columns[None, :], owner[None, :], 0), axis=1)
    from_right = hot((inv + 1) % 16)
    from_left = hot((inv + 15) % 16)
    rows = lax.dynamic_slice(row_tops, (band * 16,), (16,))
    table = momentum_table()
    beta = (table[restart - 1] - 1.0) / table[restart]
    tables = dft_tables()
    unit_shape = (2, 256, N)
    z_scratch = [pltpu.VMEM((2, 2, 256, N), f32)]

    z0, send_even, send_odd = pl.pallas_call(
        prepare,
        out_shape=[
            jax.ShapeDtypeStruct((2, 2, 256, N), f32),
            jax.ShapeDtypeStruct((16, N + 40, N), f32),
            jax.ShapeDtypeStruct((16, N, N), f32),
        ],
        in_specs=[SMEM, SMEM, SMEM, VMEM, VMEM, ANY],
        out_specs=[VMEM, ANY, ANY],
        scratch_shapes=[pltpu.VMEM((16, 32, N), f32), pltpu.VMEM((16, 8, N), f32), pltpu.SemaphoreType.DMA((64,))],
        compiler_params=pltpu.CompilerParams(vmem_limit_bytes=8 * 2**20),
    )(inv, scan_cols[0], beta, obj, prev, amplitude[0])

    amp_even = swap(send_even)
    amp_odd = swap(send_odd)
    offs = jnp.round(amp_even[:, N + 32, :]).astype(jnp.int32)
    off_even, off_odd = offs[:, 0], offs[:, N // 2]

    halo = swap(pick_chunks(amp_even, from_right, N // 32)).reshape(unit_shape)
    even_low, even_high, ahead, loss_a = run(
        even_first, 16, [rows, off_even, beta], [z0, obj], probe, amp_even, tables,
        [unit_shape, unit_shape, unit_shape, (8, N)], [],
    )
    ahead = swap(ahead.reshape(16, 32, N))
    odd_low, odd_high, loss_b = run(
        odd_first, 16, [rows, off_odd], [z0, halo], probe, amp_odd, tables, [unit_shape, unit_shape, (8, N)], z_scratch
    )
    ahead = swap(pick_chunks(ahead, from_right, 0)).reshape(unit_shape)
    left = swap(odd_high.reshape(16, 32, N))
    odd_low_second, odd_high_second, loss_c = run(
        odd_second, 16, [rows, off_odd, beta], [z0, obj, even_high, odd_low, odd_high, ahead], probe, amp_odd, tables,
        [unit_shape, unit_shape, (8, N)], z_scratch,
    )
    left = swap(pick_chunks(left, from_left, 0)).reshape(unit_shape)
    last = swap(odd_high_second.reshape(16, 32, N))
    tile, sums = run(
        even_second, 16, [rows, off_even, beta],
        [z0, obj, even_low, even_high, odd_low, left, odd_low_second, loss_a, loss_b, loss_c], probe, amp_even, tables,
        [(2, 256, 256), (N, N)], [pltpu.VMEM(unit_shape, f32), pltpu.VMEM(unit_shape, f32), pltpu.VMEM((8, N), f32)] + z_scratch,
    )
    last = swap(pick_chunks(last, from_left, 0)).reshape(unit_shape)
    tile = tile.at[:, :, :N].add(-STEP * last)
    sums = lax.all_to_all(sums, ("ty", "tx"), 0, 0, tiled=True)
    losses = jnp.sum(jnp.sum(sums, axis=0).reshape(2, N // 2), axis=1) * (0.5 / 67108864.0)
    return (tile, losses)


def solution(mesh):
    in_specs = (
        P(None, "ty", "tx"),
        P(None, "ty", "tx"),
        P(),
        P(("ty", "tx"), None, None, None),
        P(),
        P(("ty", "tx"), None),
        P(),
        P(),
    )
    return jax.shard_map(
        shards, mesh=mesh, in_specs=in_specs, out_specs=(P(None, "ty", "tx"), P()), check_vma=False
    )
```

time: 930 us -> 227 us (0.24); the launches traced: 917 us -> 225 us
  local copies, waits for them, and re-layouts: 275 us -> 31.4 us
  matrix products: 241 us -> 0 us
  waiting for transfers between devices: 241 us -> 41.7 us
  other arithmetic: 68.7 us -> 1.86 us
  Pallas kernels: 0 us -> 66.5 us
  starting transfers between devices: 0.16 us -> 54.7 us
  blocking collectives: 65.4 us -> 28 us
  between operations: 26.9 us -> 0.93 us
    dot_general x32 -> x0, matrix products: 241 us -> none  [the longest x16 121 us: cols_mix(): jnp.einsum('nmab,bc->nmac', block, table, precision=lax.Precision.HIGHEST)]
    all_gather x2 -> x0, waiting for transfers between devices: 142 us -> none  [shards(): whole_band = lax.all_gather(extrapolated, 'tx', axis=2, tiled=True)]
    reduce_scatter x2 -> x0, waiting for transfers between devices: 99 us -> none  [shards(): lax.psum_scatter(band_grad, 'tx', scatter_dimension=2, tiled=True)]
    gather x8 -> x2, local copies, waits for them, and re-layouts: 79.5 us -> 2.58 us  [shards(): beta = (table[restart - 1] - 1.0) / table[restart]]
    pallas_call x0 -> x9, Pallas kernels: none -> 66.5 us  [the longest x4 58.1 us: run(): pl.pallas_call(kernel, grid=(count // GROUP,), out_shape=out_shape, in_sp...]
    psum x1 -> x0, blocking collectives: 65.4 us -> none  [shards(): loss_sums = lax.psum(jnp.stack(loss_list), ('ty', 'tx'))]
    all_to_all x0 -> x9, starting transfers between devices: none -> 54.7 us  [the longest x8 39.9 us: swap(): return lax.all_to_all(block, 'tx', 0, 0, tiled=True)]
    dynamic_update_slice x2 -> x0, local copies, waits for them, and re-layouts: 48.8 us -> none  [shards(): lax.dynamic_update_slice_in_dim(jnp.zeros((2, height, full_width), jnp.fl...]
  transfers between devices with their start and end apart: 4 -> 9, of which waited for: 4 -> 5; matrix products, arithmetic and copies ran while one was open for 0% -> 1% of each run, Pallas kernels for 0% -> 28%
where the time goes in v1:
time: 227 us; the launch traced here: 225 us
  Pallas kernels  66.5 us (29%)
  starting transfers between devices  54.7 us (24%)
  waiting for transfers between devices  41.7 us (18%)
  local copies, waits for them, and re-layouts  31.4 us (14%)
  blocking collectives  28 us (12%)
    pallas_call x4, Pallas kernels, run(): pl.pallas_call(kernel, grid=(count // GROUP,), out_shape=out_shape, in_sp...  58.1 us
    all_to_all x8, starting transfers between devices, swap(): return lax.all_to_all(block, 'tx', 0, 0, tiled=True)  39.9 us
    all_to_all x8, waiting for transfers between devices, swap(): return lax.all_to_all(block, 'tx', 0, 0, tiled=True)  33.2 us
    unnamed x74, local copies, waits for them, and re-layouts  28.5 us
    all_to_all x1, blocking collectives, swap(): return lax.all_to_all(block, 'tx', 0, 0, tiled=True)  28 us
    all_to_all x1, starting transfers between devices, shards(): sums = lax.all_to_all(sums, ('ty', 'tx'), 0, 0, tiled=True)  14.8 us
    all_to_all x1, waiting for transfers between devices, shards(): sums = lax.all_to_all(sums, ('ty', 'tx'), 0, 0, tiled=True)  8.51 us
    pallas_call x4, Pallas kernels, pick_chunks(): pl.pallas_call(pick, grid=(1,), out_shape=jax.ShapeDtypeStruct((16, 32, N...  5.07 us
  transfers between devices with their start and end apart: 9, of which 5 were waited for; matrix products, arithmetic and copies ran while one was open for 1% of the time, Pallas kernels for 28%

profile of v1, /device:TPU:1, one launch (start us, length us, event | category | flops | bytes accessed | tf_op | source)
XLA Modules:
  0.0 225.1 jit_solution(17429752714443814490)
XLA Ops:
  2.1 1.3 gather_fusion
  3.4 1.3 gather_fusion.1
  4.7 1.6 copy-done.1
  7.0 3.3 %shard_map.122 = (f32[2,2,256,128]{3,2,1,0:T(8,128)S(1)}, f32[16,168,128]{2,1,0:T(8,128)S(1)}, f32[16,128,128]{2,1,0:T(8,128)}) custom-call(s32[16]{0:T(128)S(1)} %select_reduce_fusion.2.inv, s32[32]{0:T(128)S(1)} %bitcast.24, f32[2]{0:T(128)S(1)} %add_divide_fusion.beta, f32[2,256,256]{2,1,0:T(8,128)S(1)} %copy-done.3, f32[2,256,256]{2,1,0:T(8,128)S(1)} %copy-done.2, ...), custom_call_target="tpu_custom_call" | custom-call | tf_op jit(solution)/shard_map/pallas_call | solution.py:263
  11.1 28.0 %all_to_all.54.amp.got = f32[16,168,128]{2,1,0:T(8,128)S(1)} all-to-all(f32[16,168,128]{2,1,0:T(8,128)S(1)} %get-tuple-element.29), channel_id=1, replica_groups=mesh['ty'=8,'tx'=16] {'tx'}, dimensions={0} | all-to-all | bytes 2752512 | tf_op jit(solution)/shard_map/all_to_all | solution.py:245
  39.1 3.8 %all-to-all-start.2 = ((f32[16,128,128]{2,1,0:T(8,128)}), f32[16,128,128]{2,1,0:T(8,128)S(1)}, u32[]{:S(2)}, u32[]{:S(2)}) async-start(f32[16,128,128]{2,1,0:T(8,128)} %get-tuple-element.33), calls=%async_computation.2 | async-start | bytes 2097152 | tf_op jit(solution)/shard_map/all_to_all | solution.py:245
  43.2 1.3 shard_map.124
  44.7 13.4 %all-to-all-done.2.amp = f32[16,128,128]{2,1,0:T(8,128)S(1)} async-done(((f32[16,128,128]{2,1,0:T(8,128)}), f32[16,128,128]{2,1,0:T(8,128)S(1)}, u32[]{:S(2)}, u32[]{:S(2)}) %all-to-all-start.2) | async-done | bytes 1048608 | tf_op jit(solution)/shard_map/all_to_all | solution.py:245
  58.1 4.9 %all-to-all-start.1 = ((f32[16,32,128]{2,1,0:T(8,128)}), f32[16,32,128]{2,1,0:T(8,128)S(1)}, u32[]{:S(2)}, u32[]{:S(2)}) async-start(f32[16,32,128]{2,1,0:T(8,128)} %shard_map.124), calls=%async_computation.1 | async-start | bytes 524288 | tf_op jit(solution)/shard_map/all_to_all | solution.py:245
  66.1 14.0 %shard_map.123 = (f32[2,256,128]{2,1,0:T(8,128)S(1)}, f32[2,256,128]{2,1,0:T(8,128)S(1)}, f32[2,256,128]{2,1,0:T(8,128)S(1)}, f32[8,128]{1,0:T(8,128)S(1)}) custom-call(s32[16]{0:T(128)S(1)} %dynamic_slice.6.rows, s32[16]{0:T(128)S(1)} %get-tuple-element.45.offs, f32[2]{0:T(128)S(1)} %add_divide_fusion.beta, f32[2,2,256,128]{3,2,1,0:T(8,128)S(1)} %copy-done.9, ...), custom_call_target="tpu_custom_call" | custom-call | flops 6400000000 | bytes 4194304 | tf_op jit(solution)/shard_map/pallas_call | solution.py:182
  82.3 6.7 %all-to-all-start.5 = ((f32[16,32,128]{2,1,0:T(8,128)}), f32[16,32,128]{2,1,0:T(8,128)S(1)}, u32[]{:S(2)}, u32[]{:S(2)}) async-start(f32[16,32,128]{2,1,0:T(8,128)} %bitcast.23), calls=%async_computation.5 | async-start | bytes 524288 | tf_op jit(solution)/shard_map/all_to_all | solution.py:245
  93.0 13.9 %shard_map.125 = (f32[2,256,128]{2,1,0:T(8,128)S(1)}, f32[2,256,128]{2,1,0:T(8,128)S(1)}, f32[8,128]{1,0:T(8,128)S(1)}) custom-call(s32[16]{0:T(128)S(1)} %dynamic_slice.6.rows, s32[16]{0:T(128)S(1)} %get-tuple-element.44.offs, f32[2,2,256,128]{3,2,1,0:T(8,128)S(1)} %copy-done.10, f32[2,256,128]{2,1,0:T(8,128)S(1)} %bitcast.22, ...), custom_call_target="tpu_custom_call" | custom-call | flops 6400000000 | bytes 4194304 | tf_op jit(solution)/shard_map/pallas_call | solution.py:182
  108.3 6.7 %all-to-all-start.3 = ((f32[16,32,128]{2,1,0:T(8,128)}), f32[16,32,128]{2,1,0:T(8,128)S(1)}, u32[]{:S(2)}, u32[]{:S(2)}) async-start(f32[16,32,128]{2,1,0:T(8,128)} %bitcast.20), calls=%async_computation.3 | async-start | bytes 524288 | tf_op jit(solution)/shard_map/all_to_all | solution.py:245
  116.2 6.5 %all-to-all-done.3.got = f32[16,32,128]{2,1,0:T(8,128)S(1)} async-done(((f32[16,32,128]{2,1,0:T(8,128)}), f32[16,32,128]{2,1,0:T(8,128)S(1)}, u32[]{:S(2)}, u32[]{:S(2)}) %all-to-all-start.3) | async-done | bytes 262176 | tf_op jit(solution)/shard_map/all_to_all | solution.py:245
  122.7 4.2 %all-to-all-start.6 = ((f32[16,32,128]{2,1,0:T(8,128)}), f32[16,32,128]{2,1,0:T(8,128)}, u32[]{:S(2)}, u32[]{:S(2)}) async-start(f32[16,32,128]{2,1,0:T(8,128)} %shard_map.127), calls=%async_computation.6 | async-start | bytes 524288 | tf_op jit(solution)/shard_map/all_to_all | solution.py:245
  128.2 6.3 %all-to-all-done.6 = f32[16,32,128]{2,1,0:T(8,128)} async-done(((f32[16,32,128]{2,1,0:T(8,128)}), f32[16,32,128]{2,1,0:T(8,128)}, u32[]{:S(2)}, u32[]{:S(2)}) %all-to-all-start.6) | async-done | bytes 262176 | tf_op jit(solution)/shard_map/all_to_all | solution.py:245
  134.4 3.5 %all-to-all-start.4 = ((f32[16,32,128]{2,1,0:T(8,128)}), f32[16,32,128]{2,1,0:T(8,128)S(1)}, u32[]{:S(2)}, u32[]{:S(2)}) async-start(f32[16,32,128]{2,1,0:T(8,128)} %shard_map.126), calls=%async_computation.4 | async-start | bytes 524288 | tf_op jit(solution)/shard_map/all_to_all | solution.py:245
  143.9 15.1 %shard_map.128 = (f32[2,256,128]{2,1,0:T(8,128)S(1)}, f32[2,256,128]{2,1,0:T(8,128)}, f32[8,128]{1,0:T(8,128)S(1)}) custom-call(s32[16]{0:T(128)S(1)} %dynamic_slice.6.rows, s32[16]{0:T(128)S(1)} %get-tuple-element.44.offs, f32[2]{0:T(128)S(1)} %add_divide_fusion.beta, f32[2,2,256,128]{3,2,1,0:T(8,128)S(1)} %copy-done.11, f32[2,256,256]{2,1,0:T(8,128)S(1)} %copy-done.3, ...), custom_call_target="tpu_custom_call" | custom-call | flops 6400000000 | bytes 4194304 | tf_op jit(solution)/shard_map/pallas_call | solution.py:182
  159.7 6.6 %all-to-all-start.7 = ((f32[16,32,128]{2,1,0:T(8,128)}), f32[16,32,128]{2,1,0:T(8,128)S(1)}, u32[]{:S(2)}, u32[]{:S(2)}) async-start(f32[16,32,128]{2,1,0:T(8,128)} %bitcast.9), calls=%async_computation.7 | async-start | bytes 524288 | tf_op jit(solution)/shard_map/all_to_all | solution.py:245
  173.2 15.0 %shard_map.129 = (f32[2,256,256]{2,1,0:T(8,128)}, f32[128,128]{1,0:T(8,128)}) custom-call(s32[16]{0:T(128)S(1)} %dynamic_slice.6.rows, s32[16]{0:T(128)S(1)} %get-tuple-element.45.offs, f32[2]{0:T(128)S(1)} %add_divide_fusion.beta, f32[2,2,256,128]{3,2,1,0:T(8,128)S(1)} %copy-done.12, f32[2,256,256]{2,1,0:T(8,128)S(1)} %copy-done.3, ...), custom_call_target="tpu_custom_call" | custom-call | flops 6400000000 | bytes 4194304 | tf_op jit(solution)/shard_map/pallas_call | solution.py:182
  188.2 14.8 %all-to-all-start.9 = ((f32[128,1,128]{2,1,0:T(1,128)}), f32[128,1,128]{2,1,0:T(1,128)S(1)}, u32[]{:S(2)}, u32[]{:S(2)}) async-start(f32[128,1,128]{2,1,0:T(1,128)} %bitcast.12), calls=%async_computation.9 | async-start | bytes 131072 | tf_op jit(solution)/shard_map/all_to_all | solution.py:305
  204.2 8.5 %all-to-all-done.9 = f32[128,1,128]{2,1,0:T(1,128)S(1)} async-done(((f32[128,1,128]{2,1,0:T(1,128)}), f32[128,1,128]{2,1,0:T(1,128)S(1)}, u32[]{:S(2)}, u32[]{:S(2)}) %all-to-all-start.9) | async-done | bytes 65568 | tf_op jit(solution)/shard_map/all_to_all | solution.py:305
  212.7 3.5 %all-to-all-start.8 = ((f32[16,32,128]{2,1,0:T(8,128)}), f32[16,32,128]{2,1,0:T(8,128)S(1)}, u32[]{:S(2)}, u32[]{:S(2)}) async-start(f32[16,32,128]{2,1,0:T(8,128)} %shard_map.130), calls=%async_computation.8 | async-start | bytes 524288 | tf_op jit(solution)/shard_map/all_to_all | solution.py:245
  217.1 7.0 %all-to-all-done.8 = f32[16,32,128]{2,1,0:T(8,128)S(1)} async-done(((f32[16,32,128]{2,1,0:T(8,128)}), f32[16,32,128]{2,1,0:T(8,128)S(1)}, u32[]{:S(2)}, u32[]{:S(2)}) %all-to-all-start.8) | async-done | bytes 262176 | tf_op jit(solution)/shard_map/all_to_all | solution.py:245
  (96 shorter events, 32.9 us)
Async XLA Ops:
  0.6 4.1 %copy-start.3 = (f32[2,256,256]{2,1,0:T(8,128)S(1)}, f32[2,256,256]{2,1,0:T(8,128)}, u32[]{:S(2)}) copy-start(f32[2,256,256]{2,1,0:T(8,128)} %obj.7) | copy-start | bytes 1572868
  0.7 4.1 %copy-start.2 = (f32[2,256,256]{2,1,0:T(8,128)S(1)}, f32[2,256,256]{2,1,0:T(8,128)}, u32[]{:S(2)}) copy-start(f32[2,256,256]{2,1,0:T(8,128)} %prev.1) | copy-start | bytes 1572868
  4.7 1.6 copy-start.1
  39.1 3.8 %copy-start.36 = (s32[128]{0:T(128)S(1)}, s32[128]{0:T(128)}, u32[]{:S(2)}) copy-start(s32[128]{0:T(128)} %param.17) | copy-start | bytes 1540
  39.1 19.0 %all-to-all-start.2 = ((f32[16,128,128]{2,1,0:T(8,128)}), f32[16,128,128]{2,1,0:T(8,128)S(1)}, u32[]{:S(2)}, u32[]{:S(2)}) async-start(f32[16,128,128]{2,1,0:T(8,128)} %get-tuple-element.33), calls=%async_computation.2 | async-start | bytes 2097152 | tf_op jit(solution)/shard_map/all_to_all | solution.py:245
  42.9 20.2 %copy-start.13 = (f32[2,2,128,128]{3,2,1,0:T(8,128)S(1)}, f32[2,2,128,128]{3,2,1,0:T(8,128)}, u32[]{:S(2)}) copy-start(f32[2,2,128,128]{3,2,1,0:T(8,128)} %probe.7) | copy-start | bytes 786436
  58.1 24.2 %all-to-all-start.1 = ((f32[16,32,128]{2,1,0:T(8,128)}), f32[16,32,128]{2,1,0:T(8,128)S(1)}, u32[]{:S(2)}, u32[]{:S(2)}) async-start(f32[16,32,128]{2,1,0:T(8,128)} %shard_map.124), calls=%async_computation.1 | async-start | bytes 524288 | tf_op jit(solution)/shard_map/all_to_all | solution.py:245
  63.1 1.0 copy-start.9
  64.1 1.0 copy-start.16
  82.3 26.0 %all-to-all-start.5 = ((f32[16,32,128]{2,1,0:T(8,128)}), f32[16,32,128]{2,1,0:T(8,128)S(1)}, u32[]{:S(2)}, u32[]{:S(2)}) async-start(f32[16,32,128]{2,1,0:T(8,128)} %bitcast.23), calls=%async_computation.5 | async-start | bytes 524288 | tf_op jit(solution)/shard_map/all_to_all | solution.py:245
  89.0 1.0 copy-start.10
  91.0 1.0 copy-start.17
  108.3 14.4 %all-to-all-start.3 = ((f32[16,32,128]{2,1,0:T(8,128)}), f32[16,32,128]{2,1,0:T(8,128)S(1)}, u32[]{:S(2)}, u32[]{:S(2)}) async-start(f32[16,32,128]{2,1,0:T(8,128)} %bitcast.20), calls=%async_computation.3 | async-start | bytes 524288 | tf_op jit(solution)/shard_map/all_to_all | solution.py:245
  116.2 21.8 %copy-start.15 = (f32[2,2,128,128]{3,2,1,0:T(8,128)S(1)}, f32[2,2,128,128]{3,2,1,0:T(8,128)}, u32[]{:S(2)}) copy-start(f32[2,2,128,128]{3,2,1,0:T(8,128)} %probe.7) | copy-start | bytes 786436
  122.7 11.8 %all-to-all-start.6 = ((f32[16,32,128]{2,1,0:T(8,128)}), f32[16,32,128]{2,1,0:T(8,128)}, u32[]{:S(2)}, u32[]{:S(2)}) async-start(f32[16,32,128]{2,1,0:T(8,128)} %shard_map.127), calls=%async_computation.6 | async-start | bytes 524288 | tf_op jit(solution)/shard_map/all_to_all | solution.py:245
  134.4 25.3 %all-to-all-start.4 = ((f32[16,32,128]{2,1,0:T(8,128)}), f32[16,32,128]{2,1,0:T(8,128)S(1)}, u32[]{:S(2)}, u32[]{:S(2)}) async-start(f32[16,32,128]{2,1,0:T(8,128)} %shard_map.126), calls=%async_computation.4 | async-start | bytes 524288 | tf_op jit(solution)/shard_map/all_to_all | solution.py:245
  138.9 1.0 copy-start.11
  159.7 28.5 %all-to-all-start.7 = ((f32[16,32,128]{2,1,0:T(8,128)}), f32[16,32,128]{2,1,0:T(8,128)S(1)}, u32[]{:S(2)}, u32[]{:S(2)}) async-start(f32[16,32,128]{2,1,0:T(8,128)} %bitcast.9), calls=%async_computation.7 | async-start | bytes 524288 | tf_op jit(solution)/shard_map/all_to_all | solution.py:245
  166.3 1.0 copy-start.12
  167.4 1.0 copy-start.19
  168.4 1.0 copy-start.23
  188.2 36.0 %copy-start.34 = (f32[2,256,256]{2,1,0:T(8,128)S(1)}, f32[2,256,256]{2,1,0:T(8,128)}, u32[]{:S(2)}) copy-start(f32[2,256,256]{2,1,0:T(8,128)} %get-tuple-element.41) | copy-start | bytes 1572868
  188.2 24.5 %all-to-all-start.9 = ((f32[128,1,128]{2,1,0:T(1,128)}), f32[128,1,128]{2,1,0:T(1,128)S(1)}, u32[]{:S(2)}, u32[]{:S(2)}) async-start(f32[128,1,128]{2,1,0:T(1,128)} %bitcast.12), calls=%async_computation.9 | async-start | bytes 131072 | tf_op jit(solution)/shard_map/all_to_all | solution.py:305
  212.7 11.5 %all-to-all-start.8 = ((f32[16,32,128]{2,1,0:T(8,128)}), f32[16,32,128]{2,1,0:T(8,128)S(1)}, u32[]{:S(2)}, u32[]{:S(2)}) async-start(f32[16,32,128]{2,1,0:T(8,128)} %shard_map.130), calls=%async_computation.8 | async-start | bytes 524288 | tf_op jit(solution)/shard_map/all_to_all | solution.py:245
  (22 other events, 18.8 us)

commit v2 on v1

v2 whole, which is shorter than its diff:
```python
import functools
import math

import jax
import jax.numpy as jnp
import ml_dtypes
import numpy as np
from jax import lax
from jax.experimental import pallas as pl
from jax.experimental.pallas import tpu as pltpu
from jax.sharding import PartitionSpec as P

START = 100
STABILIZER = 0.05
STEP = 0.25
N = 128
GROUP = 4
VMEM_BYTES = 60 * 2**20
f32 = jnp.float32
bf16 = jnp.bfloat16
SMEM = pl.BlockSpec(memory_space=pltpu.SMEM)
VMEM = pl.BlockSpec(memory_space=pltpu.VMEM)
ANY = pl.BlockSpec(memory_space=pl.ANY)


def momentum_table():
    values = [1.0]
    for counter in range(START):
        last = values[-1]
        values.append((1.0 + (1.0 + 4.0 * last * last) ** 0.5) / 2.0)
    return jnp.asarray(values, f32)


def dft_tables():
    index = np.arange(N)
    angle = (index[:, None] * index[None, :] % N).astype(np.float64) * (2.0 * math.pi / N)
    cos, sin = np.cos(angle) / math.sqrt(N), np.sin(angle) / math.sqrt(N)

    def stacked(table):
        high = table.astype(ml_dtypes.bfloat16)
        low = (table - high.astype(np.float64)).astype(ml_dtypes.bfloat16)
        return jnp.asarray(np.concatenate([high, high, low], 0))

    return stacked(np.block([[cos, -sin], [sin, cos]])), stacked(np.block([[cos, sin], [-sin, cos]]))


def times_table(block, table):
    high = block.astype(bf16)
    low = (block - high.astype(f32)).astype(bf16)
    return jnp.dot(jnp.concatenate([high, low, high], 1), table, preferred_element_type=f32)


def flip_blocks(block):
    rows = []
    for at in range(0, block.shape[0], N):
        rows.append(jnp.concatenate([block[at : at + N, :N].T, block[at : at + N, N:].T], 1))
    return jnp.concatenate(rows, 0)


def add_positions(rows, offs, z, probe, amp, fwd, bwd, low, high, loss):
    lane = lax.broadcasted_iota(jnp.int32, (N, N), 1)
    first = pl.program_id(0) * GROUP
    waves, places = [], []
    for u in range(GROUP):
        top, off = rows[first + u], offs[first + u]
        inside = lane >= off
        patch = [
            pltpu.roll(jnp.where(inside, z[0, k, pl.ds(top, N), :], z[1, k, pl.ds(top, N), :]), (N - off) & (N - 1), 1)
            for k in range(2)
        ]
        for m in range(2):
            re, im = probe[m, 0], probe[m, 1]
            waves.append(jnp.concatenate([re * patch[0] - im * patch[1], re * patch[1] + im * patch[0]], 1))
        places.append((top, off, inside))
    wave = times_table(flip_blocks(times_table(jnp.concatenate(waves, 0), fwd[...])), fwd[...])
    backs = []
    total = jnp.zeros((8, N), f32)
    for u in range(GROUP):
        w = wave[u * 2 * N : (u + 1) * 2 * N]
        square = w * w
        square = square[:N] + square[N:]
        square = square[:, :N] + square[:, N:] + STABILIZER
        inverse = lax.rsqrt(square)
        measured = amp[u].T
        miss = square * inverse - measured
        total = total + jnp.sum((miss * miss).reshape(N // 8, 8, N), 0)
        weight = 1.0 - measured * inverse
        weight = jnp.concatenate([weight, weight], 1)
        backs += [weight * w[:N], weight * w[N:]]
    loss[...] += total
    back = times_table(flip_blocks(times_table(jnp.concatenate(backs, 0), bwd[...])), bwd[...])
    for u, (top, off, inside) in enumerate(places):
        grad_re, grad_im = 0.0, 0.0
        for m in range(2):
            re, im = probe[m, 0], probe[m, 1]
            b = back[(2 * u + m) * N : (2 * u + m + 1) * N]
            grad_re = grad_re + re * b[:, :N] + im * b[:, N:]
            grad_im = grad_im + re * b[:, N:] - im * b[:, :N]
        for k, grad in ((0, grad_re), (1, grad_im)):
            moved = pltpu.roll(grad, off, 1)
            low[k, pl.ds(top, N), :] += jnp.where(inside, moved, 0.0)
            high[k, pl.ds(top, N), :] += jnp.where(inside, 0.0, moved)


def clear(*refs):
    for ref in refs:
        ref[...] = jnp.zeros_like(ref)


def unit(tile, k, u):
    return tile[k, :, u * N : (u + 1) * N]


def chunk_of(ref, d):
    return ref.at[d // 8, pl.ds(32 * (d % 8), 32)]


def even_first(rows, offs, beta, z0, obj, probe, amp, fwd, bwd, low, high, ahead, loss):
    @pl.when(pl.program_id(0) == 0)
    def _():
        clear(low, high, loss)

    add_positions(rows, offs, z0, probe, amp, fwd, bwd, low, high, loss)

    @pl.when(pl.program_id(0) == pl.num_programs(0) - 1)
    def _():
        b = beta[1]
        for k in range(2):
            ahead[k] = (1.0 + b) * (z0[0, k] - STEP * low[k]) - b * unit(obj, k, 0)


def odd_first(rows, offs, beta, z0, obj, even_high, ahead, halo, probe, amp, fwd, bwd, mid, send, loss, low, high, z):
    @pl.when(pl.program_id(0) == 0)
    def _():
        clear(low, high, loss)
        z[0] = z0[1]
        for d in range(16):
            chunk_of(z.at[1], d)[...] = halo[d]

    add_positions(rows, offs, z, probe, amp, fwd, bwd, low, high, loss)

    @pl.when(pl.program_id(0) == pl.num_programs(0) - 1)
    def _():
        b = beta[1]
        for k in range(2):
            now = z0[1, k] - STEP * (even_high[k] + low[k])
            mid[k] = now + b * (now - unit(obj, k, 1))
        for d in range(16):
            send[d, :32] = chunk_of(ahead, d)[...]
            send[d, 32:] = chunk_of(high, d)[...]


def odd_second(rows, offs, mid, got, probe, amp, fwd, bwd, low, high, loss, z):
    @pl.when(pl.program_id(0) == 0)
    def _():
        clear(low, high, loss)
        z[0] = mid[...]
        for d in range(16):
            chunk_of(z.at[1], d)[...] = got[d, 32:]

    add_positions(rows, offs, z, probe, amp, fwd, bwd, low, high, loss)


def even_second(
    rows, offs, mid, got, odd_low, loss_a, loss_b, loss_c, probe, amp, fwd, bwd, tile, sums, low, high, loss, z
):
    @pl.when(pl.program_id(0) == 0)
    def _():
        clear(low, high, loss)
        z[1] = mid[...]
        for d in range(16):
            chunk_of(z.at[0], d)[...] = got[d, :32]

    add_positions(rows, offs, z, probe, amp, fwd, bwd, low, high, loss)

    @pl.when(pl.program_id(0) == pl.num_programs(0) - 1)
    def _():
        for k in range(2):
            tile[k, :, :N] = z[0, k] - STEP * low[k]
            tile[k, :, N:] = z[1, k] - STEP * (high[k] + odd_low[k])
        before = jnp.sum(loss_a[...] + loss_b[...], axis=0, keepdims=True)
        after = jnp.sum(loss_c[...] + loss[...], axis=0, keepdims=True)
        lane = lax.broadcasted_iota(jnp.int32, (1, N), 1)
        line = jnp.where(lane < N // 2, before + pltpu.roll(before, N // 2, 1), after + pltpu.roll(after, N // 2, 1))
        sums[...] = jnp.broadcast_to(line, sums.shape)


def run(kernel, count, smalls, blocks, probe, amp, tables, outs, scratch):
    shape = lambda s: jax.ShapeDtypeStruct(s, f32)
    whole = lambda a: pl.BlockSpec(a.shape, lambda i, n=len(a.shape): (0,) * n)
    out_shape = [shape(s) for s in outs]
    return pl.pallas_call(
        kernel,
        grid=(count // GROUP,),
        out_shape=out_shape,
        in_specs=[SMEM] * len(smalls)
        + [spec or whole(b) for b, spec in blocks]
        + [whole(probe), pl.BlockSpec((GROUP, N, N), lambda i: (i, 0, 0))]
        + [whole(t) for t in tables],
        out_specs=[whole(o) for o in out_shape],
        scratch_shapes=scratch,
        compiler_params=pltpu.CompilerParams(vmem_limit_bytes=VMEM_BYTES),
        cost_estimate=pl.CostEstimate(flops=count * 400_000_000, bytes_accessed=2**22, transcendentals=count * N * N),
    )(*smalls, *[b for b, _ in blocks], probe, amp, *tables)


def small_call(kernel, args, outs, scratch=()):
    return pl.pallas_call(
        kernel,
        out_shape=[jax.ShapeDtypeStruct(s, d) for s, d, _ in outs],
        in_specs=[spec for _, spec in args],
        out_specs=[spec for _, _, spec in outs],
        scratch_shapes=list(scratch),
        compiler_params=pltpu.CompilerParams(vmem_limit_bytes=VMEM_BYTES),
    )(*[a for a, _ in args])


def start_all(pairs, sems):
    copies = [pltpu.make_async_copy(a, b, sems.at[i]) for i, (a, b) in enumerate(pairs)]
    for c in copies:
        c.start()
    return copies


def prepare(
    owner_map, row_tops, restart, table, cols, obj, prev, amp,
    z0, send, rows, inv, right, left, beta, sems,
):
    band = lax.axis_index("ty")
    for c in range(16):
        owner = owner_map[band, c]
        inv[owner] = c
        right[owner] = owner_map[band, (c + 1) % 16]
        left[owner] = owner_map[band, (c + 15) % 16]
        rows[c] = row_tops[band * 16 + c]
    copies = start_all([(amp.at[2 * inv[d]], send.at[d, pl.ds(0, N)]) for d in range(16)], sems)
    for k in range(2):
        beta[k] = (table[restart[k] - 1] - 1.0) / table[restart[k]]
    b = beta[0]
    for u in range(2):
        for k in range(2):
            now = unit(obj, k, u)
            z0[u, k] = now + b * (now - unit(prev, k, u))
    lane = lax.broadcasted_iota(jnp.int32, (8, N), 1)
    for d in range(16):
        col = inv[d]
        even = cols[0, 2 * col] - 2 * N * col
        odd = cols[0, 2 * col + 1] - 2 * N * col - N
        send[d, N : N + 32] = chunk_of(z0.at[0], d)[...]
        send[d, N + 32 :] = jnp.where(lane < N // 2, even, odd).astype(f32)
    for c in copies:
        c.wait()


def pass_halo(right, inv, got, amp, send, sems, more_sems):
    copies = start_all([(amp.at[2 * inv[d] + 1], send.at[d, pl.ds(0, N)]) for d in range(16)], sems)
    copies += start_all([(got.at[right[d], pl.ds(N, 32)], send.at[d, pl.ds(N, 32)]) for d in range(16)], more_sems)
    for c in copies:
        c.wait()


def join(left, right, beta, got, send, total):
    scale = (1.0 + beta[1]) * STEP
    for d in range(16):
        total[d] = got[d, :32] - scale * got[left[d], 32:]
    for d in range(16):
        send[d, :32] = total[d]
        send[d, 32:] = total[right[d]]


def pass_last(left, got, sums, send):
    for d in range(16):
        send[d, :32] = got[left[d]]
        send[d, 32:] = sums[...]


def finish(tile, got, out, sums):
    total = got[0, 32:]
    for d in range(1, 16):
        total = total + got[d, 32:]
    sums[...] = total
    for k in range(2):
        out[k, :, N:] = tile[k, :, N:]
    for d in range(16):
        at = pl.ds(32 * (d % 8), 32)
        out[d // 8, at, :N] = tile[d // 8, at, :N] - STEP * got[d, :32]


def swap(block, axis="tx"):
    return lax.all_to_all(block, axis, 0, 0, tiled=True)


def shards(obj, prev, probe, amplitude, row_tops, scan_cols, restart, owner_map):
    tables = dft_tables()
    unit_shape = (2, 256, N)
    unit_vmem = pltpu.VMEM(unit_shape, f32)
    z_vmem = pltpu.VMEM((2,) + unit_shape, f32)
    ints = ((16,), jnp.int32, SMEM)

    z0, send, rows, inv, right, left, beta = small_call(
        prepare,
        [(owner_map, SMEM), (row_tops, SMEM), (restart, SMEM), (momentum_table(), SMEM), (scan_cols, SMEM),
         (obj, VMEM), (prev, VMEM), (amplitude[0], ANY)],
        [((2,) + unit_shape, f32, VMEM), ((16, N + 40, N), f32, VMEM), ints, ints, ints, ints, ((2,), f32, SMEM)],
        [pltpu.SemaphoreType.DMA((16,))],
    )
    amp_even = swap(send)
    (send,) = small_call(
        pass_halo,
        [(right, SMEM), (inv, SMEM), (amp_even, ANY), (amplitude[0], ANY)],
        [((16, N + 32, N), f32, VMEM)],
        [pltpu.SemaphoreType.DMA((16,)), pltpu.SemaphoreType.DMA((16,))],
    )
    amp_odd = swap(send)
    offs = jnp.round(amp_even[:, N + 32, :]).astype(jnp.int32)
    off_even, off_odd = offs[:, 0], offs[:, N // 2]

    even_low, even_high, ahead, loss_a = run(
        even_first, 16, [rows, off_even, beta], [(z0, None), (obj, None)], probe, amp_even, tables,
        [unit_shape, unit_shape, unit_shape, (8, N)], [],
    )
    mid, send, loss_b = run(
        odd_first, 16, [rows, off_odd, beta],
        [(z0, None), (obj, None), (even_high, None), (ahead, None),
         (amp_odd, pl.BlockSpec((16, 32, N), lambda i: (0, N // 32, 0)))],
        probe, amp_odd, tables, [unit_shape, (16, 64, N), (8, N)], [unit_vmem, unit_vmem, z_vmem],
    )
    got = swap(send)
    (send,) = small_call(
        join, [(left, SMEM), (right, SMEM), (beta, SMEM), (got, VMEM)], [((16, 64, N), f32, VMEM)],
        [pltpu.VMEM((16, 32, N), f32)],
    )
    got = swap(send)
    odd_low, odd_high, loss_c = run(
        odd_second, 16, [rows, off_odd], [(mid, None), (got, None)], probe, amp_odd, tables,
        [unit_shape, unit_shape, (8, N)], [z_vmem],
    )
    last = swap(odd_high.reshape(16, 32, N))
    tile, sums = run(
        even_second, 16, [rows, off_even],
        [(x, None) for x in (mid, got, odd_low, loss_a, loss_b, loss_c)], probe, amp_even, tables,
        [(2, 256, 256), (8, N)], [unit_vmem, unit_vmem, pltpu.VMEM((8, N), f32), z_vmem],
    )
    (send,) = small_call(
        pass_last, [(left, SMEM), (last, VMEM), (sums, VMEM)], [((16, 40, N), f32, VMEM)]
    )
    got = swap(send)
    tile, sums = small_call(
        finish, [(tile, VMEM), (got, VMEM)], [((2, 256, 256), f32, VMEM), ((8, N), f32, VMEM)]
    )
    sums = swap(sums, "ty")
    losses = jnp.sum(jnp.sum(sums, axis=0).reshape(2, N // 2), axis=1) * (0.5 / 67108864.0)
    return (tile, losses)


def solution(mesh):
    in_specs = (
        P(None, "ty", "tx"),
        P(None, "ty", "tx"),
        P(),
        P(("ty", "tx"), None, None, None),
        P(),
        P(("ty", "tx"), None),
        P(),
        P(),
    )
    return jax.shard_map(
        shards, mesh=mesh, in_specs=in_specs, out_specs=(P(None, "ty", "tx"), P()), check_vma=False
    )
```

time: 227 us -> 177 us (0.78)
  blocking collectives: 28 us -> 86.8 us
  starting transfers between devices: 54.7 us -> 7.43 us
  waiting for transfers between devices: 41.7 us -> 0.33 us
  local copies, waits for them, and re-layouts: 31.4 us -> 2.58 us
  Pallas kernels: 66.5 us -> 76.7 us
    all_to_all x1 -> x5, blocking collectives: 28 us -> 86.8 us  [swap(): return lax.all_to_all(block, axis, 0, 0, tiled=True)]
    all_to_all x9 -> x2, starting transfers between devices: 54.7 us -> 7.43 us  [swap(): return lax.all_to_all(block, axis, 0, 0, tiled=True)]
    all_to_all x9 -> x2, waiting for transfers between devices: 41.7 us -> 0.33 us  [swap(): return lax.all_to_all(block, axis, 0, 0, tiled=True)]
    unnamed x74 -> x4, local copies, waits for them, and re-layouts: 28.5 us -> 1.75 us
    pallas_call x4, Pallas kernels: 58.1 us -> 63.9 us  [run(): pl.pallas_call(kernel, grid=(count // GROUP,), out_shape=out_shape, in_sp...]
    pallas_call x5, Pallas kernels: 8.42 us -> 12.8 us  [small_call(): pl.pallas_call(kernel, out_shape=[jax.ShapeDtypeStruct(s, d) for s, d, _...]
    gather x2 -> x0, local copies, waits for them, and re-layouts: 2.58 us -> none  [shards(): beta = (table[restart - 1] - 1.0) / table[restart]]
  transfers between devices with their start and end apart: 9 -> 2, of which waited for: 5 -> 1; matrix products, arithmetic and copies ran while one was open for 1% -> 1% of each run, Pallas kernels for 28% -> 18%
where the time goes in v2:
time: 177 us; the launch traced here: 176 us
  blocking collectives  86.8 us (49%)
  Pallas kernels  76.7 us (43%)
  starting transfers between devices  7.43 us (4%)
  local copies, waits for them, and re-layouts  2.58 us (1%)
    all_to_all x5, blocking collectives, swap(): return lax.all_to_all(block, axis, 0, 0, tiled=True)  86.8 us
    pallas_call x4, Pallas kernels, run(): pl.pallas_call(kernel, grid=(count // GROUP,), out_shape=out_shape, in_sp...  63.9 us
    pallas_call x5, Pallas kernels, small_call(): pl.pallas_call(kernel, out_shape=[jax.ShapeDtypeStruct(s, d) for s, d, _...  12.8 us
    all_to_all x2, starting transfers between devices, swap(): return lax.all_to_all(block, axis, 0, 0, tiled=True)  7.43 us
  transfers between devices with their start and end apart: 2, of which 1 were waited for; matrix products, arithmetic and copies ran while one was open for 1% of the time, Pallas kernels for 18%

profile of v2, /device:TPU:1, one launch (start us, length us, event | category | flops | bytes accessed | tf_op | source)
XLA Modules:
  0.0 176.1 jit_solution(10236019823867663924)
XLA Ops:
  0.6 4.0 %shard_map.122 = (f32[2,2,256,128]{3,2,1,0:T(8,128)}, f32[16,168,128]{2,1,0:T(8,128)}, s32[16]{0:T(128)}, s32[16]{0:T(128)}, s32[16]{0:T(128)}, /*index=5*/s32[16]{0:T(128)}, f32[2]{0:T(128)}) custom-call(s32[8,16]{1,0:T(8,128)} %owner_map.1, s32[128]{0:T(128)} %row_tops.1, s32[2]{0:T(128)} %restart.1, f32[101]{0:T(128)} %constant.12.clone.table, ...), custom_call_target="tpu_custom_call" | custom-call | tf_op jit(solution)/shard_map/pallas_call | solution.py:208
  4.6 28.3 %all_to_all.39.amp.got = f32[16,168,128]{2,1,0:T(8,128)} all-to-all(f32[16,168,128]{2,1,0:T(8,128)} %get-tuple-element.23), channel_id=1, replica_groups=mesh['ty'=8,'tx'=16] {'tx'}, dimensions={0} | all-to-all | bytes 2752512 | tf_op jit(solution)/shard_map/all_to_all | solution.py:290
  32.9 3.3 %shard_map.124 = f32[16,160,128]{2,1,0:T(8,128)} custom-call(s32[16]{0:T(128)} %get-tuple-element.28.right, s32[16]{0:T(128)} %get-tuple-element.29.inv, f32[16,168,128]{2,1,0:T(8,128)} %all_to_all.39.amp.got, f32[32,128,128]{2,1,0:T(8,128)} %bitcast.7), custom_call_target="tpu_custom_call" | custom-call | tf_op jit(solution)/shard_map/pallas_call | solution.py:208
  36.2 3.7 %all-to-all-start.1 = ((f32[16,160,128]{2,1,0:T(8,128)}), f32[16,160,128]{2,1,0:T(8,128)S(1)}, u32[]{:S(2)}, u32[]{:S(2)}) async-start(f32[16,160,128]{2,1,0:T(8,128)} %shard_map.124), calls=%async_computation.1 | async-start | bytes 2621440 | tf_op jit(solution)/shard_map/all_to_all | solution.py:290
  40.0 0.8 fusion
  40.8 0.7 slice_reduce_fusion
  41.5 16.0 %shard_map.123 = (f32[2,256,128]{2,1,0:T(8,128)}, f32[2,256,128]{2,1,0:T(8,128)}, f32[2,256,128]{2,1,0:T(8,128)}, f32[8,128]{1,0:T(8,128)}) custom-call(s32[16]{0:T(128)} %get-tuple-element.22.rows, s32[16]{0:T(128)} %get-tuple-element.43.offs, f32[2]{0:T(128)} %get-tuple-element.24.beta, f32[2,2,256,128]{3,2,1,0:T(8,128)} %get-tuple-element.25.z0, ...), custom_call_target="tpu_custom_call" | custom-call | flops 6400000000 | bytes 4194304 | tf_op jit(solution)/shard_map/pallas_call | solution.py:192
  57.5 0.3 all-to-all-done.1.halo.amp
  57.8 1.1 copy-done
  58.9 16.3 %shard_map.125 = (f32[2,256,128]{2,1,0:T(8,128)}, f32[16,64,128]{2,1,0:T(8,128)}, f32[8,128]{1,0:T(8,128)}) custom-call(s32[16]{0:T(128)} %get-tuple-element.22.rows, s32[16]{0:T(128)} %get-tuple-element.42.offs, f32[2]{0:T(128)} %get-tuple-element.24.beta, f32[2,2,256,128]{3,2,1,0:T(8,128)} %get-tuple-element.25.z0, f32[2,256,256]{2,1,0:T(8,128)} %obj.5, ...), custom_call_target="tpu_custom_call" | custom-call | flops 6400000000 | bytes 4194304 | tf_op jit(solution)/shard_map/pallas_call | solution.py:192
  75.2 15.7 %all_to_all.40.got = f32[16,64,128]{2,1,0:T(8,128)} all-to-all(f32[16,64,128]{2,1,0:T(8,128)} %get-tuple-element.32), channel_id=1, replica_groups=mesh['ty'=8,'tx'=16] {'tx'}, dimensions={0} | all-to-all | bytes 1048576 | tf_op jit(solution)/shard_map/all_to_all | solution.py:290
  90.9 1.9 %shard_map.126 = f32[16,64,128]{2,1,0:T(8,128)} custom-call(s32[16]{0:T(128)} %get-tuple-element.31.left, s32[16]{0:T(128)} %get-tuple-element.28.right, f32[2]{0:T(128)} %get-tuple-element.24.beta, f32[16,64,128]{2,1,0:T(8,128)} %all_to_all.40.got), custom_call_target="tpu_custom_call" | custom-call | tf_op jit(solution)/shard_map/pallas_call | solution.py:208
  92.8 13.2 %all_to_all.41.got = f32[16,64,128]{2,1,0:T(8,128)} all-to-all(f32[16,64,128]{2,1,0:T(8,128)} %shard_map.126), channel_id=1, replica_groups=mesh['ty'=8,'tx'=16] {'tx'}, dimensions={0} | all-to-all | bytes 1048576 | tf_op jit(solution)/shard_map/all_to_all | solution.py:290
  106.0 15.7 %shard_map.127 = (f32[2,256,128]{2,1,0:T(8,128)}, f32[2,256,128]{2,1,0:T(8,128)}, f32[8,128]{1,0:T(8,128)}) custom-call(s32[16]{0:T(128)} %get-tuple-element.22.rows, s32[16]{0:T(128)} %get-tuple-element.42.offs, f32[2,256,128]{2,1,0:T(8,128)} %get-tuple-element.30.mid, f32[16,64,128]{2,1,0:T(8,128)} %all_to_all.41.got, f32[2,2,128,128]{3,2,1,0:T(8,128)} %probe.7, ...), custom_call_target="tpu_custom_call" | custom-call | flops 6400000000 | bytes 4194304 | tf_op jit(solution)/shard_map/pallas_call | solution.py:192
  121.7 3.7 %all-to-all-start.4 = ((f32[16,32,128]{2,1,0:T(8,128)}), f32[16,32,128]{2,1,0:T(8,128)S(1)}, u32[]{:S(2)}, u32[]{:S(2)}) async-start(f32[16,32,128]{2,1,0:T(8,128)} %bitcast.8), calls=%async_computation.4 | async-start | bytes 524288 | tf_op jit(solution)/shard_map/all_to_all | solution.py:290
  125.4 16.0 %shard_map.128 = (f32[2,256,256]{2,1,0:T(8,128)}, f32[8,128]{1,0:T(8,128)}) custom-call(s32[16]{0:T(128)} %get-tuple-element.22.rows, s32[16]{0:T(128)} %get-tuple-element.43.offs, f32[2,256,128]{2,1,0:T(8,128)} %get-tuple-element.30.mid, f32[16,64,128]{2,1,0:T(8,128)} %all_to_all.41.got, f32[2,256,128]{2,1,0:T(8,128)} %get-tuple-element.33.odd_low, ...), custom_call_target="tpu_custom_call" | custom-call | flops 6400000000 | bytes 4194304 | tf_op jit(solution)/shard_map/pallas_call | solution.py:192
  141.4 0.7 copy-done.1
  142.1 1.7 shard_map.129
  143.8 14.4 %all_to_all.42.got = f32[16,40,128]{2,1,0:T(8,128)} all-to-all(f32[16,40,128]{2,1,0:T(8,128)} %shard_map.129), channel_id=1, replica_groups=mesh['ty'=8,'tx'=16] {'tx'}, dimensions={0} | all-to-all | bytes 655360 | tf_op jit(solution)/shard_map/all_to_all | solution.py:290
  158.2 2.0 %shard_map.130 = (f32[2,256,256]{2,1,0:T(8,128)}, f32[8,128]{1,0:T(8,128)}) custom-call(f32[2,256,256]{2,1,0:T(8,128)} %get-tuple-element.37.tile, f32[16,40,128]{2,1,0:T(8,128)} %all_to_all.42.got), custom_call_target="tpu_custom_call" | custom-call | tf_op jit(solution)/shard_map/pallas_call | solution.py:208
  160.2 15.2 %all_to_all.43 = f32[8,1,128]{2,1,0:T(1,128)S(1)} all-to-all(f32[8,1,128]{2,1,0:T(1,128)} %bitcast.10), channel_id=1, replica_groups=mesh['ty'=8,'tx'=16] {'ty'}, dimensions={0} | all-to-all | bytes 8192 | tf_op jit(solution)/shard_map/all_to_all | solution.py:290
  175.4 0.1 reshape.15
  175.5 0.1 reduce_sum.19
  175.6 0.5 broadcast_multiply_fusion
  (4 shorter events, 0.0 us)
Async XLA Ops:
  36.2 21.6 %all-to-all-start.1 = ((f32[16,160,128]{2,1,0:T(8,128)}), f32[16,160,128]{2,1,0:T(8,128)S(1)}, u32[]{:S(2)}, u32[]{:S(2)}) async-start(f32[16,160,128]{2,1,0:T(8,128)} %shard_map.124), calls=%async_computation.1 | async-start | bytes 2621440 | tf_op jit(solution)/shard_map/all_to_all | solution.py:290
  57.8 1.1 copy-start
  121.7 19.7 %all-to-all-start.4 = ((f32[16,32,128]{2,1,0:T(8,128)}), f32[16,32,128]{2,1,0:T(8,128)S(1)}, u32[]{:S(2)}, u32[]{:S(2)}) async-start(f32[16,32,128]{2,1,0:T(8,128)} %bitcast.8), calls=%async_computation.4 | async-start | bytes 524288 | tf_op jit(solution)/shard_map/all_to_all | solution.py:290
  141.4 0.7 copy-start.1

commit v3 on v2

v3 whole, which is shorter than its diff:
```python
import functools
import math

import jax
import jax.numpy as jnp
import ml_dtypes
import numpy as np
from jax import lax
from jax.experimental import pallas as pl
from jax.experimental.pallas import tpu as pltpu
from jax.sharding import PartitionSpec as P

START = 100
STABILIZER = 0.05
STEP = 0.25
N = 128
GROUP = 8
VMEM_BYTES = 60 * 2**20
f32 = jnp.float32
bf16 = jnp.bfloat16
SMEM = pl.BlockSpec(memory_space=pltpu.SMEM)
VMEM = pl.BlockSpec(memory_space=pltpu.VMEM)
ANY = pl.BlockSpec(memory_space=pl.ANY)


def momentum_table():
    values = [1.0]
    for counter in range(START):
        last = values[-1]
        values.append((1.0 + (1.0 + 4.0 * last * last) ** 0.5) / 2.0)
    return jnp.asarray(values, f32)


def dft_tables():
    index = np.arange(N)
    angle = (index[:, None] * index[None, :] % N).astype(np.float64) * (2.0 * math.pi / N)
    cos, sin = np.cos(angle) / math.sqrt(N), np.sin(angle) / math.sqrt(N)

    def stacked(table):
        high = table.astype(ml_dtypes.bfloat16)
        low = (table - high.astype(np.float64)).astype(ml_dtypes.bfloat16)
        return jnp.asarray(np.concatenate([high, high, low], 0))

    return stacked(np.block([[cos, -sin], [sin, cos]])), stacked(np.block([[cos, sin], [-sin, cos]]))


def times_table(block, table):
    parts = []
    for at in range(0, block.shape[0], N):
        part = block[at : at + N]
        high = part.astype(bf16)
        low = (part - high.astype(f32)).astype(bf16)
        parts.append(jnp.dot(jnp.concatenate([high, low, high], 1), table, preferred_element_type=f32))
    return jnp.concatenate(parts, 0)


def flip_blocks(block):
    rows = []
    for at in range(0, block.shape[0], N):
        rows.append(jnp.concatenate([block[at : at + N, :N].T, block[at : at + N, N:].T], 1))
    return jnp.concatenate(rows, 0)


def all_positions(rows, offs, z, probe, amp, fwd, bwd, left, right, loss):
    clear(left, right, loss)
    lane = lax.broadcasted_iota(jnp.int32, (N, N), 1)

    def group(g, carry):
        first = g * GROUP
        waves, places = [], []
        for u in range(GROUP):
            top, off = rows[first + u], offs[first + u]
            inside = lane >= off
            patch = [
                pltpu.roll(jnp.where(inside, z[0, k, pl.ds(top, N), :], z[1, k, pl.ds(top, N), :]), (N - off) & (N - 1), 1)
                for k in range(2)
            ]
            for m in range(2):
                re, im = probe[m, 0], probe[m, 1]
                waves.append(jnp.concatenate([re * patch[0] - im * patch[1], re * patch[1] + im * patch[0]], 1))
            places.append((top, off, inside))
        wave = times_table(flip_blocks(times_table(jnp.concatenate(waves, 0), fwd[...])), fwd[...])
        backs = []
        total = jnp.zeros((8, N), f32)
        for u in range(GROUP):
            w = wave[u * 2 * N : (u + 1) * 2 * N]
            square = w * w
            square = square[:N] + square[N:]
            square = square[:, :N] + square[:, N:] + STABILIZER
            inverse = lax.rsqrt(square)
            measured = amp[first + u].T
            miss = square * inverse - measured
            total = total + jnp.sum((miss * miss).reshape(N // 8, 8, N), 0)
            weight = 1.0 - measured * inverse
            weight = jnp.concatenate([weight, weight], 1)
            backs += [weight * w[:N], weight * w[N:]]
        loss[...] += total
        back = times_table(flip_blocks(times_table(jnp.concatenate(backs, 0), bwd[...])), bwd[...])
        for u, (top, off, inside) in enumerate(places):
            grad_re, grad_im = 0.0, 0.0
            for m in range(2):
                re, im = probe[m, 0], probe[m, 1]
                b = back[(2 * u + m) * N : (2 * u + m + 1) * N]
                grad_re = grad_re + re * b[:, :N] + im * b[:, N:]
                grad_im = grad_im + re * b[:, N:] - im * b[:, :N]
            for k, grad in ((0, grad_re), (1, grad_im)):
                moved = pltpu.roll(grad, off, 1)
                left[k, pl.ds(top, N), :] += jnp.where(inside, moved, 0.0)
                right[k, pl.ds(top, N), :] += jnp.where(inside, 0.0, moved)
        return carry

    lax.fori_loop(0, 16 // GROUP, group, 0)


def clear(*refs):
    for ref in refs:
        ref[...] = jnp.zeros_like(ref)


def unit(tile, k, u):
    return tile[k, :, u * N : (u + 1) * N]


def chunk_of(ref, d):
    return ref.at[d // 8, pl.ds(32 * (d % 8), 32)]


def even_first(rows, offs, beta, z0, obj, probe, amp, fwd, bwd, even_low, even_high, ahead, loss):
    all_positions(rows, offs, z0, probe, amp, fwd, bwd, even_low, even_high, loss)
    b = beta[1]
    for k in range(2):
        ahead[k] = (1.0 + b) * (z0[0, k] - STEP * even_low[k]) - b * unit(obj, k, 0)


def odd_first(rows, offs, z0, halo, probe, amp, fwd, bwd, odd_low, odd_high, loss, z):
    z[0] = z0[1]
    for d in range(16):
        chunk_of(z.at[1], d)[...] = halo[d]
    all_positions(rows, offs, z, probe, amp, fwd, bwd, odd_low, odd_high, loss)


def odd_second(
    rows, offs, beta, z0, obj, even_high, odd_low, odd_high, ahead, probe, amp, fwd, bwd,
    mid, low_second, high_second, loss, z,
):
    b = beta[1]
    scale = (1.0 + b) * STEP
    for k in range(2):
        now = z0[1, k] - STEP * (even_high[k] + odd_low[k])
        mid[k] = now + b * (now - unit(obj, k, 1))
        z[0, k] = mid[k]
    for d in range(16):
        chunk_of(z.at[1], d)[...] = ahead[d, :32] - scale * chunk_of(odd_high, d)[...]
    all_positions(rows, offs, z, probe, amp, fwd, bwd, low_second, high_second, loss)


def even_second(
    rows, offs, beta, ahead, from_left, mid, odd_low, loss_a, loss_b, loss_c, probe, amp, fwd, bwd,
    tile, sums, even_low, even_high, loss, z,
):
    scale = (1.0 + beta[1]) * STEP
    for d in range(16):
        chunk_of(z.at[0], d)[...] = chunk_of(ahead, d)[...] - scale * from_left[d]
    z[1] = mid[...]
    all_positions(rows, offs, z, probe, amp, fwd, bwd, even_low, even_high, loss)
    for k in range(2):
        tile[k, :, :N] = z[0, k] - STEP * even_low[k]
        tile[k, :, N:] = z[1, k] - STEP * (even_high[k] + odd_low[k])
    before = jnp.sum(loss_a[...] + loss_b[...], axis=0, keepdims=True)
    after = jnp.sum(loss_c[...] + loss[...], axis=0, keepdims=True)
    lane = lax.broadcasted_iota(jnp.int32, (1, N), 1)
    line = jnp.where(lane < N // 2, before + pltpu.roll(before, N // 2, 1), after + pltpu.roll(after, N // 2, 1))
    sums[...] = jnp.broadcast_to(line, sums.shape)


def run(kernel, steps, args, outs, scratch, flops):
    whole = lambda a: pl.BlockSpec(a.shape, lambda i, n=len(a.shape): (0,) * n)
    out_shape = [jax.ShapeDtypeStruct(s, d) for s, d, _ in outs]
    return pl.pallas_call(
        kernel,
        grid=(steps,),
        out_shape=out_shape,
        in_specs=[spec or whole(a) for a, spec in args],
        out_specs=[spec or whole(o) for o, (_, _, spec) in zip(out_shape, outs)],
        scratch_shapes=scratch,
        compiler_params=pltpu.CompilerParams(vmem_limit_bytes=VMEM_BYTES),
        cost_estimate=pl.CostEstimate(flops=flops, bytes_accessed=2**22, transcendentals=0),
    )(*[a for a, _ in args])


def small_call(kernel, args, outs, scratch=()):
    return pl.pallas_call(
        kernel,
        out_shape=[jax.ShapeDtypeStruct(s, d) for s, d, _ in outs],
        in_specs=[spec for _, spec in args],
        out_specs=[spec for _, _, spec in outs],
        scratch_shapes=list(scratch),
        compiler_params=pltpu.CompilerParams(vmem_limit_bytes=VMEM_BYTES),
    )(*[a for a, _ in args])


def start_all(pairs, sems):
    copies = [pltpu.make_async_copy(a, b, sems.at[i]) for i, (a, b) in enumerate(pairs)]
    for c in copies:
        c.start()
    return copies


def prepare(
    owner_map, row_tops, restart, table, cols, obj, prev, amp,
    z0, send, rows, inv, right, left, beta, sems,
):
    band = lax.axis_index("ty")
    for c in range(16):
        owner = owner_map[band, c]
        inv[owner] = c
        right[owner] = owner_map[band, (c + 1) % 16]
        left[owner] = owner_map[band, (c + 15) % 16]
        rows[c] = row_tops[band * 16 + c]
    copies = start_all([(amp.at[2 * inv[d]], send.at[d, pl.ds(0, N)]) for d in range(16)], sems)
    for k in range(2):
        beta[k] = (table[restart[k] - 1] - 1.0) / table[restart[k]]
    b = beta[0]
    for u in range(2):
        for k in range(2):
            now = unit(obj, k, u)
            z0[u, k] = now + b * (now - unit(prev, k, u))
    lane = lax.broadcasted_iota(jnp.int32, (8, N), 1)
    for d in range(16):
        col = inv[d]
        even = cols[0, 2 * col] - 2 * N * col
        odd = cols[0, 2 * col + 1] - 2 * N * col - N
        send[d, N : N + 32] = chunk_of(z0.at[0], d)[...]
        send[d, N + 32 :] = jnp.where(lane < N // 2, even, odd).astype(f32)
    for c in copies:
        c.wait()


def pass_halo(right, inv, got, amp, send, off_even, off_odd, places, sems, more_sems):
    copies = start_all([(got.at[:, pl.ds(N + 32, 8)], places)], more_sems.at[pl.ds(16, 1)])
    copies += start_all([(amp.at[2 * inv[d] + 1], send.at[d, pl.ds(0, N)]) for d in range(16)], sems)
    copies += start_all([(got.at[right[d], pl.ds(N, 32)], send.at[d, pl.ds(N, 32)]) for d in range(16)], more_sems)
    copies[0].wait()
    for r in range(16):
        off_even[r] = places[r, 0, 0].astype(jnp.int32)
        off_odd[r] = places[r, 0, N // 2].astype(jnp.int32)
    for c in copies[1:]:
        c.wait()


def pass_ahead(right, ahead, odd_high, send):
    for d in range(16):
        send[d, :32] = ahead[right[d]]
        send[d, 32:] = chunk_of(odd_high, d)[...]


def pass_left(left, got, send):
    for d in range(16):
        send[d] = got[left[d], 32:]


def pass_last(left, got, sums, send):
    for d in range(16):
        send[d, :32] = got[left[d]]
        send[d, 32:] = sums[...]


def finish(tile, got, out, sums):
    total = got[0, 32:]
    for d in range(1, 16):
        total = total + got[d, 32:]
    sums[...] = total
    for k in range(2):
        out[k, :, N:] = tile[k, :, N:]
    for d in range(16):
        at = pl.ds(32 * (d % 8), 32)
        out[d // 8, at, :N] = tile[d // 8, at, :N] - STEP * got[d, :32]


def swap(block, axis="tx"):
    return lax.all_to_all(block, axis, 0, 0, tiled=True)


def shards(obj, prev, probe, amplitude, row_tops, scan_cols, restart, owner_map):
    fwd, bwd = dft_tables()
    ints = ((16,), jnp.int32, SMEM)
    unit_out, loss_out = ((2, 256, N), f32, None), ((8, N), f32, None)
    z_vmem = pltpu.VMEM((2, 2, 256, N), f32)
    unit_vmem = pltpu.VMEM((2, 256, N), f32)
    images = pl.BlockSpec((16, N, N), lambda i: (0, 0, 0))
    edge = pl.BlockSpec((16, 32, N), lambda i: (0, N // 32, 0))
    plain = lambda *arrays: [(a, None) for a in arrays]
    small = lambda *arrays: [(a, SMEM) for a in arrays]
    flops = 16 * 400_000_000

    z0, send, rows, inv, right, left, beta = small_call(
        prepare,
        small(owner_map, row_tops, restart, momentum_table(), scan_cols) + [(obj, VMEM), (prev, VMEM), (amplitude[0], ANY)],
        [((2, 2, 256, N), f32, VMEM), ((16, N + 40, N), f32, VMEM), ints, ints, ints, ints, ((2,), f32, SMEM)],
        [pltpu.SemaphoreType.DMA((16,))],
    )
    amp_even = swap(send)
    send, off_even, off_odd = small_call(
        pass_halo,
        small(right, inv) + [(amp_even, ANY), (amplitude[0], ANY)],
        [((16, N + 32, N), f32, VMEM), ints, ints],
        [pltpu.SMEM((16, 8, N), f32), pltpu.SemaphoreType.DMA((16,)), pltpu.SemaphoreType.DMA((17,))],
    )
    amp_odd = swap(send)
    even_low, even_high, ahead, loss_a = run(
        even_first, 1, small(rows, off_even, beta) + plain(z0, obj, probe) + [(amp_even, images)] + plain(fwd, bwd),
        [unit_out, unit_out, unit_out, loss_out], [], flops,
    )
    got = swap(ahead.reshape(16, 32, N))
    odd_low, odd_high, loss_b = run(
        odd_first, 1,
        small(rows, off_odd) + plain(z0) + [(amp_odd, edge)] + plain(probe) + [(amp_odd, images)] + plain(fwd, bwd),
        [unit_out, unit_out, loss_out], [z_vmem], flops,
    )
    (send,) = small_call(
        pass_ahead, small(right) + [(got, VMEM), (odd_high, VMEM)], [((16, 64, N), f32, VMEM)]
    )
    got = swap(send)
    (send,) = small_call(pass_left, small(left) + [(got, VMEM)], [((16, 32, N), f32, VMEM)])
    from_left = swap(send)
    mid, odd_low_second, odd_high_second, loss_c = run(
        odd_second, 1,
        small(rows, off_odd, beta) + plain(z0, obj, even_high, odd_low, odd_high, got, probe)
        + [(amp_odd, images)] + plain(fwd, bwd),
        [unit_out, unit_out, unit_out, loss_out], [z_vmem], flops,
    )
    last = swap(odd_high_second.reshape(16, 32, N))
    tile, sums = run(
        even_second, 1,
        small(rows, off_even, beta) + plain(ahead, from_left, mid, odd_low_second, loss_a, loss_b, loss_c, probe)
        + [(amp_even, images)] + plain(fwd, bwd),
        [((2, 256, 256), f32, None), loss_out], [unit_vmem, unit_vmem, pltpu.VMEM((8, N), f32), z_vmem], flops,
    )
    (send,) = small_call(
        pass_last, small(left) + [(last, VMEM), (sums, VMEM)], [((16, 40, N), f32, VMEM)]
    )
    got = swap(send)
    tile, sums = small_call(
        finish, [(tile, VMEM), (got, VMEM)], [((2, 256, 256), f32, VMEM), ((8, N), f32, VMEM)]
    )
    sums = swap(sums, "ty")
    losses = jnp.sum(jnp.sum(sums, axis=0).reshape(2, N // 2), axis=1) * (0.5 / 67108864.0)
    return (tile, losses)


def solution(mesh):
    in_specs = (
        P(None, "ty", "tx"),
        P(None, "ty", "tx"),
        P(),
        P(("ty", "tx"), None, None, None),
        P(),
        P(("ty", "tx"), None),
        P(),
        P(),
    )
    return jax.shard_map(
        shards, mesh=mesh, in_specs=in_specs, out_specs=(P(None, "ty", "tx"), P()), check_vma=False
    )
```

time: 177 us -> 162 us (0.915)
  Pallas kernels: 76.7 us -> 58.4 us
  blocking collectives: 86.8 us -> 74.1 us
  starting transfers between devices: 7.43 us -> 18.5 us
  waiting for transfers between devices: 0.33 us -> 7.2 us
    pallas_call x4, Pallas kernels: 63.9 us -> 43.1 us  [run(): pl.pallas_call(kernel, grid=(steps,), out_shape=out_shape, in_specs=[spec...]
    all_to_all x5 -> x4, blocking collectives: 86.8 us -> 74.1 us  [swap(): return lax.all_to_all(block, axis, 0, 0, tiled=True)]
    all_to_all x2 -> x4, starting transfers between devices: 7.43 us -> 18.5 us  [swap(): return lax.all_to_all(block, axis, 0, 0, tiled=True)]
    all_to_all x2 -> x4, waiting for transfers between devices: 0.33 us -> 7.2 us  [swap(): return lax.all_to_all(block, axis, 0, 0, tiled=True)]
    pallas_call x5 -> x6, Pallas kernels: 12.8 us -> 15.3 us  [small_call(): pl.pallas_call(kernel, out_shape=[jax.ShapeDtypeStruct(s, d) for s, d, _...]
  transfers between devices with their start and end apart: 2 -> 4, of which waited for: 1 -> 1; matrix products, arithmetic and copies ran while one was open for 1% -> 0% of each run, Pallas kernels for 18% -> 27%
where the time goes in v3:
time: 162 us; the launch traced here: 161 us
  blocking collectives  74.1 us (46%)
  Pallas kernels  58.4 us (36%)
  starting transfers between devices  18.5 us (11%)
  waiting for transfers between devices  7.2 us (4%)
    all_to_all x4, blocking collectives, swap(): return lax.all_to_all(block, axis, 0, 0, tiled=True)  74.1 us
    pallas_call x4, Pallas kernels, run(): pl.pallas_call(kernel, grid=(steps,), out_shape=out_shape, in_specs=[spec...  43.1 us
    all_to_all x4, starting transfers between devices, swap(): return lax.all_to_all(block, axis, 0, 0, tiled=True)  18.5 us
    pallas_call x6, Pallas kernels, small_call(): pl.pallas_call(kernel, out_shape=[jax.ShapeDtypeStruct(s, d) for s, d, _...  15.3 us
    all_to_all x4, waiting for transfers between devices, swap(): return lax.all_to_all(block, axis, 0, 0, tiled=True)  7.2 us
  transfers between devices with their start and end apart: 4, of which 1 were waited for; matrix products, arithmetic and copies ran while one was open for 0% of the time, Pallas kernels for 27%

profile of v3, /device:TPU:1, one launch (start us, length us, event | category | flops | bytes accessed | tf_op | source)
XLA Modules:
  0.0 161.1 jit_solution(5617386285323874012)
XLA Ops:
  0.6 4.0 %shard_map.122 = (f32[2,2,256,128]{3,2,1,0:T(8,128)}, f32[16,168,128]{2,1,0:T(8,128)}, s32[16]{0:T(128)}, s32[16]{0:T(128)}, s32[16]{0:T(128)}, /*index=5*/s32[16]{0:T(128)}, f32[2]{0:T(128)}) custom-call(s32[8,16]{1,0:T(8,128)} %owner_map.1, s32[128]{0:T(128)} %row_tops.1, s32[2]{0:T(128)} %restart.1, f32[101]{0:T(128)} %constant.12.clone.table, ...), custom_call_target="tpu_custom_call" | custom-call | tf_op jit(solution)/shard_map/pallas_call | solution.py:192
  4.6 28.3 %all_to_all.44.got.amp = f32[16,168,128]{2,1,0:T(8,128)} all-to-all(f32[16,168,128]{2,1,0:T(8,128)} %get-tuple-element.29), channel_id=1, replica_groups=mesh['ty'=8,'tx'=16] {'tx'}, dimensions={0} | all-to-all | bytes 2752512 | tf_op jit(solution)/shard_map/all_to_all | solution.py:281
  32.9 4.1 %shard_map.123 = (f32[16,160,128]{2,1,0:T(8,128)}, s32[16]{0:T(128)}, s32[16]{0:T(128)}) custom-call(s32[16]{0:T(128)} %get-tuple-element.27.right, s32[16]{0:T(128)} %get-tuple-element.28.inv, f32[16,168,128]{2,1,0:T(8,128)} %all_to_all.44.got.amp, f32[32,128,128]{2,1,0:T(8,128)} %bitcast.7), custom_call_target="tpu_custom_call" | custom-call | tf_op jit(solution)/shard_map/pallas_call | solution.py:192
  37.0 3.7 %all-to-all-start.2 = ((f32[16,160,128]{2,1,0:T(8,128)}), f32[16,160,128]{2,1,0:T(8,128)S(1)}, u32[]{:S(2)}, u32[]{:S(2)}) async-start(f32[16,160,128]{2,1,0:T(8,128)} %get-tuple-element.36), calls=%async_computation.2 | async-start | bytes 2621440 | tf_op jit(solution)/shard_map/all_to_all | solution.py:281
  40.7 10.7 %shard_map.124 = (f32[2,256,128]{2,1,0:T(8,128)}, f32[2,256,128]{2,1,0:T(8,128)}, f32[2,256,128]{2,1,0:T(8,128)}, f32[8,128]{1,0:T(8,128)}) custom-call(s32[16]{0:T(128)} %get-tuple-element.26.rows, s32[16]{0:T(128)} %get-tuple-element.30.offs, f32[2]{0:T(128)} %get-tuple-element.31.beta, f32[2,2,256,128]{3,2,1,0:T(8,128)} %get-tuple-element.32.z0, ...), custom_call_target="tpu_custom_call" | custom-call | flops 6400000000 | bytes 4194304 | tf_op jit(solution)/shard_map/pallas_call | solution.py:179
  51.4 7.2 %all-to-all-done.2.halo.amp = f32[16,160,128]{2,1,0:T(8,128)S(1)} async-done(((f32[16,160,128]{2,1,0:T(8,128)}), f32[16,160,128]{2,1,0:T(8,128)S(1)}, u32[]{:S(2)}, u32[]{:S(2)}) %all-to-all-start.2) | async-done | bytes 1310752 | tf_op jit(solution)/shard_map/all_to_all | solution.py:281
  58.6 4.7 %all-to-all-start.1 = ((f32[16,32,128]{2,1,0:T(8,128)}), f32[16,32,128]{2,1,0:T(8,128)S(1)}, u32[]{:S(2)}, u32[]{:S(2)}) async-start(f32[16,32,128]{2,1,0:T(8,128)} %bitcast.8), calls=%async_computation.1 | async-start | bytes 524288 | tf_op jit(solution)/shard_map/all_to_all | solution.py:281
  63.3 10.6 %shard_map.125 = (f32[2,256,128]{2,1,0:T(8,128)}, f32[2,256,128]{2,1,0:T(8,128)}, f32[8,128]{1,0:T(8,128)}) custom-call(s32[16]{0:T(128)} %get-tuple-element.26.rows, s32[16]{0:T(128)} %get-tuple-element.35.offs, f32[2,2,256,128]{3,2,1,0:T(8,128)} %get-tuple-element.32.z0, f32[16,160,128]{2,1,0:T(8,128)} %copy-done, f32[2,2,128,128]{3,2,1,0:T(8,128)} %probe.7, ...), custom_call_target="tpu_custom_call" | custom-call | flops 6400000000 | bytes 4194304 | tf_op jit(solution)/shard_map/pallas_call | solution.py:179
  73.9 0.7 copy-done.2
  74.6 1.9 %shard_map.126 = f32[16,64,128]{2,1,0:T(8,128)} custom-call(s32[16]{0:T(128)} %get-tuple-element.27.right, f32[16,32,128]{2,1,0:T(8,128)} %copy-done.2, f32[2,256,128]{2,1,0:T(8,128)} %get-tuple-element.37.odd_high), custom_call_target="tpu_custom_call" | custom-call | tf_op jit(solution)/shard_map/pallas_call | solution.py:192
  76.5 15.7 %all_to_all.45.got.ahead = f32[16,64,128]{2,1,0:T(8,128)} all-to-all(f32[16,64,128]{2,1,0:T(8,128)} %shard_map.126), channel_id=1, replica_groups=mesh['ty'=8,'tx'=16] {'tx'}, dimensions={0} | all-to-all | bytes 1048576 | tf_op jit(solution)/shard_map/all_to_all | solution.py:281
  92.2 1.8 %shard_map.127 = f32[16,32,128]{2,1,0:T(8,128)} custom-call(s32[16]{0:T(128)} %get-tuple-element.34.left, f32[16,64,128]{2,1,0:T(8,128)} %all_to_all.45.got.ahead), custom_call_target="tpu_custom_call" | custom-call | tf_op jit(solution)/shard_map/pallas_call | solution.py:192
  94.0 3.7 %all-to-all-start.4 = ((f32[16,32,128]{2,1,0:T(8,128)}), f32[16,32,128]{2,1,0:T(8,128)S(1)}, u32[]{:S(2)}, u32[]{:S(2)}) async-start(f32[16,32,128]{2,1,0:T(8,128)} %shard_map.127), calls=%async_computation.4 | async-start | bytes 524288 | tf_op jit(solution)/shard_map/all_to_all | solution.py:281
  97.7 11.1 %shard_map.128 = (f32[2,256,128]{2,1,0:T(8,128)}, f32[2,256,128]{2,1,0:T(8,128)}, f32[2,256,128]{2,1,0:T(8,128)}, f32[8,128]{1,0:T(8,128)}) custom-call(s32[16]{0:T(128)} %get-tuple-element.26.rows, s32[16]{0:T(128)} %get-tuple-element.35.offs, f32[2]{0:T(128)} %get-tuple-element.31.beta, f32[2,2,256,128]{3,2,1,0:T(8,128)} %get-tuple-element.32.z0, ...), custom_call_target="tpu_custom_call" | custom-call | flops 6400000000 | bytes 4194304 | tf_op jit(solution)/shard_map/pallas_call | solution.py:179
  108.8 6.4 %all-to-all-start.5 = ((f32[16,32,128]{2,1,0:T(8,128)}), f32[16,32,128]{2,1,0:T(8,128)S(1)}, u32[]{:S(2)}, u32[]{:S(2)}) async-start(f32[16,32,128]{2,1,0:T(8,128)} %bitcast.9), calls=%async_computation.5 | async-start | bytes 524288 | tf_op jit(solution)/shard_map/all_to_all | solution.py:281
  115.2 10.7 %shard_map.129 = (f32[2,256,256]{2,1,0:T(8,128)}, f32[8,128]{1,0:T(8,128)}) custom-call(s32[16]{0:T(128)} %get-tuple-element.26.rows, s32[16]{0:T(128)} %get-tuple-element.30.offs, f32[2]{0:T(128)} %get-tuple-element.31.beta, f32[2,256,128]{2,1,0:T(8,128)} %get-tuple-element.33.ahead, f32[16,32,128]{2,1,0:T(8,128)} %copy-done.3, ...), custom_call_target="tpu_custom_call" | custom-call | flops 6400000000 | bytes 4194304 | tf_op jit(solution)/shard_map/pallas_call | solution.py:179
  126.0 0.7 copy-done.1
  126.6 1.7 %shard_map.130 = f32[16,40,128]{2,1,0:T(8,128)} custom-call(s32[16]{0:T(128)} %get-tuple-element.34.left, f32[16,32,128]{2,1,0:T(8,128)} %copy-done.1, f32[8,128]{1,0:T(8,128)} %get-tuple-element.47.sums), custom_call_target="tpu_custom_call" | custom-call | tf_op jit(solution)/shard_map/pallas_call | solution.py:192
  128.4 14.7 %all_to_all.46.got = f32[16,40,128]{2,1,0:T(8,128)} all-to-all(f32[16,40,128]{2,1,0:T(8,128)} %shard_map.130), channel_id=1, replica_groups=mesh['ty'=8,'tx'=16] {'tx'}, dimensions={0} | all-to-all | bytes 655360 | tf_op jit(solution)/shard_map/all_to_all | solution.py:281
  143.0 2.0 %shard_map.131 = (f32[2,256,256]{2,1,0:T(8,128)}, f32[8,128]{1,0:T(8,128)}) custom-call(f32[2,256,256]{2,1,0:T(8,128)} %get-tuple-element.45.tile, f32[16,40,128]{2,1,0:T(8,128)} %all_to_all.46.got), custom_call_target="tpu_custom_call" | custom-call | tf_op jit(solution)/shard_map/pallas_call | solution.py:192
  145.0 15.3 %all_to_all.47 = f32[8,1,128]{2,1,0:T(1,128)S(1)} all-to-all(f32[8,1,128]{2,1,0:T(1,128)} %bitcast.10), channel_id=1, replica_groups=mesh['ty'=8,'tx'=16] {'ty'}, dimensions={0} | all-to-all | bytes 8192 | tf_op jit(solution)/shard_map/all_to_all | solution.py:281
  160.4 0.1 reshape.17
  160.4 0.1 reduce_sum.19
  160.6 0.5 broadcast_multiply_fusion
  (10 shorter events, 0.0 us)
Async XLA Ops:
  37.0 21.6 %all-to-all-start.2 = ((f32[16,160,128]{2,1,0:T(8,128)}), f32[16,160,128]{2,1,0:T(8,128)S(1)}, u32[]{:S(2)}, u32[]{:S(2)}) async-start(f32[16,160,128]{2,1,0:T(8,128)} %get-tuple-element.36), calls=%async_computation.2 | async-start | bytes 2621440 | tf_op jit(solution)/shard_map/all_to_all | solution.py:281
  58.6 4.7 %copy-start = (f32[16,160,128]{2,1,0:T(8,128)}, f32[16,160,128]{2,1,0:T(8,128)S(1)}, u32[]{:S(2)}) copy-start(f32[16,160,128]{2,1,0:T(8,128)S(1)} %all-to-all-done.2.halo.amp) | copy-start | bytes 3932164
  58.6 15.3 %all-to-all-start.1 = ((f32[16,32,128]{2,1,0:T(8,128)}), f32[16,32,128]{2,1,0:T(8,128)S(1)}, u32[]{:S(2)}, u32[]{:S(2)}) async-start(f32[16,32,128]{2,1,0:T(8,128)} %bitcast.8), calls=%async_computation.1 | async-start | bytes 524288 | tf_op jit(solution)/shard_map/all_to_all | solution.py:281
  73.9 0.7 copy-start.2
  94.0 14.8 %all-to-all-start.4 = ((f32[16,32,128]{2,1,0:T(8,128)}), f32[16,32,128]{2,1,0:T(8,128)S(1)}, u32[]{:S(2)}, u32[]{:S(2)}) async-start(f32[16,32,128]{2,1,0:T(8,128)} %shard_map.127), calls=%async_computation.4 | async-start | bytes 524288 | tf_op jit(solution)/shard_map/all_to_all | solution.py:281
  108.8 6.4 %copy-start.3 = (f32[16,32,128]{2,1,0:T(8,128)}, f32[16,32,128]{2,1,0:T(8,128)S(1)}, u32[]{:S(2)}) copy-start(f32[16,32,128]{2,1,0:T(8,128)S(1)} %all-to-all-done.4.from_left) | copy-start | bytes 786436
  108.8 17.1 %all-to-all-start.5 = ((f32[16,32,128]{2,1,0:T(8,128)}), f32[16,32,128]{2,1,0:T(8,128)S(1)}, u32[]{:S(2)}, u32[]{:S(2)}) async-start(f32[16,32,128]{2,1,0:T(8,128)} %bitcast.9), calls=%async_computation.5 | async-start | bytes 524288 | tf_op jit(solution)/shard_map/all_to_all | solution.py:281
  126.0 0.7 copy-start.1

commit v4 on v3

v4 whole, which is shorter than its diff:
```python
import functools
import math

import jax
import jax.numpy as jnp
import ml_dtypes
import numpy as np
from jax import lax
from jax.experimental import pallas as pl
from jax.experimental.pallas import tpu as pltpu
from jax.sharding import PartitionSpec as P

START = 100
STABILIZER = 0.05
STEP = 0.25
N = 128
GROUP = 8
VMEM_BYTES = 60 * 2**20
f32 = jnp.float32
bf16 = jnp.bfloat16
SMEM = pl.BlockSpec(memory_space=pltpu.SMEM)
VMEM = pl.BlockSpec(memory_space=pltpu.VMEM)
ANY = pl.BlockSpec(memory_space=pl.ANY)


def momentum_table():
    values = [1.0]
    for counter in range(START):
        last = values[-1]
        values.append((1.0 + (1.0 + 4.0 * last * last) ** 0.5) / 2.0)
    return jnp.asarray(values, f32)


def dft_tables():
    index = np.arange(N)
    angle = (index[:, None] * index[None, :] % N).astype(np.float64) * (2.0 * math.pi / N)
    cos, sin = np.cos(angle) / math.sqrt(N), np.sin(angle) / math.sqrt(N)

    def stacked(table):
        high = table.astype(ml_dtypes.bfloat16)
        low = (table - high.astype(np.float64)).astype(ml_dtypes.bfloat16)
        return jnp.asarray(np.concatenate([high, high, low], 0))

    return stacked(np.block([[cos, -sin], [sin, cos]])), stacked(np.block([[cos, sin], [-sin, cos]]))


def times_table(block, table):
    parts = []
    for at in range(0, GROUP * 2 * N, N):
        if isinstance(block, tuple):
            high, low = block[0][at : at + N], block[1][at : at + N]
        else:
            part = block[at : at + N]
            high = part.astype(bf16)
            low = (part - high.astype(f32)).astype(bf16)
        parts.append(jnp.dot(jnp.concatenate([high, low, high], 1), table, preferred_element_type=f32))
    return jnp.concatenate(parts, 0)


def flip_blocks(block):
    rows = []
    for at in range(0, block.shape[0], N):
        rows.append(jnp.concatenate([block[at : at + N, :N].T, block[at : at + N, N:].T], 1))
    return jnp.concatenate(rows, 0)


def way_out(rows, offs, z, probe, amp, amp_first, fwd, loss, first):
    lane = lax.broadcasted_iota(jnp.int32, (N, N), 1)
    waves = []
    for u in range(GROUP):
        top, off = rows[first + u], offs[first + u]
        inside = lane >= off
        patch = [
            pltpu.roll(jnp.where(inside, z[0, k, pl.ds(top, N), :], z[1, k, pl.ds(top, N), :]), (N - off) & (N - 1), 1)
            for k in range(2)
        ]
        for m in range(2):
            re, im = probe[m, 0], probe[m, 1]
            waves.append(jnp.concatenate([re * patch[0] - im * patch[1], re * patch[1] + im * patch[0]], 1))
    wave = times_table(flip_blocks(times_table(jnp.concatenate(waves, 0), fwd[...])), fwd[...])
    weighted = []
    total = jnp.zeros((8, N), f32)
    for u in range(GROUP):
        w = wave[u * 2 * N : (u + 1) * 2 * N]
        square = w * w
        square = square[:N] + square[N:]
        square = square[:, :N] + square[:, N:] + STABILIZER
        inverse = lax.rsqrt(square)
        measured = amp[amp_first + u].T
        miss = square * inverse - measured
        total = total + jnp.sum((miss * miss).reshape(N // 8, 8, N), 0)
        weight = 1.0 - measured * inverse
        weight = jnp.concatenate([weight, weight], 1)
        weighted += [weight * w[:N], weight * w[N:]]
    loss[...] += total
    return jnp.concatenate(weighted, 0)


def way_back(rows, offs, probe, weighted, bwd, left, right, first):
    lane = lax.broadcasted_iota(jnp.int32, (N, N), 1)
    back = times_table(flip_blocks(times_table(weighted, bwd[...])), bwd[...])
    for u in range(GROUP):
        top, off = rows[first + u], offs[first + u]
        inside = lane >= off
        grad_re, grad_im = 0.0, 0.0
        for m in range(2):
            re, im = probe[m, 0], probe[m, 1]
            b = back[(2 * u + m) * N : (2 * u + m + 1) * N]
            grad_re = grad_re + re * b[:, :N] + im * b[:, N:]
            grad_im = grad_im + re * b[:, N:] - im * b[:, :N]
        for k, grad in ((0, grad_re), (1, grad_im)):
            moved = pltpu.roll(grad, off, 1)
            left[k, pl.ds(top, N), :] += jnp.where(inside, moved, 0.0)
            right[k, pl.ds(top, N), :] += jnp.where(inside, 0.0, moved)


def all_positions(rows, offs, z, probe, amp, fwd, bwd, left, right, loss):
    clear(left, right, loss)

    def group(g, carry):
        first = g * GROUP
        weighted = way_out(rows, offs, z, probe, amp, first, fwd, loss, first)
        way_back(rows, offs, probe, weighted, bwd, left, right, first)
        return carry

    lax.fori_loop(0, 16 // GROUP, group, 0)


def clear(*refs):
    for ref in refs:
        ref[...] = jnp.zeros_like(ref)


def unit(tile, k, u):
    return tile[k, :, u * N : (u + 1) * N]


def chunk_of(ref, d):
    return ref.at[d // 8, pl.ds(32 * (d % 8), 32)]


def even_first(rows, offs, beta, obj, prev, probe, amp, fwd, bwd, z0, even_low, even_high, ahead, loss):
    for u in range(2):
        for k in range(2):
            now = unit(obj, k, u)
            z0[u, k] = now + beta[0] * (now - unit(prev, k, u))
    all_positions(rows, offs, z0, probe, amp, fwd, bwd, even_low, even_high, loss)
    b = beta[1]
    for k in range(2):
        ahead[k] = (1.0 + b) * (z0[0, k] - STEP * even_low[k]) - b * unit(obj, k, 0)


def odd_first(rows, offs, z0, halo, probe, amp, fwd, bwd, odd_low, odd_high, loss, z):
    z[0] = z0[1]
    for d in range(16):
        chunk_of(z.at[1], d)[...] = halo[d]
    all_positions(rows, offs, z, probe, amp, fwd, bwd, odd_low, odd_high, loss)


def odd_second(
    rows, offs, beta, z0, obj, even_high, odd_low, odd_high, ahead, probe, amp, fwd, bwd,
    mid, low_second, high_second, loss, z,
):
    b = beta[1]
    scale = (1.0 + b) * STEP
    for k in range(2):
        now = z0[1, k] - STEP * (even_high[k] + odd_low[k])
        mid[k] = now + b * (now - unit(obj, k, 1))
        z[0, k] = mid[k]
    for d in range(16):
        chunk_of(z.at[1], d)[...] = ahead[d, :32] - scale * chunk_of(odd_high, d)[...]
    all_positions(rows, offs, z, probe, amp, fwd, bwd, low_second, high_second, loss)


def even_out(rows, offs, beta, ahead, from_left, mid, loss_a, loss_b, loss_c, probe, amp, fwd, start, sums, high, low, loss, z):
    @pl.when(pl.program_id(0) == 0)
    def _():
        clear(loss)
        scale = (1.0 + beta[1]) * STEP
        for d in range(16):
            chunk_of(z.at[0], d)[...] = chunk_of(ahead, d)[...] - scale * from_left[d]
        z[1] = mid[...]
        start[...] = z[0]

    weighted = way_out(rows, offs, z, probe, amp, 0, fwd, loss, pl.program_id(0) * GROUP)
    high[...] = weighted.astype(bf16)
    low[...] = (weighted - high[...].astype(f32)).astype(bf16)

    @pl.when(pl.program_id(0) == pl.num_programs(0) - 1)
    def _():
        before = jnp.sum(loss_a[...] + loss_b[...], axis=0, keepdims=True)
        after = jnp.sum(loss_c[...] + loss[...], axis=0, keepdims=True)
        lane = lax.broadcasted_iota(jnp.int32, (1, N), 1)
        line = jnp.where(lane < N // 2, before + pltpu.roll(before, N // 2, 1), after + pltpu.roll(after, N // 2, 1))
        sums[...] = jnp.broadcast_to(line, sums.shape)


def even_back(rows, offs, start, mid, odd_low, probe, high, low, bwd, tile, done, even_low, even_high):
    @pl.when(pl.program_id(0) == 0)
    def _():
        clear(even_low, even_high, done)

    way_back(rows, offs, probe, (high, low), bwd, even_low, even_high, pl.program_id(0) * GROUP)

    @pl.when(pl.program_id(0) == pl.num_programs(0) - 1)
    def _():
        for k in range(2):
            tile[k, :, :N] = start[k] - STEP * even_low[k]
            tile[k, :, N:] = mid[k] - STEP * (even_high[k] + odd_low[k])


def run(kernel, steps, args, outs, scratch, flops, limit=VMEM_BYTES):
    whole = lambda a: pl.BlockSpec(a.shape, lambda i, n=len(a.shape): (0,) * n)
    out_shape = [jax.ShapeDtypeStruct(s, d) for s, d, _ in outs]
    return pl.pallas_call(
        kernel,
        grid=(steps,),
        out_shape=out_shape,
        in_specs=[spec or whole(a) for a, spec in args],
        out_specs=[spec or whole(o) for o, (_, _, spec) in zip(out_shape, outs)],
        scratch_shapes=scratch,
        compiler_params=pltpu.CompilerParams(vmem_limit_bytes=limit),
        cost_estimate=pl.CostEstimate(flops=flops, bytes_accessed=2**22, transcendentals=0),
    )(*[a for a, _ in args])


def small_call(kernel, args, outs, scratch=(), limit=6 * 2**20):
    return pl.pallas_call(
        kernel,
        out_shape=[jax.ShapeDtypeStruct(s, d) for s, d, _ in outs],
        in_specs=[spec for _, spec in args],
        out_specs=[spec for _, _, spec in outs],
        scratch_shapes=list(scratch),
        compiler_params=pltpu.CompilerParams(vmem_limit_bytes=limit),
    )(*[a for a, _ in args])


def start_all(pairs, sems):
    copies = [pltpu.make_async_copy(a, b, sems.at[i]) for i, (a, b) in enumerate(pairs)]
    for c in copies:
        c.start()
    return copies


def prepare(
    owner_map, row_tops, restart, table, cols, obj, prev, amp, send, rows, inv, right, left, beta, now, before, sems
):
    edges = start_all([(obj.at[:, :, pl.ds(0, N)], now), (prev.at[:, :, pl.ds(0, N)], before)], sems.at[pl.ds(16, 2)])
    band = lax.axis_index("ty")
    for c in range(16):
        owner = owner_map[band, c]
        inv[owner] = c
        right[owner] = owner_map[band, (c + 1) % 16]
        left[owner] = owner_map[band, (c + 15) % 16]
        rows[c] = row_tops[band * 16 + c]
    copies = start_all([(amp.at[2 * inv[d]], send.at[d, pl.ds(0, N)]) for d in range(16)], sems)
    for k in range(2):
        beta[k] = (table[restart[k] - 1] - 1.0) / table[restart[k]]
    for c in edges:
        c.wait()
    now[...] = now[...] + beta[0] * (now[...] - before[...])
    lane = lax.broadcasted_iota(jnp.int32, (8, N), 1)
    for d in range(16):
        col = inv[d]
        even = cols[0, 2 * col] - 2 * N * col
        odd = cols[0, 2 * col + 1] - 2 * N * col - N
        send[d, N : N + 32] = chunk_of(now, d)[...]
        send[d, N + 32 :] = jnp.where(lane < N // 2, even, odd).astype(f32)
    for c in copies:
        c.wait()


def pass_halo(right, inv, got, amp, send, off_even, off_odd, places, sems):
    fetch_places = pltpu.make_async_copy(got.at[:, pl.ds(N + 32, 1)], places, sems.at[32])
    fetch_places.start()
    copies = start_all(
        [(amp.at[2 * inv[d] + 1], send.at[d, pl.ds(0, N)]) for d in range(16)]
        + [(got.at[right[d], pl.ds(N, 32)], send.at[d, pl.ds(N, 32)]) for d in range(16)],
        sems,
    )
    fetch_places.wait()
    for r in range(16):
        off_even[r] = places[r, 0, 0].astype(jnp.int32)
        off_odd[r] = places[r, 0, N // 2].astype(jnp.int32)
    for c in copies:
        c.wait()


def pass_ahead(right, ahead, odd_high, send):
    for d in range(16):
        send[d, :32] = ahead[right[d]]
        send[d, 32:] = chunk_of(odd_high, d)[...]


def pass_left(left, got, send):
    for d in range(16):
        send[d] = got[left[d], 32:]


def pass_last(left, got, sums, send):
    for d in range(16):
        send[d, :32] = got[left[d]]
        send[d, 32:] = sums[...]


def finish(tile, got, out):
    for d in range(16):
        at = pl.ds(32 * (d % 8), 32)
        out[d // 8, at] = tile[d // 8, at] - STEP * got[d]


def swap(block, axis="tx"):
    return lax.all_to_all(block, axis, 0, 0, tiled=True)


def shards(obj, prev, probe, amplitude, row_tops, scan_cols, restart, owner_map):
    fwd, bwd = dft_tables()
    ints = ((16,), jnp.int32, SMEM)
    unit_out, loss_out = ((2, 256, N), f32, None), ((8, N), f32, None)
    z_vmem = pltpu.VMEM((2, 2, 256, N), f32)
    unit_vmem = pltpu.VMEM((2, 256, N), f32)
    images = pl.BlockSpec((16, N, N), lambda i: (0, 0, 0))
    edge = pl.BlockSpec((16, 32, N), lambda i: (0, N // 32, 0))
    plain = lambda *arrays: [(a, None) for a in arrays]
    small = lambda *arrays: [(a, SMEM) for a in arrays]
    flops = 16 * 400_000_000

    amplitude = amplitude[0]
    send, rows, inv, right, left, beta = small_call(
        prepare,
        small(owner_map, row_tops, restart, momentum_table(), scan_cols)
        + [(obj, ANY), (prev, ANY), (amplitude, ANY)],
        [((16, N + 40, N), f32, VMEM), ints, ints, ints, ints, ((2,), f32, SMEM)],
        [unit_vmem, unit_vmem, pltpu.SemaphoreType.DMA((18,))], limit=VMEM_BYTES,
    )
    amp_even = swap(send)
    send, off_even, off_odd = small_call(
        pass_halo, small(right, inv) + [(amp_even, ANY), (amplitude, ANY)],
        [((16, N + 32, N), f32, VMEM), ints, ints],
        [pltpu.SMEM((16, 1, N), f32), pltpu.SemaphoreType.DMA((33,))], limit=VMEM_BYTES,
    )
    amp_odd = swap(send)
    z0, even_low, even_high, ahead, loss_a = run(
        even_first, 1, small(rows, off_even, beta) + plain(obj, prev, probe) + [(amp_even, images)] + plain(fwd, bwd),
        [((2, 2, 256, N), f32, None), unit_out, unit_out, unit_out, loss_out], [], flops,
    )
    got = swap(ahead.reshape(16, 32, N))
    odd_low, odd_high, loss_b = run(
        odd_first, 1,
        small(rows, off_odd) + plain(z0) + [(amp_odd, edge)] + plain(probe) + [(amp_odd, images)] + plain(fwd, bwd),
        [unit_out, unit_out, loss_out], [z_vmem], flops,
    )
    (send,) = small_call(
        pass_ahead, small(right) + [(got, VMEM), (odd_high, VMEM)], [((16, 64, N), f32, VMEM)]
    )
    got = swap(send)
    (send,) = small_call(pass_left, small(left) + [(got, VMEM)], [((16, 32, N), f32, VMEM)])
    from_left = swap(send)
    mid, odd_low_second, odd_high_second, loss_c = run(
        odd_second, 1,
        small(rows, off_odd, beta) + plain(z0, obj, even_high, odd_low, odd_high, got, probe)
        + [(amp_odd, images)] + plain(fwd, bwd),
        [unit_out, unit_out, unit_out, loss_out], [z_vmem], flops,
    )
    last = swap(odd_high_second.reshape(16, 32, N))
    half_block = pl.BlockSpec((GROUP * 2 * N, 2 * N), lambda i: (i, 0))
    half_out = ((16 * 2 * N, 2 * N), bf16, half_block)
    start, sums, high, low = run(
        even_out, 16 // GROUP,
        small(rows, off_even, beta) + plain(ahead, from_left, mid, loss_a, loss_b, loss_c, probe)
        + [(amp_even, pl.BlockSpec((GROUP, N, N), lambda i: (i, 0, 0)))] + plain(fwd),
        [unit_out, loss_out, half_out, half_out], [pltpu.VMEM((8, N), f32), z_vmem], flops // 2,
    )
    (send,) = small_call(
        pass_last, small(left) + [(last, VMEM), (sums, VMEM)], [((16, 40, N), f32, VMEM)]
    )
    got = swap(send)
    tile, done = run(
        even_back, 16 // GROUP,
        small(rows, off_even) + plain(start, mid, odd_low_second, probe)
        + [(high, half_block), (low, half_block)] + plain(bwd),
        [((2, 256, 256), f32, None), loss_out], [unit_vmem, unit_vmem], flops // 2,
    )
    sums = jnp.sum(got[:, 32:], axis=0) + done
    sums = swap(sums, "ty")
    left_block = pl.BlockSpec((2, 256, N), lambda i: (0, 0, 0))
    tile = pl.pallas_call(
        finish,
        grid=(1,),
        out_shape=jax.ShapeDtypeStruct((2, 256, 256), f32),
        in_specs=[left_block, pl.BlockSpec((16, 32, N), lambda i: (0, 0, 0))],
        out_specs=left_block,
        input_output_aliases={0: 0},
        compiler_params=pltpu.CompilerParams(vmem_limit_bytes=VMEM_BYTES),
    )(tile, got)
    losses = jnp.sum(jnp.sum(sums, axis=0).reshape(2, N // 2), axis=1) * (0.5 / 67108864.0)
    return (tile, losses)


def solution(mesh):
    in_specs = (
        P(None, "ty", "tx"),
        P(None, "ty", "tx"),
        P(),
        P(("ty", "tx"), None, None, None),
        P(),
        P(("ty", "tx"), None),
        P(),
        P(),
    )
    return jax.shard_map(
        shards, mesh=mesh, in_specs=in_specs, out_specs=(P(None, "ty", "tx"), P()), check_vma=False
    )
```

time: 162 us -> 155 us (0.957)
  blocking collectives: 74.1 us -> 43.8 us
  starting transfers between devices: 18.5 us -> 35.9 us
  waiting for transfers between devices: 7.2 us -> 11.1 us
    all_to_all x4 -> x2, blocking collectives: 74.1 us -> 43.8 us  [swap(): return lax.all_to_all(block, axis, 0, 0, tiled=True)]
    all_to_all x4 -> x6, starting transfers between devices: 18.5 us -> 35.9 us  [swap(): return lax.all_to_all(block, axis, 0, 0, tiled=True)]
    pallas_call x6 -> x5, Pallas kernels: 15.3 us -> 9.83 us  [small_call(): pl.pallas_call(kernel, out_shape=[jax.ShapeDtypeStruct(s, d) for s, d, _...]
    all_to_all x4 -> x6, waiting for transfers between devices: 7.2 us -> 11.1 us  [swap(): return lax.all_to_all(block, axis, 0, 0, tiled=True)]
    pallas_call x4 -> x5, Pallas kernels: 43.1 us -> 46.6 us  [run(): pl.pallas_call(kernel, grid=(steps,), out_shape=out_shape, in_specs=[spec...]
    pallas_call x0 -> x1, Pallas kernels: none -> 1.76 us  [shards(): pl.pallas_call(finish, grid=(1,), out_shape=jax.ShapeDtypeStruct((2, 256,...]
  transfers between devices with their start and end apart: 4 -> 6, of which waited for: 1 -> 3; matrix products, arithmetic and copies ran while one was open for 0% -> 0% of each run, Pallas kernels for 27% -> 32%
where the time goes in v4:
time: 155 us; the launch traced here: 153 us
  Pallas kernels  58.2 us (38%)
  blocking collectives  43.8 us (28%)
  starting transfers between devices  35.9 us (23%)
  waiting for transfers between devices  11.1 us (7%)
  other arithmetic  1.97 us (1%)
  local copies, waits for them, and re-layouts  1.73 us (1%)
    pallas_call x5, Pallas kernels, run(): pl.pallas_call(kernel, grid=(steps,), out_shape=out_shape, in_specs=[spec...  46.6 us
    all_to_all x2, blocking collectives, swap(): return lax.all_to_all(block, axis, 0, 0, tiled=True)  43.8 us
    all_to_all x6, starting transfers between devices, swap(): return lax.all_to_all(block, axis, 0, 0, tiled=True)  35.9 us
    all_to_all x6, waiting for transfers between devices, swap(): return lax.all_to_all(block, axis, 0, 0, tiled=True)  11.1 us
    pallas_call x5, Pallas kernels, small_call(): pl.pallas_call(kernel, out_shape=[jax.ShapeDtypeStruct(s, d) for s, d, _...  9.83 us
  transfers between devices with their start and end apart: 6, of which 3 were waited for; matrix products, arithmetic and copies ran while one was open for 0% of the time, Pallas kernels for 32%

profile of v4, /device:TPU:1, one launch (start us, length us, event | category | flops | bytes accessed | tf_op | source)
XLA Modules:
  0.0 153.5 jit_solution(5209338251998548649)
XLA Ops:
  0.6 3.3 %shard_map.122 = (f32[16,168,128]{2,1,0:T(8,128)}, s32[16]{0:T(128)}, s32[16]{0:T(128)}, s32[16]{0:T(128)}, s32[16]{0:T(128)}, /*index=5*/f32[2]{0:T(128)}) custom-call(s32[8,16]{1,0:T(8,128)} %owner_map.1, s32[128]{0:T(128)} %row_tops.1, s32[2]{0:T(128)} %restart.1, f32[101]{0:T(128)} %constant.12.clone.table, s32[1,32]{1,0:T(1,128)} %cols.1, ...), custom_call_target="tpu_custom_call" | custom-call | tf_op jit(solution)/shard_map/pallas_call | solution.py:228
  4.0 28.3 %all_to_all.44.got.amp = f32[16,168,128]{2,1,0:T(8,128)} all-to-all(f32[16,168,128]{2,1,0:T(8,128)} %get-tuple-element.31), channel_id=1, replica_groups=mesh['ty'=8,'tx'=16] {'tx'}, dimensions={0} | all-to-all | bytes 2752512 | tf_op jit(solution)/shard_map/all_to_all | solution.py:313
  32.3 3.3 %shard_map.123 = (f32[16,160,128]{2,1,0:T(8,128)}, s32[16]{0:T(128)}, s32[16]{0:T(128)}) custom-call(s32[16]{0:T(128)} %get-tuple-element.29.right, s32[16]{0:T(128)} %get-tuple-element.30.inv, f32[16,168,128]{2,1,0:T(8,128)} %all_to_all.44.got.amp, f32[32,128,128]{2,1,0:T(8,128)} %bitcast.7), custom_call_target="tpu_custom_call" | custom-call | tf_op jit(solution)/shard_map/pallas_call | solution.py:228
  35.7 3.7 %all-to-all-start.2 = ((f32[16,160,128]{2,1,0:T(8,128)}), f32[16,160,128]{2,1,0:T(8,128)S(1)}, u32[]{:S(2)}, u32[]{:S(2)}) async-start(f32[16,160,128]{2,1,0:T(8,128)} %get-tuple-element.38), calls=%async_computation.2 | async-start | bytes 2621440 | tf_op jit(solution)/shard_map/all_to_all | solution.py:313
  39.4 10.7 %shard_map.124 = (f32[2,2,256,128]{3,2,1,0:T(8,128)}, f32[2,256,128]{2,1,0:T(8,128)}, f32[2,256,128]{2,1,0:T(8,128)}, f32[2,256,128]{2,1,0:T(8,128)}, f32[8,128]{1,0:T(8,128)}) custom-call(s32[16]{0:T(128)} %get-tuple-element.28.rows, s32[16]{0:T(128)} %get-tuple-element.32.offs, f32[2]{0:T(128)} %get-tuple-element.33.beta, f32[2,256,256]{2,1,0:T(8,128)} %obj.5, ...), custom_call_target="tpu_custom_call" | custom-call | flops 6400000000 | bytes 4194304 | tf_op jit(solution)/shard_map/pallas_call | solution.py:215
  50.0 7.2 %all-to-all-done.2.halo.amp = f32[16,160,128]{2,1,0:T(8,128)S(1)} async-done(((f32[16,160,128]{2,1,0:T(8,128)}), f32[16,160,128]{2,1,0:T(8,128)S(1)}, u32[]{:S(2)}, u32[]{:S(2)}) %all-to-all-start.2) | async-done | bytes 1310752 | tf_op jit(solution)/shard_map/all_to_all | solution.py:313
  57.3 4.7 %all-to-all-start.1 = ((f32[16,32,128]{2,1,0:T(8,128)}), f32[16,32,128]{2,1,0:T(8,128)S(1)}, u32[]{:S(2)}, u32[]{:S(2)}) async-start(f32[16,32,128]{2,1,0:T(8,128)} %bitcast.8), calls=%async_computation.1 | async-start | bytes 524288 | tf_op jit(solution)/shard_map/all_to_all | solution.py:313
  62.0 10.5 %shard_map.125 = (f32[2,256,128]{2,1,0:T(8,128)}, f32[2,256,128]{2,1,0:T(8,128)}, f32[8,128]{1,0:T(8,128)}) custom-call(s32[16]{0:T(128)} %get-tuple-element.28.rows, s32[16]{0:T(128)} %get-tuple-element.36.offs, f32[2,2,256,128]{3,2,1,0:T(8,128)} %get-tuple-element.37.z0, f32[16,160,128]{2,1,0:T(8,128)} %copy-done.6, f32[2,2,128,128]{3,2,1,0:T(8,128)} %probe.9, ...), custom_call_target="tpu_custom_call" | custom-call | flops 6400000000 | bytes 4194304 | tf_op jit(solution)/shard_map/pallas_call | solution.py:215
  72.5 0.9 copy-done.1
  74.0 15.4 %all_to_all.45.got.ahead = f32[16,64,128]{2,1,0:T(8,128)S(1)} all-to-all(f32[16,64,128]{2,1,0:T(8,128)S(1)} %shard_map.126), channel_id=1, replica_groups=mesh['ty'=8,'tx'=16] {'tx'}, dimensions={0} | all-to-all | bytes 1048576 | tf_op jit(solution)/shard_map/all_to_all | solution.py:313
  89.5 1.3 shard_map.127
  90.8 3.7 %all-to-all-start.4 = ((f32[16,32,128]{2,1,0:T(8,128)}), f32[16,32,128]{2,1,0:T(8,128)S(1)}, u32[]{:S(2)}, u32[]{:S(2)}) async-start(f32[16,32,128]{2,1,0:T(8,128)} %shard_map.127), calls=%async_computation.4 | async-start | bytes 524288 | tf_op jit(solution)/shard_map/all_to_all | solution.py:313
  94.5 11.1 %shard_map.128 = (f32[2,256,128]{2,1,0:T(8,128)}, f32[2,256,128]{2,1,0:T(8,128)}, f32[2,256,128]{2,1,0:T(8,128)}, f32[8,128]{1,0:T(8,128)}) custom-call(s32[16]{0:T(128)} %get-tuple-element.28.rows, s32[16]{0:T(128)} %get-tuple-element.36.offs, f32[2]{0:T(128)} %get-tuple-element.33.beta, f32[2,2,256,128]{3,2,1,0:T(8,128)} %get-tuple-element.37.z0, ...), custom_call_target="tpu_custom_call" | custom-call | flops 6400000000 | bytes 4194304 | tf_op jit(solution)/shard_map/pallas_call | solution.py:215
  105.6 6.4 %all-to-all-start.5 = ((f32[16,32,128]{2,1,0:T(8,128)}), f32[16,32,128]{2,1,0:T(8,128)S(1)}, u32[]{:S(2)}, u32[]{:S(2)}) async-start(f32[16,32,128]{2,1,0:T(8,128)} %bitcast.9), calls=%async_computation.5 | async-start | bytes 524288 | tf_op jit(solution)/shard_map/all_to_all | solution.py:313
  112.0 7.5 %shard_map.129 = (f32[2,256,128]{2,1,0:T(8,128)}, f32[8,128]{1,0:T(8,128)}, bf16[4096,256]{1,0:T(8,128)(2,1)}, bf16[4096,256]{1,0:T(8,128)(2,1)}) custom-call(s32[16]{0:T(128)} %get-tuple-element.28.rows, s32[16]{0:T(128)} %get-tuple-element.32.offs, f32[2]{0:T(128)} %get-tuple-element.33.beta, f32[2,256,128]{2,1,0:T(8,128)} %get-tuple-element.34.ahead, ...), custom_call_target="tpu_custom_call" | custom-call | flops 3200000000 | bytes 4194304 | tf_op jit(solution)/shard_map/pallas_call | solution.py:215
  119.6 0.7 copy-done.2
  120.2 1.3 shard_map.131
  121.5 6.6 %all-to-all-start.6 = ((f32[16,40,128]{2,1,0:T(8,128)}), f32[16,40,128]{2,1,0:T(8,128)S(1)}, u32[]{:S(2)}, u32[]{:S(2)}) async-start(f32[16,40,128]{2,1,0:T(8,128)} %shard_map.131), calls=%async_computation.6 | async-start | bytes 655360 | tf_op jit(solution)/shard_map/all_to_all | solution.py:313
  128.2 6.9 %shard_map.130 = (f32[2,256,256]{2,1,0:T(8,128)}, f32[8,128]{1,0:T(8,128)}) custom-call(s32[16]{0:T(128)} %get-tuple-element.28.rows, s32[16]{0:T(128)} %get-tuple-element.32.offs, f32[2,256,128]{2,1,0:T(8,128)} %get-tuple-element.46.start, f32[2,256,128]{2,1,0:T(8,128)} %get-tuple-element.42.mid, f32[2,256,128]{2,1,0:T(8,128)} %get-tuple-element.47.odd_low, ...), custom_call_target="tpu_custom_call" | custom-call | flops 3200000000 | bytes 4194304 | tf_op jit(solution)/shard_map/pallas_call | solution.py:215
  135.0 1.0 all-to-all-done.6.got
  136.1 1.3 add.3
  137.4 10.8 %all-to-all-start.7 = ((f32[8,1,128]{2,1,0:T(1,128)}), f32[8,1,128]{2,1,0:T(1,128)S(1)}, u32[]{:S(2)}, u32[]{:S(2)}) async-start(f32[8,1,128]{2,1,0:T(1,128)} %bitcast.4), calls=%async_computation.7 | async-start | bytes 8192 | tf_op jit(solution)/shard_map/all_to_all | solution.py:313
  148.2 1.8 %shard_map.132 = f32[2,256,256]{2,1,0:T(8,128)} custom-call(f32[2,256,256]{2,1,0:T(8,128)} %get-tuple-element.50.tile, f32[16,40,128]{2,1,0:T(8,128)} %copy-done.5), custom_call_target="tpu_custom_call", output_to_operand_aliasing={{}: (0, {})} | custom-call | tf_op jit(solution)/shard_map/pallas_call | solution.py:387
  149.9 2.8 %all-to-all-done.7 = f32[8,1,128]{2,1,0:T(1,128)S(1)} async-done(((f32[8,1,128]{2,1,0:T(1,128)}), f32[8,1,128]{2,1,0:T(1,128)S(1)}, u32[]{:S(2)}, u32[]{:S(2)}) %all-to-all-start.7) | async-done | bytes 4128 | tf_op jit(solution)/shard_map/all_to_all | solution.py:313
  (23 shorter events, 1.4 us)
Async XLA Ops:
  35.7 21.6 %all-to-all-start.2 = ((f32[16,160,128]{2,1,0:T(8,128)}), f32[16,160,128]{2,1,0:T(8,128)S(1)}, u32[]{:S(2)}, u32[]{:S(2)}) async-start(f32[16,160,128]{2,1,0:T(8,128)} %get-tuple-element.38), calls=%async_computation.2 | async-start | bytes 2621440 | tf_op jit(solution)/shard_map/all_to_all | solution.py:313
  57.3 4.7 %copy-start.6 = (f32[16,160,128]{2,1,0:T(8,128)}, f32[16,160,128]{2,1,0:T(8,128)S(1)}, u32[]{:S(2)}) copy-start(f32[16,160,128]{2,1,0:T(8,128)S(1)} %all-to-all-done.2.halo.amp) | copy-start | bytes 3932164
  57.3 15.2 %all-to-all-start.1 = ((f32[16,32,128]{2,1,0:T(8,128)}), f32[16,32,128]{2,1,0:T(8,128)S(1)}, u32[]{:S(2)}, u32[]{:S(2)}) async-start(f32[16,32,128]{2,1,0:T(8,128)} %bitcast.8), calls=%async_computation.1 | async-start | bytes 524288 | tf_op jit(solution)/shard_map/all_to_all | solution.py:313
  62.0 10.5 %copy-start.3 = (s32[16]{0:T(128)S(1)}, s32[16]{0:T(128)}, u32[]{:S(2)}) copy-start(s32[16]{0:T(128)} %get-tuple-element.29.right) | copy-start | bytes 196
  72.5 17.0 %copy-start.4 = (s32[16]{0:T(128)S(1)}, s32[16]{0:T(128)}, u32[]{:S(2)}) copy-start(s32[16]{0:T(128)} %get-tuple-element.35.left) | copy-start | bytes 196
  72.5 1.0 copy-start.1
  89.5 5.0 %copy-start = (f32[16,64,128]{2,1,0:T(8,128)}, f32[16,64,128]{2,1,0:T(8,128)S(1)}, u32[]{:S(2)}) copy-start(f32[16,64,128]{2,1,0:T(8,128)S(1)} %all_to_all.45.got.ahead) | copy-start | bytes 1572868
  90.8 14.8 %all-to-all-start.4 = ((f32[16,32,128]{2,1,0:T(8,128)}), f32[16,32,128]{2,1,0:T(8,128)S(1)}, u32[]{:S(2)}, u32[]{:S(2)}) async-start(f32[16,32,128]{2,1,0:T(8,128)} %shard_map.127), calls=%async_computation.4 | async-start | bytes 524288 | tf_op jit(solution)/shard_map/all_to_all | solution.py:313
  105.6 6.4 %copy-start.7 = (f32[16,32,128]{2,1,0:T(8,128)}, f32[16,32,128]{2,1,0:T(8,128)S(1)}, u32[]{:S(2)}) copy-start(f32[16,32,128]{2,1,0:T(8,128)S(1)} %all-to-all-done.4.from_left) | copy-start | bytes 786436
  105.6 14.0 %all-to-all-start.5 = ((f32[16,32,128]{2,1,0:T(8,128)}), f32[16,32,128]{2,1,0:T(8,128)S(1)}, u32[]{:S(2)}, u32[]{:S(2)}) async-start(f32[16,32,128]{2,1,0:T(8,128)} %bitcast.9), calls=%async_computation.5 | async-start | bytes 524288 | tf_op jit(solution)/shard_map/all_to_all | solution.py:313
  119.6 0.7 copy-start.2
  121.5 14.5 %all-to-all-start.6 = ((f32[16,40,128]{2,1,0:T(8,128)}), f32[16,40,128]{2,1,0:T(8,128)S(1)}, u32[]{:S(2)}, u32[]{:S(2)}) async-start(f32[16,40,128]{2,1,0:T(8,128)} %shard_map.131), calls=%async_computation.6 | async-start | bytes 655360 | tf_op jit(solution)/shard_map/all_to_all | solution.py:313
  136.1 12.1 %copy-start.5 = (f32[16,40,128]{2,1,0:T(8,128)}, f32[16,40,128]{2,1,0:T(8,128)S(1)}, u32[]{:S(2)}) copy-start(f32[16,40,128]{2,1,0:T(8,128)S(1)} %all-to-all-done.6.got) | copy-start | bytes 983044
  137.4 15.4 %all-to-all-start.7 = ((f32[8,1,128]{2,1,0:T(1,128)}), f32[8,1,128]{2,1,0:T(1,128)S(1)}, u32[]{:S(2)}, u32[]{:S(2)}) async-start(f32[8,1,128]{2,1,0:T(1,128)} %bitcast.4), calls=%async_computation.7 | async-start | bytes 8192 | tf_op jit(solution)/shard_map/all_to_all | solution.py:313

commit v5 on v4

--- a/solution.py
+++ b/solution.py
@@ -151,7 +151,7 @@
 
 
 def odd_first(rows, offs, z0, halo, probe, amp, fwd, bwd, odd_low, odd_high, loss, z):
-    z[0] = z0[1]
+    z[0] = z0[0]
     for d in range(16):
         chunk_of(z.at[1], d)[...] = halo[d]
     all_positions(rows, offs, z, probe, amp, fwd, bwd, odd_low, odd_high, loss)
@@ -164,8 +164,8 @@
     b = beta[1]
     scale = (1.0 + b) * STEP
     for k in range(2):
-        now = z0[1, k] - STEP * (even_high[k] + odd_low[k])
-        mid[k] = now + b * (now - unit(obj, k, 1))
+        now = z0[0, k] - STEP * (even_high[k] + odd_low[k])
+        mid[k] = now + b * (now - obj[k])
         z[0, k] = mid[k]
     for d in range(16):
         chunk_of(z.at[1], d)[...] = ahead[d, :32] - scale * chunk_of(odd_high, d)[...]
@@ -195,10 +195,10 @@
         sums[...] = jnp.broadcast_to(line, sums.shape)
 
 
-def even_back(rows, offs, start, mid, odd_low, probe, high, low, bwd, tile, done, even_low, even_high):
+def even_back(rows, offs, start, mid, odd_low, probe, high, low, bwd, tile, even_low, even_high):
     @pl.when(pl.program_id(0) == 0)
     def _():
-        clear(even_low, even_high, done)
+        clear(even_low, even_high)
 
     way_back(rows, offs, probe, (high, low), bwd, even_low, even_high, pl.program_id(0) * GROUP)
 
@@ -320,6 +320,7 @@
     z_vmem = pltpu.VMEM((2, 2, 256, N), f32)
     unit_vmem = pltpu.VMEM((2, 256, N), f32)
     images = pl.BlockSpec((16, N, N), lambda i: (0, 0, 0))
+    right_unit = pl.BlockSpec((1, 2, 256, N), lambda i: (1, 0, 0, 0))
     edge = pl.BlockSpec((16, 32, N), lambda i: (0, N // 32, 0))
     plain = lambda *arrays: [(a, None) for a in arrays]
     small = lambda *arrays: [(a, SMEM) for a in arrays]
@@ -347,7 +348,7 @@
     got = swap(ahead.reshape(16, 32, N))
     odd_low, odd_high, loss_b = run(
         odd_first, 1,
-        small(rows, off_odd) + plain(z0) + [(amp_odd, edge)] + plain(probe) + [(amp_odd, images)] + plain(fwd, bwd),
+        small(rows, off_odd) + [(z0, right_unit), (amp_odd, edge)] + plain(probe) + [(amp_odd, images)] + plain(fwd, bwd),
         [unit_out, unit_out, loss_out], [z_vmem], flops,
     )
     (send,) = small_call(
@@ -358,7 +359,8 @@
     from_left = swap(send)
     mid, odd_low_second, odd_high_second, loss_c = run(
         odd_second, 1,
-        small(rows, off_odd, beta) + plain(z0, obj, even_high, odd_low, odd_high, got, probe)
+        small(rows, off_odd, beta) + [(z0, right_unit), (obj, pl.BlockSpec((2, 256, N), lambda i: (0, 0, 1)))]
+        + plain(even_high, odd_low, odd_high, got, probe)
         + [(amp_odd, images)] + plain(fwd, bwd),
         [unit_out, unit_out, unit_out, loss_out], [z_vmem], flops,
     )
@@ -375,13 +377,14 @@
         pass_last, small(left) + [(last, VMEM), (sums, VMEM)], [((16, 40, N), f32, VMEM)]
     )
     got = swap(send)
-    tile, done = run(
+    (tile,) = run(
         even_back, 16 // GROUP,
         small(rows, off_even) + plain(start, mid, odd_low_second, probe)
         + [(high, half_block), (low, half_block)] + plain(bwd),
-        [((2, 256, 256), f32, None), loss_out], [unit_vmem, unit_vmem], flops // 2,
-    )
-    sums = jnp.sum(got[:, 32:], axis=0) + done
+        [((2, 256, 256), f32, None)], [unit_vmem, unit_vmem], flops // 2,
+    )
+    got, tile = lax.optimization_barrier((got, tile))
+    sums = jnp.sum(got[:, 32:], axis=0)
     sums = swap(sums, "ty")
     left_block = pl.BlockSpec((2, 256, N), lambda i: (0, 0, 0))
     tile = pl.pallas_call(

time: 155 us -> 154 us (level)
  no operation moved by 1% of the time
where the time goes in v5:
time: 154 us; the launch traced here: 153 us
  Pallas kernels  58.1 us (38%)
  blocking collectives  43.8 us (28%)
  starting transfers between devices  35.9 us (23%)
  waiting for transfers between devices  11 us (7%)
  local copies, waits for them, and re-layouts  1.73 us (1%)
    pallas_call x5, Pallas kernels, run(): pl.pallas_call(kernel, grid=(steps,), out_shape=out_shape, in_specs=[spec...  46.5 us
    all_to_all x2, blocking collectives, swap(): return lax.all_to_all(block, axis, 0, 0, tiled=True)  43.8 us
    all_to_all x6, starting transfers between devices, swap(): return lax.all_to_all(block, axis, 0, 0, tiled=True)  35.9 us
    all_to_all x6, waiting for transfers between devices, swap(): return lax.all_to_all(block, axis, 0, 0, tiled=True)  11 us
    pallas_call x5, Pallas kernels, small_call(): pl.pallas_call(kernel, out_shape=[jax.ShapeDtypeStruct(s, d) for s, d, _...  9.83 us
  transfers between devices with their start and end apart: 6, of which 3 were waited for; matrix products, arithmetic and copies ran while one was open for 0% of the time, Pallas kernels for 32%

profile of v5, /device:TPU:1, one launch (start us, length us, event | category | flops | bytes accessed | tf_op | source)
XLA Modules:
  0.0 152.7 jit_solution(12232055279061921303)
XLA Ops:
  0.6 3.3 %shard_map.122 = (f32[16,168,128]{2,1,0:T(8,128)}, s32[16]{0:T(128)}, s32[16]{0:T(128)}, s32[16]{0:T(128)}, s32[16]{0:T(128)}, /*index=5*/f32[2]{0:T(128)}) custom-call(s32[8,16]{1,0:T(8,128)} %owner_map.1, s32[128]{0:T(128)} %row_tops.1, s32[2]{0:T(128)} %restart.1, f32[101]{0:T(128)} %constant.12.clone.table, s32[1,32]{1,0:T(1,128)} %cols.1, ...), custom_call_target="tpu_custom_call" | custom-call | tf_op jit(solution)/shard_map/pallas_call | solution.py:228
  4.0 28.3 %all_to_all.44.got.amp = f32[16,168,128]{2,1,0:T(8,128)} all-to-all(f32[16,168,128]{2,1,0:T(8,128)} %get-tuple-element.32), channel_id=1, replica_groups=mesh['ty'=8,'tx'=16] {'tx'}, dimensions={0} | all-to-all | bytes 2752512 | tf_op jit(solution)/shard_map/all_to_all | solution.py:313
  32.3 3.3 %shard_map.123 = (f32[16,160,128]{2,1,0:T(8,128)}, s32[16]{0:T(128)}, s32[16]{0:T(128)}) custom-call(s32[16]{0:T(128)} %get-tuple-element.30.right, s32[16]{0:T(128)} %get-tuple-element.31.inv, f32[16,168,128]{2,1,0:T(8,128)} %all_to_all.44.got.amp, f32[32,128,128]{2,1,0:T(8,128)} %bitcast.5), custom_call_target="tpu_custom_call" | custom-call | tf_op jit(solution)/shard_map/pallas_call | solution.py:228
  35.6 3.7 %all-to-all-start.1 = ((f32[16,160,128]{2,1,0:T(8,128)}), f32[16,160,128]{2,1,0:T(8,128)S(1)}, u32[]{:S(2)}, u32[]{:S(2)}) async-start(f32[16,160,128]{2,1,0:T(8,128)} %get-tuple-element.38), calls=%async_computation.1 | async-start | bytes 2621440 | tf_op jit(solution)/shard_map/all_to_all | solution.py:313
  39.4 10.7 %shard_map.124 = (f32[2,2,256,128]{3,2,1,0:T(8,128)}, f32[2,256,128]{2,1,0:T(8,128)}, f32[2,256,128]{2,1,0:T(8,128)}, f32[2,256,128]{2,1,0:T(8,128)}, f32[8,128]{1,0:T(8,128)}) custom-call(s32[16]{0:T(128)} %get-tuple-element.29.rows, s32[16]{0:T(128)} %get-tuple-element.35.offs, f32[2]{0:T(128)} %get-tuple-element.34.beta, f32[2,256,256]{2,1,0:T(8,128)} %obj.5, ...), custom_call_target="tpu_custom_call" | custom-call | flops 6400000000 | bytes 4194304 | tf_op jit(solution)/shard_map/pallas_call | solution.py:215
  50.1 7.2 %all-to-all-done.1.halo.amp = f32[16,160,128]{2,1,0:T(8,128)S(1)} async-done(((f32[16,160,128]{2,1,0:T(8,128)}), f32[16,160,128]{2,1,0:T(8,128)S(1)}, u32[]{:S(2)}, u32[]{:S(2)}) %all-to-all-start.1) | async-done | bytes 1310752 | tf_op jit(solution)/shard_map/all_to_all | solution.py:313
  57.2 4.7 %all-to-all-start.2 = ((f32[16,32,128]{2,1,0:T(8,128)}), f32[16,32,128]{2,1,0:T(8,128)S(1)}, u32[]{:S(2)}, u32[]{:S(2)}) async-start(f32[16,32,128]{2,1,0:T(8,128)} %bitcast.6), calls=%async_computation.2 | async-start | bytes 524288 | tf_op jit(solution)/shard_map/all_to_all | solution.py:313
  62.0 10.5 %shard_map.125 = (f32[2,256,128]{2,1,0:T(8,128)}, f32[2,256,128]{2,1,0:T(8,128)}, f32[8,128]{1,0:T(8,128)}) custom-call(s32[16]{0:T(128)} %get-tuple-element.29.rows, s32[16]{0:T(128)} %get-tuple-element.33.offs, f32[2,2,256,128]{3,2,1,0:T(8,128)} %get-tuple-element.36.z0, f32[16,160,128]{2,1,0:T(8,128)} %copy-done.6, f32[2,2,128,128]{3,2,1,0:T(8,128)} %probe.9, ...), custom_call_target="tpu_custom_call" | custom-call | flops 6400000000 | bytes 4194304 | tf_op jit(solution)/shard_map/pallas_call | solution.py:215
  72.5 0.9 copy-done.1
  74.0 15.4 %all_to_all.45.ahead.got = f32[16,64,128]{2,1,0:T(8,128)S(1)} all-to-all(f32[16,64,128]{2,1,0:T(8,128)S(1)} %shard_map.126), channel_id=1, replica_groups=mesh['ty'=8,'tx'=16] {'tx'}, dimensions={0} | all-to-all | bytes 1048576 | tf_op jit(solution)/shard_map/all_to_all | solution.py:313
  89.5 1.3 shard_map.128
  90.7 3.7 %all-to-all-start.5 = ((f32[16,32,128]{2,1,0:T(8,128)}), f32[16,32,128]{2,1,0:T(8,128)S(1)}, u32[]{:S(2)}, u32[]{:S(2)}) async-start(f32[16,32,128]{2,1,0:T(8,128)} %shard_map.128), calls=%async_computation.5 | async-start | bytes 524288 | tf_op jit(solution)/shard_map/all_to_all | solution.py:313
  94.5 10.9 %shard_map.127 = (f32[2,256,128]{2,1,0:T(8,128)}, f32[2,256,128]{2,1,0:T(8,128)}, f32[2,256,128]{2,1,0:T(8,128)}, f32[8,128]{1,0:T(8,128)}) custom-call(s32[16]{0:T(128)} %get-tuple-element.29.rows, s32[16]{0:T(128)} %get-tuple-element.33.offs, f32[2]{0:T(128)} %get-tuple-element.34.beta, f32[2,2,256,128]{3,2,1,0:T(8,128)} %get-tuple-element.36.z0, ...), custom_call_target="tpu_custom_call" | custom-call | flops 6400000000 | bytes 4194304 | tf_op jit(solution)/shard_map/pallas_call | solution.py:215
  105.4 6.4 %all-to-all-start.4 = ((f32[16,32,128]{2,1,0:T(8,128)}), f32[16,32,128]{2,1,0:T(8,128)S(1)}, u32[]{:S(2)}, u32[]{:S(2)}) async-start(f32[16,32,128]{2,1,0:T(8,128)} %bitcast.7), calls=%async_computation.4 | async-start | bytes 524288 | tf_op jit(solution)/shard_map/all_to_all | solution.py:313
  111.9 7.5 %shard_map.129 = (f32[2,256,128]{2,1,0:T(8,128)}, f32[8,128]{1,0:T(8,128)}, bf16[4096,256]{1,0:T(8,128)(2,1)}, bf16[4096,256]{1,0:T(8,128)(2,1)}) custom-call(s32[16]{0:T(128)} %get-tuple-element.29.rows, s32[16]{0:T(128)} %get-tuple-element.35.offs, f32[2]{0:T(128)} %get-tuple-element.34.beta, f32[2,256,128]{2,1,0:T(8,128)} %get-tuple-element.41.ahead, ...), custom_call_target="tpu_custom_call" | custom-call | flops 3200000000 | bytes 4194304 | tf_op jit(solution)/shard_map/pallas_call | solution.py:215
  119.4 0.7 copy-done.2
  120.1 1.3 shard_map.130
  121.4 6.6 %all-to-all-start.6 = ((f32[16,40,128]{2,1,0:T(8,128)}), f32[16,40,128]{2,1,0:T(8,128)S(1)}, u32[]{:S(2)}, u32[]{:S(2)}) async-start(f32[16,40,128]{2,1,0:T(8,128)} %shard_map.130), calls=%async_computation.6 | async-start | bytes 655360 | tf_op jit(solution)/shard_map/all_to_all | solution.py:313
  128.0 6.9 %shard_map.131.tile = f32[2,256,256]{2,1,0:T(8,128)} custom-call(s32[16]{0:T(128)} %get-tuple-element.29.rows, s32[16]{0:T(128)} %get-tuple-element.35.offs, f32[2,256,128]{2,1,0:T(8,128)} %get-tuple-element.48.start, f32[2,256,128]{2,1,0:T(8,128)} %get-tuple-element.43.mid, f32[2,256,128]{2,1,0:T(8,128)} %get-tuple-element.49.odd_low, ...), custom_call_target="tpu_custom_call" | custom-call | flops 3200000000 | bytes 4194304 | tf_op jit(solution)/shard_map/pallas_call | solution.py:215
  134.9 1.0 all-to-all-done.6.got
  135.9 0.6 slice_reduce_fusion
  136.6 10.8 %all-to-all-start.7 = ((f32[8,1,128]{2,1,0:T(1,128)}), f32[8,1,128]{2,1,0:T(1,128)S(1)}, u32[]{:S(2)}, u32[]{:S(2)}) async-start(f32[8,1,128]{2,1,0:T(1,128)} %bitcast.3), calls=%async_computation.7 | async-start | bytes 8192 | tf_op jit(solution)/shard_map/all_to_all | solution.py:313
  147.3 1.8 %shard_map.132 = f32[2,256,256]{2,1,0:T(8,128)} custom-call(f32[2,256,256]{2,1,0:T(8,128)} %shard_map.131.tile, f32[16,40,128]{2,1,0:T(8,128)} %copy-done.5), custom_call_target="tpu_custom_call", output_to_operand_aliasing={{}: (0, {})} | custom-call | tf_op jit(solution)/shard_map/pallas_call | solution.py:390
  149.1 2.8 %all-to-all-done.7 = f32[8,1,128]{2,1,0:T(1,128)S(1)} async-done(((f32[8,1,128]{2,1,0:T(1,128)}), f32[8,1,128]{2,1,0:T(1,128)S(1)}, u32[]{:S(2)}, u32[]{:S(2)}) %all-to-all-start.7) | async-done | bytes 4128 | tf_op jit(solution)/shard_map/all_to_all | solution.py:313
  (22 shorter events, 1.4 us)
Async XLA Ops:
  35.6 21.6 %all-to-all-start.1 = ((f32[16,160,128]{2,1,0:T(8,128)}), f32[16,160,128]{2,1,0:T(8,128)S(1)}, u32[]{:S(2)}, u32[]{:S(2)}) async-start(f32[16,160,128]{2,1,0:T(8,128)} %get-tuple-element.38), calls=%async_computation.1 | async-start | bytes 2621440 | tf_op jit(solution)/shard_map/all_to_all | solution.py:313
  57.2 4.7 %copy-start.6 = (f32[16,160,128]{2,1,0:T(8,128)}, f32[16,160,128]{2,1,0:T(8,128)S(1)}, u32[]{:S(2)}) copy-start(f32[16,160,128]{2,1,0:T(8,128)S(1)} %all-to-all-done.1.halo.amp) | copy-start | bytes 3932164
  57.2 15.2 %all-to-all-start.2 = ((f32[16,32,128]{2,1,0:T(8,128)}), f32[16,32,128]{2,1,0:T(8,128)S(1)}, u32[]{:S(2)}, u32[]{:S(2)}) async-start(f32[16,32,128]{2,1,0:T(8,128)} %bitcast.6), calls=%async_computation.2 | async-start | bytes 524288 | tf_op jit(solution)/shard_map/all_to_all | solution.py:313
  62.0 10.5 %copy-start.3 = (s32[16]{0:T(128)S(1)}, s32[16]{0:T(128)}, u32[]{:S(2)}) copy-start(s32[16]{0:T(128)} %get-tuple-element.30.right) | copy-start | bytes 196
  72.5 17.0 %copy-start.4 = (s32[16]{0:T(128)S(1)}, s32[16]{0:T(128)}, u32[]{:S(2)}) copy-start(s32[16]{0:T(128)} %get-tuple-element.28.left) | copy-start | bytes 196
  72.5 1.0 copy-start.1
  89.5 5.0 %copy-start = (f32[16,64,128]{2,1,0:T(8,128)}, f32[16,64,128]{2,1,0:T(8,128)S(1)}, u32[]{:S(2)}) copy-start(f32[16,64,128]{2,1,0:T(8,128)S(1)} %all_to_all.45.ahead.got) | copy-start | bytes 1572868
  90.7 14.7 %all-to-all-start.5 = ((f32[16,32,128]{2,1,0:T(8,128)}), f32[16,32,128]{2,1,0:T(8,128)S(1)}, u32[]{:S(2)}, u32[]{:S(2)}) async-start(f32[16,32,128]{2,1,0:T(8,128)} %shard_map.128), calls=%async_computation.5 | async-start | bytes 524288 | tf_op jit(solution)/shard_map/all_to_all | solution.py:313
  105.4 6.4 %copy-start.7 = (f32[16,32,128]{2,1,0:T(8,128)}, f32[16,32,128]{2,1,0:T(8,128)S(1)}, u32[]{:S(2)}) copy-start(f32[16,32,128]{2,1,0:T(8,128)S(1)} %all-to-all-done.5.from_left) | copy-start | bytes 786436
  105.4 14.0 %all-to-all-start.4 = ((f32[16,32,128]{2,1,0:T(8,128)}), f32[16,32,128]{2,1,0:T(8,128)S(1)}, u32[]{:S(2)}, u32[]{:S(2)}) async-start(f32[16,32,128]{2,1,0:T(8,128)} %bitcast.7), calls=%async_computation.4 | async-start | bytes 524288 | tf_op jit(solution)/shard_map/all_to_all | solution.py:313
  119.4 0.7 copy-start.2
  121.4 14.6 %all-to-all-start.6 = ((f32[16,40,128]{2,1,0:T(8,128)}), f32[16,40,128]{2,1,0:T(8,128)S(1)}, u32[]{:S(2)}, u32[]{:S(2)}) async-start(f32[16,40,128]{2,1,0:T(8,128)} %shard_map.130), calls=%async_computation.6 | async-start | bytes 655360 | tf_op jit(solution)/shard_map/all_to_all | solution.py:313
  135.9 11.4 %copy-start.5 = (f32[16,40,128]{2,1,0:T(8,128)}, f32[16,40,128]{2,1,0:T(8,128)S(1)}, u32[]{:S(2)}) copy-start(f32[16,40,128]{2,1,0:T(8,128)S(1)} %all-to-all-done.6.got) | copy-start | bytes 983044
  136.6 15.3 %all-to-all-start.7 = ((f32[8,1,128]{2,1,0:T(1,128)}), f32[8,1,128]{2,1,0:T(1,128)S(1)}, u32[]{:S(2)}, u32[]{:S(2)}) async-start(f32[8,1,128]{2,1,0:T(1,128)} %bitcast.3), calls=%async_computation.7 | async-start | bytes 8192 | tf_op jit(solution)/shard_map/all_to_all | solution.py:313

commit v6 on v5

--- a/solution.py
+++ b/solution.py
@@ -21,6 +21,7 @@
 SMEM = pl.BlockSpec(memory_space=pltpu.SMEM)
 VMEM = pl.BlockSpec(memory_space=pltpu.VMEM)
 ANY = pl.BlockSpec(memory_space=pl.ANY)
+HBM = pl.BlockSpec(memory_space=pltpu.HBM)
 
 
 def momentum_table():
@@ -188,11 +189,11 @@
 
     @pl.when(pl.program_id(0) == pl.num_programs(0) - 1)
     def _():
-        before = jnp.sum(loss_a[...] + loss_b[...], axis=0, keepdims=True)
-        after = jnp.sum(loss_c[...] + loss[...], axis=0, keepdims=True)
-        lane = lax.broadcasted_iota(jnp.int32, (1, N), 1)
-        line = jnp.where(lane < N // 2, before + pltpu.roll(before, N // 2, 1), after + pltpu.roll(after, N // 2, 1))
-        sums[...] = jnp.broadcast_to(line, sums.shape)
+        whole = lambda x: jnp.sum(jnp.sum(x, axis=0, keepdims=True), axis=1, keepdims=True)
+        lane = lax.broadcasted_iota(jnp.int32, (32, N), 1)
+        line = lax.broadcasted_iota(jnp.int32, (32, N), 0)
+        both = jnp.where(line < 16, whole(loss_a[...] + loss_b[...]), whole(loss_c[...] + loss[...]))
+        sums[...] = jnp.where(lane == N - 1, both, 0.0)
 
 
 def even_back(rows, offs, start, mid, odd_low, probe, high, low, bwd, tile, even_low, even_high):
@@ -259,19 +260,20 @@
     for c in edges:
         c.wait()
     now[...] = now[...] + beta[0] * (now[...] - before[...])
-    lane = lax.broadcasted_iota(jnp.int32, (8, N), 1)
+    lane = lax.broadcasted_iota(jnp.int32, (32, N), 1)
+    line = lax.broadcasted_iota(jnp.int32, (32, N), 0)
     for d in range(16):
         col = inv[d]
         even = cols[0, 2 * col] - 2 * N * col
         odd = cols[0, 2 * col + 1] - 2 * N * col - N
-        send[d, N : N + 32] = chunk_of(now, d)[...]
-        send[d, N + 32 :] = jnp.where(lane < N // 2, even, odd).astype(f32)
+        places = jnp.where(line == 0, even, odd).astype(f32)
+        send[d, N:] = jnp.where(lane == N - 1, places, chunk_of(now, d)[...])
     for c in copies:
         c.wait()
 
 
 def pass_halo(right, inv, got, amp, send, off_even, off_odd, places, sems):
-    fetch_places = pltpu.make_async_copy(got.at[:, pl.ds(N + 32, 1)], places, sems.at[32])
+    fetch_places = pltpu.make_async_copy(got.at[:, pl.ds(N, 2)], places, sems.at[32])
     fetch_places.start()
     copies = start_all(
         [(amp.at[2 * inv[d] + 1], send.at[d, pl.ds(0, N)]) for d in range(16)]
@@ -280,16 +282,20 @@
     )
     fetch_places.wait()
     for r in range(16):
-        off_even[r] = places[r, 0, 0].astype(jnp.int32)
-        off_odd[r] = places[r, 0, N // 2].astype(jnp.int32)
+        off_even[r] = places[r, 0, N - 1].astype(jnp.int32)
+        off_odd[r] = places[r, 1, N - 1].astype(jnp.int32)
     for c in copies:
         c.wait()
 
 
-def pass_ahead(right, ahead, odd_high, send):
+def pass_ahead(right, ahead, odd_high, send, edge, sem):
+    fetch = pltpu.make_async_copy(odd_high, edge, sem)
+    fetch.start()
     for d in range(16):
         send[d, :32] = ahead[right[d]]
-        send[d, 32:] = chunk_of(odd_high, d)[...]
+    fetch.wait()
+    for d in range(16):
+        send[d, 32:] = chunk_of(edge, d)[...]
 
 
 def pass_left(left, got, send):
@@ -299,14 +305,14 @@
 
 def pass_last(left, got, sums, send):
     for d in range(16):
-        send[d, :32] = got[left[d]]
-        send[d, 32:] = sums[...]
+        send[d] = got[left[d]] + sums[...]
 
 
 def finish(tile, got, out):
+    edge = lax.broadcasted_iota(jnp.int32, (32, N), 1) < N - 1
     for d in range(16):
         at = pl.ds(32 * (d % 8), 32)
-        out[d // 8, at] = tile[d // 8, at] - STEP * got[d]
+        out[d // 8, at] = tile[d // 8, at] - STEP * jnp.where(edge, got[d], 0.0)
 
 
 def swap(block, axis="tx"):
@@ -331,14 +337,14 @@
         prepare,
         small(owner_map, row_tops, restart, momentum_table(), scan_cols)
         + [(obj, ANY), (prev, ANY), (amplitude, ANY)],
-        [((16, N + 40, N), f32, VMEM), ints, ints, ints, ints, ((2,), f32, SMEM)],
+        [((16, N + 32, N), f32, VMEM), ints, ints, ints, ints, ((2,), f32, SMEM)],
         [unit_vmem, unit_vmem, pltpu.SemaphoreType.DMA((18,))], limit=VMEM_BYTES,
     )
     amp_even = swap(send)
     send, off_even, off_odd = small_call(
         pass_halo, small(right, inv) + [(amp_even, ANY), (amplitude, ANY)],
         [((16, N + 32, N), f32, VMEM), ints, ints],
-        [pltpu.SMEM((16, 1, N), f32), pltpu.SemaphoreType.DMA((33,))], limit=VMEM_BYTES,
+        [pltpu.SMEM((16, 2, N), f32), pltpu.SemaphoreType.DMA((33,))], limit=VMEM_BYTES,
     )
     amp_odd = swap(send)
     z0, even_low, even_high, ahead, loss_a = run(
@@ -352,7 +358,8 @@
         [unit_out, unit_out, loss_out], [z_vmem], flops,
     )
     (send,) = small_call(
-        pass_ahead, small(right) + [(got, VMEM), (odd_high, VMEM)], [((16, 64, N), f32, VMEM)]
+        pass_ahead, small(right) + [(got, VMEM), (odd_high, HBM)], [((16, 64, N), f32, VMEM)],
+        [unit_vmem, pltpu.SemaphoreType.DMA(())],
     )
     got = swap(send)
     (send,) = small_call(pass_left, small(left) + [(got, VMEM)], [((16, 32, N), f32, VMEM)])
@@ -371,10 +378,10 @@
         even_out, 16 // GROUP,
         small(rows, off_even, beta) + plain(ahead, from_left, mid, loss_a, loss_b, loss_c, probe)
         + [(amp_even, pl.BlockSpec((GROUP, N, N), lambda i: (i, 0, 0)))] + plain(fwd),
-        [unit_out, loss_out, half_out, half_out], [pltpu.VMEM((8, N), f32), z_vmem], flops // 2,
+        [unit_out, ((32, N), f32, None), half_out, half_out], [pltpu.VMEM((8, N), f32), z_vmem], flops // 2,
     )
     (send,) = small_call(
-        pass_last, small(left) + [(last, VMEM), (sums, VMEM)], [((16, 40, N), f32, VMEM)]
+        pass_last, small(left) + [(last, VMEM), (sums, VMEM)], [((16, 32, N), f32, VMEM)]
     )
     got = swap(send)
     (tile,) = run(
@@ -384,7 +391,7 @@
         [((2, 256, 256), f32, None)], [unit_vmem, unit_vmem], flops // 2,
     )
     got, tile = lax.optimization_barrier((got, tile))
-    sums = jnp.sum(got[:, 32:], axis=0)
+    sums = jnp.broadcast_to(jnp.tile(jnp.sum(got[:, :, N - 1], axis=0), 4), (8, N))
     sums = swap(sums, "ty")
     left_block = pl.BlockSpec((2, 256, N), lambda i: (0, 0, 0))
     tile = pl.pallas_call(
@@ -396,7 +403,7 @@
         input_output_aliases={0: 0},
         compiler_params=pltpu.CompilerParams(vmem_limit_bytes=VMEM_BYTES),
     )(tile, got)
-    losses = jnp.sum(jnp.sum(sums, axis=0).reshape(2, N // 2), axis=1) * (0.5 / 67108864.0)
+    losses = jnp.sum(sums, axis=0)[: 32 : 16] * (0.5 / 67108864.0)
     return (tile, losses)
 
 

time: 154 us -> 153 us (level)
  no operation moved by 1% of the time
where the time goes in v6:
time: 153 us; the launch traced here: 152 us
  Pallas kernels  58.1 us (38%)
  blocking collectives  43.1 us (28%)
  starting transfers between devices  35.9 us (23%)
  waiting for transfers between devices  10.7 us (7%)
  local copies, waits for them, and re-layouts  2.47 us (2%)
    pallas_call x5, Pallas kernels, run(): pl.pallas_call(kernel, grid=(steps,), out_shape=out_shape, in_specs=[spec...  46.6 us
    all_to_all x2, blocking collectives, swap(): return lax.all_to_all(block, axis, 0, 0, tiled=True)  43.1 us
    all_to_all x6, starting transfers between devices, swap(): return lax.all_to_all(block, axis, 0, 0, tiled=True)  35.9 us
    all_to_all x6, waiting for transfers between devices, swap(): return lax.all_to_all(block, axis, 0, 0, tiled=True)  10.7 us
    pallas_call x5, Pallas kernels, small_call(): pl.pallas_call(kernel, out_shape=[jax.ShapeDtypeStruct(s, d) for s, d, _...  9.82 us
  transfers between devices with their start and end apart: 6, of which 3 were waited for; matrix products, arithmetic and copies ran while one was open for 0% of the time, Pallas kernels for 32%

profile of v6, /device:TPU:1, one launch (start us, length us, event | category | flops | bytes accessed | tf_op | source)
XLA Modules:
  0.0 151.8 jit_solution(5708172979167964456)
XLA Ops:
  0.6 3.3 %shard_map.122 = (f32[16,160,128]{2,1,0:T(8,128)}, s32[16]{0:T(128)}, s32[16]{0:T(128)}, s32[16]{0:T(128)}, s32[16]{0:T(128)}, /*index=5*/f32[2]{0:T(128)}) custom-call(s32[8,16]{1,0:T(8,128)} %owner_map.1, s32[128]{0:T(128)} %row_tops.1, s32[2]{0:T(128)} %restart.1, f32[101]{0:T(128)} %constant.12.clone.table, s32[1,32]{1,0:T(1,128)} %cols.1, ...), custom_call_target="tpu_custom_call" | custom-call | tf_op jit(solution)/shard_map/pallas_call | solution.py:229
  4.0 27.7 %all_to_all.41.got.amp = f32[16,160,128]{2,1,0:T(8,128)} all-to-all(f32[16,160,128]{2,1,0:T(8,128)} %get-tuple-element.32), channel_id=1, replica_groups=mesh['ty'=8,'tx'=16] {'tx'}, dimensions={0} | all-to-all | bytes 2621440 | tf_op jit(solution)/shard_map/all_to_all | solution.py:319
  31.6 3.3 %shard_map.123 = (f32[16,160,128]{2,1,0:T(8,128)}, s32[16]{0:T(128)}, s32[16]{0:T(128)}) custom-call(s32[16]{0:T(128)} %get-tuple-element.30.right, s32[16]{0:T(128)} %get-tuple-element.31.inv, f32[16,160,128]{2,1,0:T(8,128)} %all_to_all.41.got.amp, f32[32,128,128]{2,1,0:T(8,128)} %bitcast.5), custom_call_target="tpu_custom_call" | custom-call | tf_op jit(solution)/shard_map/pallas_call | solution.py:229
  35.0 3.7 %all-to-all-start.1 = ((f32[16,160,128]{2,1,0:T(8,128)}), f32[16,160,128]{2,1,0:T(8,128)S(1)}, u32[]{:S(2)}, u32[]{:S(2)}) async-start(f32[16,160,128]{2,1,0:T(8,128)} %get-tuple-element.38), calls=%async_computation.1 | async-start | bytes 2621440 | tf_op jit(solution)/shard_map/all_to_all | solution.py:319
  38.7 10.7 %shard_map.124 = (f32[2,2,256,128]{3,2,1,0:T(8,128)}, f32[2,256,128]{2,1,0:T(8,128)}, f32[2,256,128]{2,1,0:T(8,128)}, f32[2,256,128]{2,1,0:T(8,128)}, f32[8,128]{1,0:T(8,128)}) custom-call(s32[16]{0:T(128)} %get-tuple-element.29.rows, s32[16]{0:T(128)} %get-tuple-element.35.offs, f32[2]{0:T(128)} %get-tuple-element.34.beta, f32[2,256,256]{2,1,0:T(8,128)} %obj.5, ...), custom_call_target="tpu_custom_call" | custom-call | flops 6400000000 | bytes 4194304 | tf_op jit(solution)/shard_map/pallas_call | solution.py:216
  49.4 7.2 %all-to-all-done.1.halo.amp = f32[16,160,128]{2,1,0:T(8,128)S(1)} async-done(((f32[16,160,128]{2,1,0:T(8,128)}), f32[16,160,128]{2,1,0:T(8,128)S(1)}, u32[]{:S(2)}, u32[]{:S(2)}) %all-to-all-start.1) | async-done | bytes 1310752 | tf_op jit(solution)/shard_map/all_to_all | solution.py:319
  56.6 4.7 %all-to-all-start.2 = ((f32[16,32,128]{2,1,0:T(8,128)}), f32[16,32,128]{2,1,0:T(8,128)S(1)}, u32[]{:S(2)}, u32[]{:S(2)}) async-start(f32[16,32,128]{2,1,0:T(8,128)} %bitcast.6), calls=%async_computation.2 | async-start | bytes 524288 | tf_op jit(solution)/shard_map/all_to_all | solution.py:319
  61.3 10.5 %shard_map.125 = (f32[2,256,128]{2,1,0:T(8,128)}, f32[2,256,128]{2,1,0:T(8,128)}, f32[8,128]{1,0:T(8,128)}) custom-call(s32[16]{0:T(128)} %get-tuple-element.29.rows, s32[16]{0:T(128)} %get-tuple-element.33.offs, f32[2,2,256,128]{3,2,1,0:T(8,128)} %get-tuple-element.36.z0, f32[16,160,128]{2,1,0:T(8,128)} %copy-done.6, f32[2,2,128,128]{3,2,1,0:T(8,128)} %probe.9, ...), custom_call_target="tpu_custom_call" | custom-call | flops 6400000000 | bytes 4194304 | tf_op jit(solution)/shard_map/pallas_call | solution.py:216
  71.8 0.9 copy-done.1
  72.7 0.6 shard_map.126
  73.3 15.4 %all_to_all.42.ahead.got = f32[16,64,128]{2,1,0:T(8,128)S(1)} all-to-all(f32[16,64,128]{2,1,0:T(8,128)S(1)} %shard_map.126), channel_id=1, replica_groups=mesh['ty'=8,'tx'=16] {'tx'}, dimensions={0} | all-to-all | bytes 1048576 | tf_op jit(solution)/shard_map/all_to_all | solution.py:319
  88.8 1.3 shard_map.128
  90.1 3.7 %all-to-all-start.5 = ((f32[16,32,128]{2,1,0:T(8,128)}), f32[16,32,128]{2,1,0:T(8,128)S(1)}, u32[]{:S(2)}, u32[]{:S(2)}) async-start(f32[16,32,128]{2,1,0:T(8,128)} %shard_map.128), calls=%async_computation.5 | async-start | bytes 524288 | tf_op jit(solution)/shard_map/all_to_all | solution.py:319
  93.8 10.9 %shard_map.127 = (f32[2,256,128]{2,1,0:T(8,128)}, f32[2,256,128]{2,1,0:T(8,128)}, f32[2,256,128]{2,1,0:T(8,128)}, f32[8,128]{1,0:T(8,128)}) custom-call(s32[16]{0:T(128)} %get-tuple-element.29.rows, s32[16]{0:T(128)} %get-tuple-element.33.offs, f32[2]{0:T(128)} %get-tuple-element.34.beta, f32[2,2,256,128]{3,2,1,0:T(8,128)} %get-tuple-element.36.z0, ...), custom_call_target="tpu_custom_call" | custom-call | flops 6400000000 | bytes 4194304 | tf_op jit(solution)/shard_map/pallas_call | solution.py:216
  104.8 6.4 %all-to-all-start.4 = ((f32[16,32,128]{2,1,0:T(8,128)}), f32[16,32,128]{2,1,0:T(8,128)S(1)}, u32[]{:S(2)}, u32[]{:S(2)}) async-start(f32[16,32,128]{2,1,0:T(8,128)} %bitcast.7), calls=%async_computation.4 | async-start | bytes 524288 | tf_op jit(solution)/shard_map/all_to_all | solution.py:319
  111.2 7.5 %shard_map.129 = (f32[2,256,128]{2,1,0:T(8,128)}, f32[32,128]{1,0:T(8,128)}, bf16[4096,256]{1,0:T(8,128)(2,1)}, bf16[4096,256]{1,0:T(8,128)(2,1)}) custom-call(s32[16]{0:T(128)} %get-tuple-element.29.rows, s32[16]{0:T(128)} %get-tuple-element.35.offs, f32[2]{0:T(128)} %get-tuple-element.34.beta, f32[2,256,128]{2,1,0:T(8,128)} %get-tuple-element.41.ahead, ...), custom_call_target="tpu_custom_call" | custom-call | flops 3200000000 | bytes 4194304 | tf_op jit(solution)/shard_map/pallas_call | solution.py:216
  118.8 0.7 copy-done.2
  119.5 1.3 shard_map.130
  120.7 6.7 %all-to-all-start.6 = ((f32[16,32,128]{2,1,0:T(8,128)}), f32[16,32,128]{2,1,0:T(8,128)S(1)}, u32[]{:S(2)}, u32[]{:S(2)}) async-start(f32[16,32,128]{2,1,0:T(8,128)} %shard_map.130), calls=%async_computation.6 | async-start | bytes 524288 | tf_op jit(solution)/shard_map/all_to_all | solution.py:319
  127.4 6.9 %shard_map.131.tile = f32[2,256,256]{2,1,0:T(8,128)} custom-call(s32[16]{0:T(128)} %get-tuple-element.29.rows, s32[16]{0:T(128)} %get-tuple-element.35.offs, f32[2,256,128]{2,1,0:T(8,128)} %get-tuple-element.48.start, f32[2,256,128]{2,1,0:T(8,128)} %get-tuple-element.43.mid, f32[2,256,128]{2,1,0:T(8,128)} %get-tuple-element.49.odd_low, ...), custom_call_target="tpu_custom_call" | custom-call | flops 3200000000 | bytes 4194304 | tf_op jit(solution)/shard_map/pallas_call | solution.py:216
  134.3 0.7 all-to-all-done.6.got
  135.9 10.7 %all-to-all-start.7 = ((f32[8,1,128]{2,1,0:T(1,128)}), f32[8,1,128]{2,1,0:T(1,128)S(1)}, u32[]{:S(2)}, u32[]{:S(2)}) async-start(f32[8,1,128]{2,1,0:T(1,128)} %broadcast_in_dim.6), calls=%async_computation.7 | async-start | bytes 8192 | tf_op jit(solution)/shard_map/all_to_all | solution.py:319
  146.6 1.8 %shard_map.132 = f32[2,256,256]{2,1,0:T(8,128)} custom-call(f32[2,256,256]{2,1,0:T(8,128)} %shard_map.131.tile, f32[16,32,128]{2,1,0:T(8,128)} %copy-done.5), custom_call_target="tpu_custom_call", output_to_operand_aliasing={{}: (0, {})} | custom-call | tf_op jit(solution)/shard_map/pallas_call | solution.py:397
  148.4 2.8 %all-to-all-done.7 = f32[8,1,128]{2,1,0:T(1,128)S(1)} async-done(((f32[8,1,128]{2,1,0:T(1,128)}), f32[8,1,128]{2,1,0:T(1,128)S(1)}, u32[]{:S(2)}, u32[]{:S(2)}) %all-to-all-start.7) | async-done | bytes 4128 | tf_op jit(solution)/shard_map/all_to_all | solution.py:319
  (24 shorter events, 1.6 us)
Async XLA Ops:
  35.0 21.6 %all-to-all-start.1 = ((f32[16,160,128]{2,1,0:T(8,128)}), f32[16,160,128]{2,1,0:T(8,128)S(1)}, u32[]{:S(2)}, u32[]{:S(2)}) async-start(f32[16,160,128]{2,1,0:T(8,128)} %get-tuple-element.38), calls=%async_computation.1 | async-start | bytes 2621440 | tf_op jit(solution)/shard_map/all_to_all | solution.py:319
  56.6 4.7 %copy-start.6 = (f32[16,160,128]{2,1,0:T(8,128)}, f32[16,160,128]{2,1,0:T(8,128)S(1)}, u32[]{:S(2)}) copy-start(f32[16,160,128]{2,1,0:T(8,128)S(1)} %all-to-all-done.1.halo.amp) | copy-start | bytes 3932164
  56.6 15.2 %all-to-all-start.2 = ((f32[16,32,128]{2,1,0:T(8,128)}), f32[16,32,128]{2,1,0:T(8,128)S(1)}, u32[]{:S(2)}, u32[]{:S(2)}) async-start(f32[16,32,128]{2,1,0:T(8,128)} %bitcast.6), calls=%async_computation.2 | async-start | bytes 524288 | tf_op jit(solution)/shard_map/all_to_all | solution.py:319
  61.3 10.5 %copy-start.3 = (s32[16]{0:T(128)S(1)}, s32[16]{0:T(128)}, u32[]{:S(2)}) copy-start(s32[16]{0:T(128)} %get-tuple-element.30.right) | copy-start | bytes 196
  71.8 17.0 %copy-start.4 = (s32[16]{0:T(128)S(1)}, s32[16]{0:T(128)}, u32[]{:S(2)}) copy-start(s32[16]{0:T(128)} %get-tuple-element.28.left) | copy-start | bytes 196
  71.8 1.0 copy-start.1
  88.8 5.0 %copy-start = (f32[16,64,128]{2,1,0:T(8,128)}, f32[16,64,128]{2,1,0:T(8,128)S(1)}, u32[]{:S(2)}) copy-start(f32[16,64,128]{2,1,0:T(8,128)S(1)} %all_to_all.42.ahead.got) | copy-start | bytes 1572868
  90.1 14.7 %all-to-all-start.5 = ((f32[16,32,128]{2,1,0:T(8,128)}), f32[16,32,128]{2,1,0:T(8,128)S(1)}, u32[]{:S(2)}, u32[]{:S(2)}) async-start(f32[16,32,128]{2,1,0:T(8,128)} %shard_map.128), calls=%async_computation.5 | async-start | bytes 524288 | tf_op jit(solution)/shard_map/all_to_all | solution.py:319
  104.7 6.4 %copy-start.7 = (f32[16,32,128]{2,1,0:T(8,128)}, f32[16,32,128]{2,1,0:T(8,128)S(1)}, u32[]{:S(2)}) copy-start(f32[16,32,128]{2,1,0:T(8,128)S(1)} %all-to-all-done.5.from_left) | copy-start | bytes 786436
  104.8 14.0 %all-to-all-start.4 = ((f32[16,32,128]{2,1,0:T(8,128)}), f32[16,32,128]{2,1,0:T(8,128)S(1)}, u32[]{:S(2)}, u32[]{:S(2)}) async-start(f32[16,32,128]{2,1,0:T(8,128)} %bitcast.7), calls=%async_computation.4 | async-start | bytes 524288 | tf_op jit(solution)/shard_map/all_to_all | solution.py:319
  118.7 0.7 copy-start.2
  120.7 14.2 %all-to-all-start.6 = ((f32[16,32,128]{2,1,0:T(8,128)}), f32[16,32,128]{2,1,0:T(8,128)S(1)}, u32[]{:S(2)}, u32[]{:S(2)}) async-start(f32[16,32,128]{2,1,0:T(8,128)} %shard_map.130), calls=%async_computation.6 | async-start | bytes 524288 | tf_op jit(solution)/shard_map/all_to_all | solution.py:319
  135.0 11.7 %copy-start.5 = (f32[16,32,128]{2,1,0:T(8,128)}, f32[16,32,128]{2,1,0:T(8,128)S(1)}, u32[]{:S(2)}) copy-start(f32[16,32,128]{2,1,0:T(8,128)S(1)} %all-to-all-done.6.got) | copy-start | bytes 786436
  135.9 15.3 %all-to-all-start.7 = ((f32[8,1,128]{2,1,0:T(1,128)}), f32[8,1,128]{2,1,0:T(1,128)S(1)}, u32[]{:S(2)}, u32[]{:S(2)}) async-start(f32[8,1,128]{2,1,0:T(1,128)} %broadcast_in_dim.6), calls=%async_computation.7 | async-start | bytes 8192 | tf_op jit(solution)/shard_map/all_to_all | solution.py:319

commit v7 on v6

--- a/solution.py
+++ b/solution.py
@@ -272,14 +272,15 @@
         c.wait()
 
 
-def pass_halo(right, inv, got, amp, send, off_even, off_odd, places, sems):
-    fetch_places = pltpu.make_async_copy(got.at[:, pl.ds(N, 2)], places, sems.at[32])
+def pass_halo(right, inv, got, amp, send, off_even, off_odd, places, edges, sems):
+    fetch_edges = pltpu.make_async_copy(got.at[:, pl.ds(N, 32)], edges, sems.at[16])
+    fetch_places = pltpu.make_async_copy(got.at[:, pl.ds(N, 2)], places, sems.at[17])
+    fetch_edges.start()
     fetch_places.start()
-    copies = start_all(
-        [(amp.at[2 * inv[d] + 1], send.at[d, pl.ds(0, N)]) for d in range(16)]
-        + [(got.at[right[d], pl.ds(N, 32)], send.at[d, pl.ds(N, 32)]) for d in range(16)],
-        sems,
-    )
+    copies = start_all([(amp.at[2 * inv[d] + 1], send.at[d, pl.ds(0, N)]) for d in range(16)], sems)
+    fetch_edges.wait()
+    for d in range(16):
+        send[d, N:] = edges[right[d]]
     fetch_places.wait()
     for r in range(16):
         off_even[r] = places[r, 0, N - 1].astype(jnp.int32)
@@ -344,7 +345,7 @@
     send, off_even, off_odd = small_call(
         pass_halo, small(right, inv) + [(amp_even, ANY), (amplitude, ANY)],
         [((16, N + 32, N), f32, VMEM), ints, ints],
-        [pltpu.SMEM((16, 2, N), f32), pltpu.SemaphoreType.DMA((33,))], limit=VMEM_BYTES,
+        [pltpu.SMEM((16, 2, N), f32), pltpu.VMEM((16, 32, N), f32), pltpu.SemaphoreType.DMA((18,))], limit=VMEM_BYTES,
     )
     amp_odd = swap(send)
     z0, even_low, even_high, ahead, loss_a = run(

time: 153 us -> 153 us (level)
  no operation moved by 1% of the time
where the time goes in v7:
time: 153 us; the launch traced here: 152 us
  Pallas kernels  57.9 us (38%)
  blocking collectives  43.1 us (28%)
  starting transfers between devices  36 us (24%)
  waiting for transfers between devices  10.7 us (7%)
  local copies, waits for them, and re-layouts  2.47 us (2%)
    pallas_call x5, Pallas kernels, run(): pl.pallas_call(kernel, grid=(steps,), out_shape=out_shape, in_specs=[spec...  46.4 us
    all_to_all x2, blocking collectives, swap(): return lax.all_to_all(block, axis, 0, 0, tiled=True)  43.1 us
    all_to_all x6, starting transfers between devices, swap(): return lax.all_to_all(block, axis, 0, 0, tiled=True)  36 us
    all_to_all x6, waiting for transfers between devices, swap(): return lax.all_to_all(block, axis, 0, 0, tiled=True)  10.7 us
    pallas_call x5, Pallas kernels, small_call(): pl.pallas_call(kernel, out_shape=[jax.ShapeDtypeStruct(s, d) for s, d, _...  9.68 us
  transfers between devices with their start and end apart: 6, of which 3 were waited for; matrix products, arithmetic and copies ran while one was open for 0% of the time, Pallas kernels for 32%

profile of v7, /device:TPU:1, one launch (start us, length us, event | category | flops | bytes accessed | tf_op | source)
XLA Modules:
  0.0 151.7 jit_solution(17186975376435685662)
XLA Ops:
  0.6 3.3 %shard_map.122 = (f32[16,160,128]{2,1,0:T(8,128)}, s32[16]{0:T(128)}, s32[16]{0:T(128)}, s32[16]{0:T(128)}, s32[16]{0:T(128)}, /*index=5*/f32[2]{0:T(128)}) custom-call(s32[8,16]{1,0:T(8,128)} %owner_map.1, s32[128]{0:T(128)} %row_tops.1, s32[2]{0:T(128)} %restart.1, f32[101]{0:T(128)} %constant.12.clone.table, s32[1,32]{1,0:T(1,128)} %cols.1, ...), custom_call_target="tpu_custom_call" | custom-call | tf_op jit(solution)/shard_map/pallas_call | solution.py:229
  4.0 27.7 %all_to_all.41.got.amp = f32[16,160,128]{2,1,0:T(8,128)} all-to-all(f32[16,160,128]{2,1,0:T(8,128)} %get-tuple-element.32), channel_id=1, replica_groups=mesh['ty'=8,'tx'=16] {'tx'}, dimensions={0} | all-to-all | bytes 2621440 | tf_op jit(solution)/shard_map/all_to_all | solution.py:320
  31.6 3.2 %shard_map.123 = (f32[16,160,128]{2,1,0:T(8,128)}, s32[16]{0:T(128)}, s32[16]{0:T(128)}) custom-call(s32[16]{0:T(128)} %get-tuple-element.30.right, s32[16]{0:T(128)} %get-tuple-element.31.inv, f32[16,160,128]{2,1,0:T(8,128)} %all_to_all.41.got.amp, f32[32,128,128]{2,1,0:T(8,128)} %bitcast.5), custom_call_target="tpu_custom_call" | custom-call | tf_op jit(solution)/shard_map/pallas_call | solution.py:229
  34.8 3.7 %all-to-all-start.1 = ((f32[16,160,128]{2,1,0:T(8,128)}), f32[16,160,128]{2,1,0:T(8,128)S(1)}, u32[]{:S(2)}, u32[]{:S(2)}) async-start(f32[16,160,128]{2,1,0:T(8,128)} %get-tuple-element.38), calls=%async_computation.1 | async-start | bytes 2621440 | tf_op jit(solution)/shard_map/all_to_all | solution.py:320
  38.5 10.7 %shard_map.124 = (f32[2,2,256,128]{3,2,1,0:T(8,128)}, f32[2,256,128]{2,1,0:T(8,128)}, f32[2,256,128]{2,1,0:T(8,128)}, f32[2,256,128]{2,1,0:T(8,128)}, f32[8,128]{1,0:T(8,128)}) custom-call(s32[16]{0:T(128)} %get-tuple-element.29.rows, s32[16]{0:T(128)} %get-tuple-element.35.offs, f32[2]{0:T(128)} %get-tuple-element.34.beta, f32[2,256,256]{2,1,0:T(8,128)} %obj.5, ...), custom_call_target="tpu_custom_call" | custom-call | flops 6400000000 | bytes 4194304 | tf_op jit(solution)/shard_map/pallas_call | solution.py:216
  49.2 7.2 %all-to-all-done.1.halo.amp = f32[16,160,128]{2,1,0:T(8,128)S(1)} async-done(((f32[16,160,128]{2,1,0:T(8,128)}), f32[16,160,128]{2,1,0:T(8,128)S(1)}, u32[]{:S(2)}, u32[]{:S(2)}) %all-to-all-start.1) | async-done | bytes 1310752 | tf_op jit(solution)/shard_map/all_to_all | solution.py:320
  56.5 4.7 %all-to-all-start.2 = ((f32[16,32,128]{2,1,0:T(8,128)}), f32[16,32,128]{2,1,0:T(8,128)S(1)}, u32[]{:S(2)}, u32[]{:S(2)}) async-start(f32[16,32,128]{2,1,0:T(8,128)} %bitcast.6), calls=%async_computation.2 | async-start | bytes 524288 | tf_op jit(solution)/shard_map/all_to_all | solution.py:320
  61.1 10.4 %shard_map.125 = (f32[2,256,128]{2,1,0:T(8,128)}, f32[2,256,128]{2,1,0:T(8,128)}, f32[8,128]{1,0:T(8,128)}) custom-call(s32[16]{0:T(128)} %get-tuple-element.29.rows, s32[16]{0:T(128)} %get-tuple-element.33.offs, f32[2,2,256,128]{3,2,1,0:T(8,128)} %get-tuple-element.36.z0, f32[16,160,128]{2,1,0:T(8,128)} %copy-done.6, f32[2,2,128,128]{3,2,1,0:T(8,128)} %probe.9, ...), custom_call_target="tpu_custom_call" | custom-call | flops 6400000000 | bytes 4194304 | tf_op jit(solution)/shard_map/pallas_call | solution.py:216
  71.6 0.9 copy-done.1
  72.6 0.6 shard_map.126
  73.2 15.4 %all_to_all.42.ahead.got = f32[16,64,128]{2,1,0:T(8,128)S(1)} all-to-all(f32[16,64,128]{2,1,0:T(8,128)S(1)} %shard_map.126), channel_id=1, replica_groups=mesh['ty'=8,'tx'=16] {'tx'}, dimensions={0} | all-to-all | bytes 1048576 | tf_op jit(solution)/shard_map/all_to_all | solution.py:320
  88.6 1.3 shard_map.128
  89.9 3.7 %all-to-all-start.5 = ((f32[16,32,128]{2,1,0:T(8,128)}), f32[16,32,128]{2,1,0:T(8,128)S(1)}, u32[]{:S(2)}, u32[]{:S(2)}) async-start(f32[16,32,128]{2,1,0:T(8,128)} %shard_map.128), calls=%async_computation.5 | async-start | bytes 524288 | tf_op jit(solution)/shard_map/all_to_all | solution.py:320
  93.6 10.9 %shard_map.127 = (f32[2,256,128]{2,1,0:T(8,128)}, f32[2,256,128]{2,1,0:T(8,128)}, f32[2,256,128]{2,1,0:T(8,128)}, f32[8,128]{1,0:T(8,128)}) custom-call(s32[16]{0:T(128)} %get-tuple-element.29.rows, s32[16]{0:T(128)} %get-tuple-element.33.offs, f32[2]{0:T(128)} %get-tuple-element.34.beta, f32[2,2,256,128]{3,2,1,0:T(8,128)} %get-tuple-element.36.z0, ...), custom_call_target="tpu_custom_call" | custom-call | flops 6400000000 | bytes 4194304 | tf_op jit(solution)/shard_map/pallas_call | solution.py:216
  104.5 6.4 %all-to-all-start.4 = ((f32[16,32,128]{2,1,0:T(8,128)}), f32[16,32,128]{2,1,0:T(8,128)S(1)}, u32[]{:S(2)}, u32[]{:S(2)}) async-start(f32[16,32,128]{2,1,0:T(8,128)} %bitcast.7), calls=%async_computation.4 | async-start | bytes 524288 | tf_op jit(solution)/shard_map/all_to_all | solution.py:320
  111.0 7.6 %shard_map.129 = (f32[2,256,128]{2,1,0:T(8,128)}, f32[32,128]{1,0:T(8,128)}, bf16[4096,256]{1,0:T(8,128)(2,1)}, bf16[4096,256]{1,0:T(8,128)(2,1)}) custom-call(s32[16]{0:T(128)} %get-tuple-element.29.rows, s32[16]{0:T(128)} %get-tuple-element.35.offs, f32[2]{0:T(128)} %get-tuple-element.34.beta, f32[2,256,128]{2,1,0:T(8,128)} %get-tuple-element.41.ahead, ...), custom_call_target="tpu_custom_call" | custom-call | flops 3200000000 | bytes 4194304 | tf_op jit(solution)/shard_map/pallas_call | solution.py:216
  118.6 0.7 copy-done.2
  119.3 1.3 shard_map.130
  120.6 6.7 %all-to-all-start.6 = ((f32[16,32,128]{2,1,0:T(8,128)}), f32[16,32,128]{2,1,0:T(8,128)S(1)}, u32[]{:S(2)}, u32[]{:S(2)}) async-start(f32[16,32,128]{2,1,0:T(8,128)} %shard_map.130), calls=%async_computation.6 | async-start | bytes 524288 | tf_op jit(solution)/shard_map/all_to_all | solution.py:320
  127.2 6.9 %shard_map.131.tile = f32[2,256,256]{2,1,0:T(8,128)} custom-call(s32[16]{0:T(128)} %get-tuple-element.29.rows, s32[16]{0:T(128)} %get-tuple-element.35.offs, f32[2,256,128]{2,1,0:T(8,128)} %get-tuple-element.48.start, f32[2,256,128]{2,1,0:T(8,128)} %get-tuple-element.43.mid, f32[2,256,128]{2,1,0:T(8,128)} %get-tuple-element.49.odd_low, ...), custom_call_target="tpu_custom_call" | custom-call | flops 3200000000 | bytes 4194304 | tf_op jit(solution)/shard_map/pallas_call | solution.py:216
  134.1 0.7 all-to-all-done.6.got
  135.7 10.8 %all-to-all-start.7 = ((f32[8,1,128]{2,1,0:T(1,128)}), f32[8,1,128]{2,1,0:T(1,128)S(1)}, u32[]{:S(2)}, u32[]{:S(2)}) async-start(f32[8,1,128]{2,1,0:T(1,128)} %broadcast_in_dim.6), calls=%async_computation.7 | async-start | bytes 8192 | tf_op jit(solution)/shard_map/all_to_all | solution.py:320
  146.5 1.8 %shard_map.132 = f32[2,256,256]{2,1,0:T(8,128)} custom-call(f32[2,256,256]{2,1,0:T(8,128)} %shard_map.131.tile, f32[16,32,128]{2,1,0:T(8,128)} %copy-done.5), custom_call_target="tpu_custom_call", output_to_operand_aliasing={{}: (0, {})} | custom-call | tf_op jit(solution)/shard_map/pallas_call | solution.py:398
  148.3 2.8 %all-to-all-done.7 = f32[8,1,128]{2,1,0:T(1,128)S(1)} async-done(((f32[8,1,128]{2,1,0:T(1,128)}), f32[8,1,128]{2,1,0:T(1,128)S(1)}, u32[]{:S(2)}, u32[]{:S(2)}) %all-to-all-start.7) | async-done | bytes 4128 | tf_op jit(solution)/shard_map/all_to_all | solution.py:320
  (24 shorter events, 1.6 us)
Async XLA Ops:
  34.8 21.6 %all-to-all-start.1 = ((f32[16,160,128]{2,1,0:T(8,128)}), f32[16,160,128]{2,1,0:T(8,128)S(1)}, u32[]{:S(2)}, u32[]{:S(2)}) async-start(f32[16,160,128]{2,1,0:T(8,128)} %get-tuple-element.38), calls=%async_computation.1 | async-start | bytes 2621440 | tf_op jit(solution)/shard_map/all_to_all | solution.py:320
  56.4 4.7 %copy-start.6 = (f32[16,160,128]{2,1,0:T(8,128)}, f32[16,160,128]{2,1,0:T(8,128)S(1)}, u32[]{:S(2)}) copy-start(f32[16,160,128]{2,1,0:T(8,128)S(1)} %all-to-all-done.1.halo.amp) | copy-start | bytes 3932164
  56.5 15.1 %all-to-all-start.2 = ((f32[16,32,128]{2,1,0:T(8,128)}), f32[16,32,128]{2,1,0:T(8,128)S(1)}, u32[]{:S(2)}, u32[]{:S(2)}) async-start(f32[16,32,128]{2,1,0:T(8,128)} %bitcast.6), calls=%async_computation.2 | async-start | bytes 524288 | tf_op jit(solution)/shard_map/all_to_all | solution.py:320
  61.1 10.5 %copy-start.3 = (s32[16]{0:T(128)S(1)}, s32[16]{0:T(128)}, u32[]{:S(2)}) copy-start(s32[16]{0:T(128)} %get-tuple-element.30.right) | copy-start | bytes 196
  71.6 17.0 %copy-start.4 = (s32[16]{0:T(128)S(1)}, s32[16]{0:T(128)}, u32[]{:S(2)}) copy-start(s32[16]{0:T(128)} %get-tuple-element.28.left) | copy-start | bytes 196
  71.6 1.0 copy-start.1
  88.6 5.0 %copy-start = (f32[16,64,128]{2,1,0:T(8,128)}, f32[16,64,128]{2,1,0:T(8,128)S(1)}, u32[]{:S(2)}) copy-start(f32[16,64,128]{2,1,0:T(8,128)S(1)} %all_to_all.42.ahead.got) | copy-start | bytes 1572868
  89.9 14.6 %all-to-all-start.5 = ((f32[16,32,128]{2,1,0:T(8,128)}), f32[16,32,128]{2,1,0:T(8,128)S(1)}, u32[]{:S(2)}, u32[]{:S(2)}) async-start(f32[16,32,128]{2,1,0:T(8,128)} %shard_map.128), calls=%async_computation.5 | async-start | bytes 524288 | tf_op jit(solution)/shard_map/all_to_all | solution.py:320
  104.5 6.4 %copy-start.7 = (f32[16,32,128]{2,1,0:T(8,128)}, f32[16,32,128]{2,1,0:T(8,128)S(1)}, u32[]{:S(2)}) copy-start(f32[16,32,128]{2,1,0:T(8,128)S(1)} %all-to-all-done.5.from_left) | copy-start | bytes 786436
  104.5 14.0 %all-to-all-start.4 = ((f32[16,32,128]{2,1,0:T(8,128)}), f32[16,32,128]{2,1,0:T(8,128)S(1)}, u32[]{:S(2)}, u32[]{:S(2)}) async-start(f32[16,32,128]{2,1,0:T(8,128)} %bitcast.7), calls=%async_computation.4 | async-start | bytes 524288 | tf_op jit(solution)/shard_map/all_to_all | solution.py:320
  118.5 0.7 copy-start.2
  120.6 14.2 %all-to-all-start.6 = ((f32[16,32,128]{2,1,0:T(8,128)}), f32[16,32,128]{2,1,0:T(8,128)S(1)}, u32[]{:S(2)}, u32[]{:S(2)}) async-start(f32[16,32,128]{2,1,0:T(8,128)} %shard_map.130), calls=%async_computation.6 | async-start | bytes 524288 | tf_op jit(solution)/shard_map/all_to_all | solution.py:320
  134.8 11.8 %copy-start.5 = (f32[16,32,128]{2,1,0:T(8,128)}, f32[16,32,128]{2,1,0:T(8,128)S(1)}, u32[]{:S(2)}) copy-start(f32[16,32,128]{2,1,0:T(8,128)S(1)} %all-to-all-done.6.got) | copy-start | bytes 786436
  135.7 15.4 %all-to-all-start.7 = ((f32[8,1,128]{2,1,0:T(1,128)}), f32[8,1,128]{2,1,0:T(1,128)S(1)}, u32[]{:S(2)}, u32[]{:S(2)}) async-start(f32[8,1,128]{2,1,0:T(1,128)} %broadcast_in_dim.6), calls=%async_computation.7 | async-start | bytes 8192 | tf_op jit(solution)/shard_map/all_to_all | solution.py:320

commit v8 on v7

--- a/solution.py
+++ b/solution.py
@@ -246,15 +246,16 @@
 def prepare(
     owner_map, row_tops, restart, table, cols, obj, prev, amp, send, rows, inv, right, left, beta, now, before, sems
 ):
-    edges = start_all([(obj.at[:, :, pl.ds(0, N)], now), (prev.at[:, :, pl.ds(0, N)], before)], sems.at[pl.ds(16, 2)])
     band = lax.axis_index("ty")
     for c in range(16):
+        inv[owner_map[band, c]] = c
+    copies = start_all([(amp.at[2 * inv[d]], send.at[d, pl.ds(0, N)]) for d in range(16)], sems)
+    edges = start_all([(obj.at[:, :, pl.ds(0, N)], now), (prev.at[:, :, pl.ds(0, N)], before)], sems.at[pl.ds(16, 2)])
+    for c in range(16):
         owner = owner_map[band, c]
-        inv[owner] = c
         right[owner] = owner_map[band, (c + 1) % 16]
         left[owner] = owner_map[band, (c + 15) % 16]
         rows[c] = row_tops[band * 16 + c]
-    copies = start_all([(amp.at[2 * inv[d]], send.at[d, pl.ds(0, N)]) for d in range(16)], sems)
     for k in range(2):
         beta[k] = (table[restart[k] - 1] - 1.0) / table[restart[k]]
     for c in edges:
@@ -273,11 +274,11 @@
 
 
 def pass_halo(right, inv, got, amp, send, off_even, off_odd, places, edges, sems):
+    copies = start_all([(amp.at[2 * inv[d] + 1], send.at[d, pl.ds(0, N)]) for d in range(16)], sems)
     fetch_edges = pltpu.make_async_copy(got.at[:, pl.ds(N, 32)], edges, sems.at[16])
     fetch_places = pltpu.make_async_copy(got.at[:, pl.ds(N, 2)], places, sems.at[17])
     fetch_edges.start()
     fetch_places.start()
-    copies = start_all([(amp.at[2 * inv[d] + 1], send.at[d, pl.ds(0, N)]) for d in range(16)], sems)
     fetch_edges.wait()
     for d in range(16):
         send[d, N:] = edges[right[d]]

time: 153 us -> 153 us (level)
  no operation moved by 1% of the time
where the time goes in v8:
time: 153 us; the launch traced here: 152 us
  Pallas kernels  58.5 us (38%)
  blocking collectives  43.1 us (28%)
  starting transfers between devices  36 us (24%)
  waiting for transfers between devices  10.7 us (7%)
  local copies, waits for them, and re-layouts  2.47 us (2%)
    pallas_call x5, Pallas kernels, run(): pl.pallas_call(kernel, grid=(steps,), out_shape=out_shape, in_specs=[spec...  46.5 us
    all_to_all x2, blocking collectives, swap(): return lax.all_to_all(block, axis, 0, 0, tiled=True)  43.1 us
    all_to_all x6, starting transfers between devices, swap(): return lax.all_to_all(block, axis, 0, 0, tiled=True)  36 us
    all_to_all x6, waiting for transfers between devices, swap(): return lax.all_to_all(block, axis, 0, 0, tiled=True)  10.7 us
    pallas_call x5, Pallas kernels, small_call(): pl.pallas_call(kernel, out_shape=[jax.ShapeDtypeStruct(s, d) for s, d, _...  10.2 us
  transfers between devices with their start and end apart: 6, of which 3 were waited for; matrix products, arithmetic and copies ran while one was open for 0% of the time, Pallas kernels for 32%

profile of v8, /device:TPU:1, one launch (start us, length us, event | category | flops | bytes accessed | tf_op | source)
XLA Modules:
  0.0 152.4 jit_solution(9376675047766743360)
XLA Ops:
  0.6 3.6 %shard_map.122 = (f32[16,160,128]{2,1,0:T(8,128)}, s32[16]{0:T(128)}, s32[16]{0:T(128)}, s32[16]{0:T(128)}, s32[16]{0:T(128)}, /*index=5*/f32[2]{0:T(128)}) custom-call(s32[8,16]{1,0:T(8,128)} %owner_map.1, s32[128]{0:T(128)} %row_tops.1, s32[2]{0:T(128)} %restart.1, f32[101]{0:T(128)} %constant.12.clone.table, s32[1,32]{1,0:T(1,128)} %cols.1, ...), custom_call_target="tpu_custom_call" | custom-call | tf_op jit(solution)/shard_map/pallas_call | solution.py:229
  4.3 27.7 %all_to_all.41.got.amp = f32[16,160,128]{2,1,0:T(8,128)} all-to-all(f32[16,160,128]{2,1,0:T(8,128)} %get-tuple-element.32), channel_id=1, replica_groups=mesh['ty'=8,'tx'=16] {'tx'}, dimensions={0} | all-to-all | bytes 2621440 | tf_op jit(solution)/shard_map/all_to_all | solution.py:321
  31.9 3.4 %shard_map.123 = (f32[16,160,128]{2,1,0:T(8,128)}, s32[16]{0:T(128)}, s32[16]{0:T(128)}) custom-call(s32[16]{0:T(128)} %get-tuple-element.30.right, s32[16]{0:T(128)} %get-tuple-element.31.inv, f32[16,160,128]{2,1,0:T(8,128)} %all_to_all.41.got.amp, f32[32,128,128]{2,1,0:T(8,128)} %bitcast.5), custom_call_target="tpu_custom_call" | custom-call | tf_op jit(solution)/shard_map/pallas_call | solution.py:229
  35.4 3.7 %all-to-all-start.1 = ((f32[16,160,128]{2,1,0:T(8,128)}), f32[16,160,128]{2,1,0:T(8,128)S(1)}, u32[]{:S(2)}, u32[]{:S(2)}) async-start(f32[16,160,128]{2,1,0:T(8,128)} %get-tuple-element.38), calls=%async_computation.1 | async-start | bytes 2621440 | tf_op jit(solution)/shard_map/all_to_all | solution.py:321
  39.1 10.7 %shard_map.124 = (f32[2,2,256,128]{3,2,1,0:T(8,128)}, f32[2,256,128]{2,1,0:T(8,128)}, f32[2,256,128]{2,1,0:T(8,128)}, f32[2,256,128]{2,1,0:T(8,128)}, f32[8,128]{1,0:T(8,128)}) custom-call(s32[16]{0:T(128)} %get-tuple-element.29.rows, s32[16]{0:T(128)} %get-tuple-element.35.offs, f32[2]{0:T(128)} %get-tuple-element.34.beta, f32[2,256,256]{2,1,0:T(8,128)} %obj.5, ...), custom_call_target="tpu_custom_call" | custom-call | flops 6400000000 | bytes 4194304 | tf_op jit(solution)/shard_map/pallas_call | solution.py:216
  49.8 7.2 %all-to-all-done.1.halo.amp = f32[16,160,128]{2,1,0:T(8,128)S(1)} async-done(((f32[16,160,128]{2,1,0:T(8,128)}), f32[16,160,128]{2,1,0:T(8,128)S(1)}, u32[]{:S(2)}, u32[]{:S(2)}) %all-to-all-start.1) | async-done | bytes 1310752 | tf_op jit(solution)/shard_map/all_to_all | solution.py:321
  57.0 4.7 %all-to-all-start.2 = ((f32[16,32,128]{2,1,0:T(8,128)}), f32[16,32,128]{2,1,0:T(8,128)S(1)}, u32[]{:S(2)}, u32[]{:S(2)}) async-start(f32[16,32,128]{2,1,0:T(8,128)} %bitcast.6), calls=%async_computation.2 | async-start | bytes 524288 | tf_op jit(solution)/shard_map/all_to_all | solution.py:321
  61.7 10.5 %shard_map.125 = (f32[2,256,128]{2,1,0:T(8,128)}, f32[2,256,128]{2,1,0:T(8,128)}, f32[8,128]{1,0:T(8,128)}) custom-call(s32[16]{0:T(128)} %get-tuple-element.29.rows, s32[16]{0:T(128)} %get-tuple-element.33.offs, f32[2,2,256,128]{3,2,1,0:T(8,128)} %get-tuple-element.36.z0, f32[16,160,128]{2,1,0:T(8,128)} %copy-done.6, f32[2,2,128,128]{3,2,1,0:T(8,128)} %probe.9, ...), custom_call_target="tpu_custom_call" | custom-call | flops 6400000000 | bytes 4194304 | tf_op jit(solution)/shard_map/pallas_call | solution.py:216
  72.2 0.9 copy-done.1
  73.1 0.6 shard_map.126
  73.7 15.4 %all_to_all.42.ahead.got = f32[16,64,128]{2,1,0:T(8,128)S(1)} all-to-all(f32[16,64,128]{2,1,0:T(8,128)S(1)} %shard_map.126), channel_id=1, replica_groups=mesh['ty'=8,'tx'=16] {'tx'}, dimensions={0} | all-to-all | bytes 1048576 | tf_op jit(solution)/shard_map/all_to_all | solution.py:321
  89.2 1.3 shard_map.128
  90.5 3.7 %all-to-all-start.5 = ((f32[16,32,128]{2,1,0:T(8,128)}), f32[16,32,128]{2,1,0:T(8,128)S(1)}, u32[]{:S(2)}, u32[]{:S(2)}) async-start(f32[16,32,128]{2,1,0:T(8,128)} %shard_map.128), calls=%async_computation.5 | async-start | bytes 524288 | tf_op jit(solution)/shard_map/all_to_all | solution.py:321
  94.2 10.9 %shard_map.127 = (f32[2,256,128]{2,1,0:T(8,128)}, f32[2,256,128]{2,1,0:T(8,128)}, f32[2,256,128]{2,1,0:T(8,128)}, f32[8,128]{1,0:T(8,128)}) custom-call(s32[16]{0:T(128)} %get-tuple-element.29.rows, s32[16]{0:T(128)} %get-tuple-element.33.offs, f32[2]{0:T(128)} %get-tuple-element.34.beta, f32[2,2,256,128]{3,2,1,0:T(8,128)} %get-tuple-element.36.z0, ...), custom_call_target="tpu_custom_call" | custom-call | flops 6400000000 | bytes 4194304 | tf_op jit(solution)/shard_map/pallas_call | solution.py:216
  105.1 6.4 %all-to-all-start.4 = ((f32[16,32,128]{2,1,0:T(8,128)}), f32[16,32,128]{2,1,0:T(8,128)S(1)}, u32[]{:S(2)}, u32[]{:S(2)}) async-start(f32[16,32,128]{2,1,0:T(8,128)} %bitcast.7), calls=%async_computation.4 | async-start | bytes 524288 | tf_op jit(solution)/shard_map/all_to_all | solution.py:321
  111.6 7.6 %shard_map.129 = (f32[2,256,128]{2,1,0:T(8,128)}, f32[32,128]{1,0:T(8,128)}, bf16[4096,256]{1,0:T(8,128)(2,1)}, bf16[4096,256]{1,0:T(8,128)(2,1)}) custom-call(s32[16]{0:T(128)} %get-tuple-element.29.rows, s32[16]{0:T(128)} %get-tuple-element.35.offs, f32[2]{0:T(128)} %get-tuple-element.34.beta, f32[2,256,128]{2,1,0:T(8,128)} %get-tuple-element.41.ahead, ...), custom_call_target="tpu_custom_call" | custom-call | flops 3200000000 | bytes 4194304 | tf_op jit(solution)/shard_map/pallas_call | solution.py:216
  119.2 0.7 copy-done.2
  119.9 1.3 shard_map.130
  121.2 6.7 %all-to-all-start.6 = ((f32[16,32,128]{2,1,0:T(8,128)}), f32[16,32,128]{2,1,0:T(8,128)S(1)}, u32[]{:S(2)}, u32[]{:S(2)}) async-start(f32[16,32,128]{2,1,0:T(8,128)} %shard_map.130), calls=%async_computation.6 | async-start | bytes 524288 | tf_op jit(solution)/shard_map/all_to_all | solution.py:321
  127.8 6.9 %shard_map.131.tile = f32[2,256,256]{2,1,0:T(8,128)} custom-call(s32[16]{0:T(128)} %get-tuple-element.29.rows, s32[16]{0:T(128)} %get-tuple-element.35.offs, f32[2,256,128]{2,1,0:T(8,128)} %get-tuple-element.48.start, f32[2,256,128]{2,1,0:T(8,128)} %get-tuple-element.43.mid, f32[2,256,128]{2,1,0:T(8,128)} %get-tuple-element.49.odd_low, ...), custom_call_target="tpu_custom_call" | custom-call | flops 3200000000 | bytes 4194304 | tf_op jit(solution)/shard_map/pallas_call | solution.py:216
  134.7 0.7 all-to-all-done.6.got
  136.3 10.9 %all-to-all-start.7 = ((f32[8,1,128]{2,1,0:T(1,128)}), f32[8,1,128]{2,1,0:T(1,128)S(1)}, u32[]{:S(2)}, u32[]{:S(2)}) async-start(f32[8,1,128]{2,1,0:T(1,128)} %broadcast_in_dim.6), calls=%async_computation.7 | async-start | bytes 8192 | tf_op jit(solution)/shard_map/all_to_all | solution.py:321
  147.2 1.8 %shard_map.132 = f32[2,256,256]{2,1,0:T(8,128)} custom-call(f32[2,256,256]{2,1,0:T(8,128)} %shard_map.131.tile, f32[16,32,128]{2,1,0:T(8,128)} %copy-done.5), custom_call_target="tpu_custom_call", output_to_operand_aliasing={{}: (0, {})} | custom-call | tf_op jit(solution)/shard_map/pallas_call | solution.py:399
  148.9 2.8 %all-to-all-done.7 = f32[8,1,128]{2,1,0:T(1,128)S(1)} async-done(((f32[8,1,128]{2,1,0:T(1,128)}), f32[8,1,128]{2,1,0:T(1,128)S(1)}, u32[]{:S(2)}, u32[]{:S(2)}) %all-to-all-start.7) | async-done | bytes 4128 | tf_op jit(solution)/shard_map/all_to_all | solution.py:321
  (24 shorter events, 1.6 us)
Async XLA Ops:
  35.4 21.6 %all-to-all-start.1 = ((f32[16,160,128]{2,1,0:T(8,128)}), f32[16,160,128]{2,1,0:T(8,128)S(1)}, u32[]{:S(2)}, u32[]{:S(2)}) async-start(f32[16,160,128]{2,1,0:T(8,128)} %get-tuple-element.38), calls=%async_computation.1 | async-start | bytes 2621440 | tf_op jit(solution)/shard_map/all_to_all | solution.py:321
  57.0 4.7 %copy-start.6 = (f32[16,160,128]{2,1,0:T(8,128)}, f32[16,160,128]{2,1,0:T(8,128)S(1)}, u32[]{:S(2)}) copy-start(f32[16,160,128]{2,1,0:T(8,128)S(1)} %all-to-all-done.1.halo.amp) | copy-start | bytes 3932164
  57.0 15.2 %all-to-all-start.2 = ((f32[16,32,128]{2,1,0:T(8,128)}), f32[16,32,128]{2,1,0:T(8,128)S(1)}, u32[]{:S(2)}, u32[]{:S(2)}) async-start(f32[16,32,128]{2,1,0:T(8,128)} %bitcast.6), calls=%async_computation.2 | async-start | bytes 524288 | tf_op jit(solution)/shard_map/all_to_all | solution.py:321
  61.7 10.5 %copy-start.3 = (s32[16]{0:T(128)S(1)}, s32[16]{0:T(128)}, u32[]{:S(2)}) copy-start(s32[16]{0:T(128)} %get-tuple-element.30.right) | copy-start | bytes 196
  72.2 17.0 %copy-start.4 = (s32[16]{0:T(128)S(1)}, s32[16]{0:T(128)}, u32[]{:S(2)}) copy-start(s32[16]{0:T(128)} %get-tuple-element.28.left) | copy-start | bytes 196
  72.2 1.0 copy-start.1
  89.2 5.0 %copy-start = (f32[16,64,128]{2,1,0:T(8,128)}, f32[16,64,128]{2,1,0:T(8,128)S(1)}, u32[]{:S(2)}) copy-start(f32[16,64,128]{2,1,0:T(8,128)S(1)} %all_to_all.42.ahead.got) | copy-start | bytes 1572868
  90.5 14.7 %all-to-all-start.5 = ((f32[16,32,128]{2,1,0:T(8,128)}), f32[16,32,128]{2,1,0:T(8,128)S(1)}, u32[]{:S(2)}, u32[]{:S(2)}) async-start(f32[16,32,128]{2,1,0:T(8,128)} %shard_map.128), calls=%async_computation.5 | async-start | bytes 524288 | tf_op jit(solution)/shard_map/all_to_all | solution.py:321
  105.1 6.4 %copy-start.7 = (f32[16,32,128]{2,1,0:T(8,128)}, f32[16,32,128]{2,1,0:T(8,128)S(1)}, u32[]{:S(2)}) copy-start(f32[16,32,128]{2,1,0:T(8,128)S(1)} %all-to-all-done.5.from_left) | copy-start | bytes 786436
  105.1 14.0 %all-to-all-start.4 = ((f32[16,32,128]{2,1,0:T(8,128)}), f32[16,32,128]{2,1,0:T(8,128)S(1)}, u32[]{:S(2)}, u32[]{:S(2)}) async-start(f32[16,32,128]{2,1,0:T(8,128)} %bitcast.7), calls=%async_computation.4 | async-start | bytes 524288 | tf_op jit(solution)/shard_map/all_to_all | solution.py:321
  119.2 0.7 copy-start.2
  121.2 14.2 %all-to-all-start.6 = ((f32[16,32,128]{2,1,0:T(8,128)}), f32[16,32,128]{2,1,0:T(8,128)S(1)}, u32[]{:S(2)}, u32[]{:S(2)}) async-start(f32[16,32,128]{2,1,0:T(8,128)} %shard_map.130), calls=%async_computation.6 | async-start | bytes 524288 | tf_op jit(solution)/shard_map/all_to_all | solution.py:321
  135.4 11.8 %copy-start.5 = (f32[16,32,128]{2,1,0:T(8,128)}, f32[16,32,128]{2,1,0:T(8,128)S(1)}, u32[]{:S(2)}) copy-start(f32[16,32,128]{2,1,0:T(8,128)S(1)} %all-to-all-done.6.got) | copy-start | bytes 786436
  136.3 15.4 %all-to-all-start.7 = ((f32[8,1,128]{2,1,0:T(1,128)}), f32[8,1,128]{2,1,0:T(1,128)S(1)}, u32[]{:S(2)}, u32[]{:S(2)}) async-start(f32[8,1,128]{2,1,0:T(1,128)} %broadcast_in_dim.6), calls=%async_computation.7 | async-start | bytes 8192 | tf_op jit(solution)/shard_map/all_to_all | solution.py:321
